TPU v7x, 32 devices: a whole 2x2x4 slice. The times are simulated.
32 devices in a mesh: win: 16 (over z, y, x), rcv: 2 (over core).
Axes of the slice: x: 2, y: 2, z: 4, core: 2. Of those that a mesh axis runs over, the one named last changes fastest.
Arguments:
- spectra: bfloat16 [32, 2, 32, 4096], P('win', None, 'rcv'), may hold values from -6 to 6
- source_channel: int32 [8], replicated, may hold values from 0 to 31
Outputs:
- stack: float32 [512, 8, 32], P('win', None, 'rcv')
All inputs are finite; a program needn't handle non-finite values.
Results may differ from a plain program's by a relative error of at most 0.0011.
Values may be sent and summed in bfloat16 or wider, within the bound.
No kernel may reach another device: no remote copies, remote signals or barrier semaphores. Data moves between devices by JAX's collectives and lax.ppermute only.
A program may use at most 64 MiB of HBM per device.

v0:
```python
import functools

import jax
import jax.numpy as jnp
import numpy as np
from jax import lax
from jax.experimental import pallas as pl
from jax.experimental.pallas import tpu as pltpu
from jax.sharding import PartitionSpec as P

L = 512
ITERS = 5


TUKEY = 4.685
EPSILON = 1e-06


def make_tables(bin_count, lag_count, rows):
    freq = np.arange(bin_count, dtype=np.int64)
    shifts = np.arange(lag_count // 2 + 1, dtype=np.int64)
    phase = shifts[:, None] * freq[None, :] % (2 * bin_count)
    angle = phase * (2.0 * np.pi / (2 * bin_count))
    factor = np.where(freq == 0, 1.0, 2.0) / np.sqrt(8.0 * bin_count)
    table = np.zeros((2, rows, bin_count), np.float32)
    table[0, : len(shifts)] = np.cos(angle) * factor
    table[1, : len(shifts)] = -np.sin(angle) * factor
    return jnp.asarray(table.astype(jnp.bfloat16))


def correlate_kernel(*refs, peers, chunk):
    rows_ref, table_ref = refs[:2]
    block_refs = refs[2 : 2 + peers]
    out_ref, even_ref, odd_ref, float_ref = refs[2 + peers :]
    win_count, _, chan_count, bin_count = block_refs[0].shape
    source_count = rows_ref.shape[0]
    half = out_ref.shape[0] // 2
    for start in range(0, bin_count, chunk):
        bins = slice(start, start + chunk)
        for k in range(peers):
            for w in range(win_count):
                for part in range(2):
                    float_ref[w, part, k * chan_count : (k + 1) * chan_count, bins] = block_refs[k][
                        w, part, :, bins
                    ].astype(jnp.float32)
        reals, imags = [], []
        for w in range(win_count):
            real_p = float_ref[w, 0, :chan_count, bins]
            imag_q = float_ref[w, 1, :chan_count, bins]
            for s in range(source_count):
                real_a = float_ref[w, 0, pl.ds(rows_ref[s], 1), bins]
                imag_b = float_ref[w, 1, pl.ds(rows_ref[s], 1), bins]
                reals.append((real_a * real_p + imag_b * imag_q).astype(jnp.bfloat16))
                imags.append((imag_b * real_p - real_a * imag_q).astype(jnp.bfloat16))
        for index, parts, sum_ref in ((0, reals, even_ref), (1, imags, odd_ref)):
            term = lax.dot_general(
                table_ref[index, :, bins],
                jnp.concatenate(parts, axis=0),
                (((1,), (1,)), ((), ())),
                preferred_element_type=jnp.float32,
            )
            if start == 0:
                sum_ref[...] = term
            else:
                sum_ref[...] += term
    out_ref[half:, :] = (even_ref[:half, :] + odd_ref[:half, :]).astype(jnp.bfloat16)
    back = (even_ref[...] - odd_ref[...]).astype(jnp.bfloat16)
    lag = lax.broadcasted_iota(jnp.int32, (half, half), 0)
    shift = lax.broadcasted_iota(jnp.int32, (half, half), 1)
    flip = (lag + shift == half).astype(jnp.bfloat16)
    turned = jnp.dot(flip, back[:half], preferred_element_type=jnp.float32)
    first = jnp.where(
        lax.broadcasted_iota(jnp.int32, turned.shape, 0) == 0,
        back[half : half + 16].astype(jnp.float32)[:1],
        turned,
    )
    out_ref[:half, :] = first.astype(jnp.bfloat16)


def correlate(blocks, source_rows):
    win_count, _, chan_count, bin_count = blocks[0].shape
    source_count = source_rows.shape[0]
    rows = L // 2 + 16
    chunk = min(512, bin_count)
    table = make_tables(bin_count, L, rows)
    width = win_count * source_count * chan_count
    vmem = pl.BlockSpec(memory_space=pltpu.VMEM)
    return pl.pallas_call(
        functools.partial(correlate_kernel, peers=len(blocks), chunk=chunk),
        out_shape=jax.ShapeDtypeStruct((L, width), jnp.bfloat16),
        in_specs=[pl.BlockSpec(memory_space=pltpu.SMEM), vmem] + [vmem] * len(blocks),
        out_specs=vmem,
        scratch_shapes=[
            pltpu.VMEM((rows, width), jnp.float32),
            pltpu.VMEM((rows, width), jnp.float32),
            pltpu.VMEM((win_count, 2, len(blocks) * chan_count, bin_count), jnp.float32),
        ],
        compiler_params=pltpu.CompilerParams(vmem_limit_bytes=40 * 2**20),
        name="correlate",
    )(source_rows, table, *blocks)


def stack_kernel(x_ref, out_ref, y_ref, *, win_count):
    parts, block, width = x_ref.shape
    pairs = width // win_count
    count = parts * win_count
    for part in range(parts):
        both = x_ref[part].astype(jnp.float32)
        for w in range(win_count):
            y_ref[part * win_count + w] = both[:, w * pairs : (w + 1) * pairs]
    rows = 8
    centers = []
    for start in range(0, block, rows):
        raw = [y_ref[n, start : start + rows, :] for n in range(count)]
        mean = tree_sum(raw) * (1.0 / count)
        samples = [x - mean for x in raw]
        variance = tree_sum([x * x for x in samples]) * (1.0 / count)
        center = jnp.zeros_like(mean)
        for iteration in range(ITERS):
            scale_two = variance + center * center + EPSILON
            inverse = 1.0 / (TUKEY * TUKEY * scale_two)
            weights, products = [], []
            for x in samples:
                deviation = x - center
                kept = jnp.maximum(1.0 - deviation * deviation * inverse, 0.0)
                weight = kept * kept
                weights.append(weight)
                products.append(weight * x)
            center = tree_sum(products) / tree_sum(weights)
        centers.append(center + mean)
    out_ref[...] = jnp.concatenate(centers, axis=0).T


def tree_sum(terms):
    sums = list(terms[:4])
    for index, term in enumerate(terms[4:]):
        sums[index % 4] = sums[index % 4] + term
    return (sums[0] + sums[1]) + (sums[2] + sums[3])


def stack_blocks(regrouped, win_count, source_count):
    parts, block, width = regrouped.shape
    pairs = width // win_count
    result = pl.pallas_call(
        functools.partial(stack_kernel, win_count=win_count),
        out_shape=jax.ShapeDtypeStruct((pairs, block), jnp.float32),
        in_specs=[pl.BlockSpec(memory_space=pltpu.VMEM)],
        out_specs=pl.BlockSpec(memory_space=pltpu.VMEM),
        scratch_shapes=[pltpu.VMEM((parts * win_count, block, pairs), jnp.float32)],
        compiler_params=pltpu.CompilerParams(vmem_limit_bytes=16 * 2**20),
        name="bisquare_stack",
    )(regrouped)
    return result.reshape(source_count, pairs // source_count, block).transpose(2, 0, 1)


def per_device(spectra, source_channel):
    win_count = spectra.shape[0]
    chan_count = spectra.shape[2]
    source_count = source_channel.shape[0]
    peers = lax.axis_size("rcv")
    me = lax.axis_index("rcv")
    blocks = [spectra]
    for step in range(1, peers):
        blocks.append(lax.ppermute(spectra, "rcv", [(i, (i + step) % peers) for i in range(peers)]))
    back = (me - source_channel // chan_count + peers) % peers
    source_rows = back * chan_count + source_channel % chan_count
    corr = correlate(blocks, source_rows)
    parts = lax.axis_size("win")
    corr = corr.reshape(parts, L // parts, corr.shape[1])
    regrouped = lax.all_to_all(corr, "win", split_axis=0, concat_axis=0, tiled=True)
    return stack_blocks(regrouped, win_count, source_count)


def solution(mesh):
    return jax.shard_map(
        per_device,
        mesh=mesh,
        in_specs=(P("win", None, "rcv", None), P()),
        out_specs=P("win", None, "rcv"),
        check_vma=False,
    )
```

profile of v0, /device:TPU:0, one launch (start us, length us, event | category | flops | bytes accessed | tf_op | source)
XLA Modules:
  0.0 27.9 jit_solution(1579610833641687118)
XLA Ops:
  0.0 0.5 %collective-permute-start = (bf16[2,2,16,4096]{3,2,1,0:T(8,128)(2,1)}, bf16[2,2,16,4096]{3,2,1,0:T(8,128)(2,1)S(1)}, u32[]{:S(2)}, u32[]{:S(2)}) collective-permute-start(bf16[2,2,16,4096]{3,2,1,0:T(8,128)(2,1)} %refs_2_.1), channel_id=1, source_target_pairs={{0,1},{1,0},{2,3},{3,2},{4,5},{5,4},{6,7},{7,6},{8,9},{9,8},{10,11... | collective-permute-start | bytes 1572872 | tf_op jit(solution)/shard_map/ppermute | solution.py:164
  0.5 0.7 %fusion.refs_0_ = s32[8]{0:T(128)S(1)} fusion(s32[8]{0:T(128)} %param.4, s32[]{:T(128)S(6)} %axis_index.12), kind=kLoop, calls=%fused_computation.8 | loop fusion | flops 272 | bytes 68 | tf_op jit(solution)/shard_map/add | solution.py:166
  1.1 1.1 %collective-permute-done.refs_3_ = bf16[2,2,16,4096]{3,2,1,0:T(8,128)(2,1)S(1)} collective-permute-done((bf16[2,2,16,4096]{3,2,1,0:T(8,128)(2,1)}, bf16[2,2,16,4096]{3,2,1,0:T(8,128)(2,1)S(1)}, u32[]{:S(2)}, u32[]{:S(2)}) %collective-permute-start) | collective-permute-done | bytes 524320 | tf_op jit(solution)/shard_map/ppermute | solution.py:164
  2.2 0.0 copy-start
  2.2 2.3 %copy-done = bf16[2,272,4096]{2,1,0:T(8,128)(2,1)S(1)} copy-done((bf16[2,272,4096]{2,1,0:T(8,128)(2,1)S(1)}, bf16[2,272,4096]{2,1,0:T(8,128)(2,1)}, u32[]{:S(2)}) %copy-start) | copy-done | bytes 4456472
  4.5 0.0 copy-start.1
  4.5 1.0 %copy-done.1 = bf16[2,2,16,4096]{3,2,1,0:T(8,128)(2,1)S(1)} copy-done((bf16[2,2,16,4096]{3,2,1,0:T(8,128)(2,1)S(1)}, bf16[2,2,16,4096]{3,2,1,0:T(8,128)(2,1)}, u32[]{:S(2)}) %copy-start.1) | copy-done | bytes 524312
  5.5 2.5 %correlate.1 = bf16[512,256]{1,0:T(8,128)(2,1)S(1)} custom-call(s32[8]{0:T(128)S(1)} %fusion.refs_0_, bf16[2,272,4096]{2,1,0:T(8,128)(2,1)S(1)} %copy-done, bf16[2,2,16,4096]{3,2,1,0:T(8,128)(2,1)S(1)} %copy-done.1, bf16[2,2,16,4096]{3,2,1,0:T(8,128)(2,1)S(1)} %collective-permute-done.refs_3_), custom_call_target="tpu_custom_call" | custom-call | tf_op jit(solution)/shard_map/correlate/pallas_call | solution.py:88
  8.0 18.2 %all_to_all.5.x_ref = bf16[16,32,256]{2,1,0:T(8,128)(2,1)S(1)} all-to-all(bf16[16,32,256]{2,1,0:T(8,128)(2,1)S(1)} %bitcast.4), channel_id=1, replica_groups=mesh['win'=16,'rcv'=2] {'win'}, dimensions={0} | all-to-all | bytes 524288 | tf_op jit(solution)/shard_map/all_to_all | solution.py:170
  26.2 1.7 %bisquare_stack.1 = f32[128,32]{1,0:T(8,128)} custom-call(bf16[16,32,256]{2,1,0:T(8,128)(2,1)S(1)} %all_to_all.5.x_ref), custom_call_target="tpu_custom_call" | custom-call | tf_op jit(solution)/shard_map/bisquare_stack/pallas_call | solution.py:144
Async XLA Ops:
  0.0 2.2 %collective-permute-start = (bf16[2,2,16,4096]{3,2,1,0:T(8,128)(2,1)}, bf16[2,2,16,4096]{3,2,1,0:T(8,128)(2,1)S(1)}, u32[]{:S(2)}, u32[]{:S(2)}) collective-permute-start(bf16[2,2,16,4096]{3,2,1,0:T(8,128)(2,1)} %refs_2_.1), channel_id=1, source_target_pairs={{0,1},{1,0},{2,3},{3,2},{4,5},{5,4},{6,7},{7,6},{8,9},{9,8},{10,11... | collective-permute-start | bytes 1572872 | tf_op jit(solution)/shard_map/ppermute | solution.py:164
  2.2 2.3 %copy-start = (bf16[2,272,4096]{2,1,0:T(8,128)(2,1)S(1)}, bf16[2,272,4096]{2,1,0:T(8,128)(2,1)}, u32[]{:S(2)}) copy-start(bf16[2,272,4096]{2,1,0:T(8,128)(2,1)} %constant.46.clone.refs_1_) | copy-start | bytes 13369348
  4.5 1.0 %copy-start.1 = (bf16[2,2,16,4096]{3,2,1,0:T(8,128)(2,1)S(1)}, bf16[2,2,16,4096]{3,2,1,0:T(8,128)(2,1)}, u32[]{:S(2)}) copy-start(bf16[2,2,16,4096]{3,2,1,0:T(8,128)(2,1)} %refs_2_.1) | copy-start | bytes 1572868
where the time goes:
time: 28.1 us; the launch traced here: 27.9 us
  blocking collectives  18.2 us (65%)
  Pallas kernels  4.17 us (15%)
  local copies, waits for them, and re-layouts  3.3 us (12%)
  waiting for transfers between devices  1.07 us (4%)
  other arithmetic  0.68 us (2%)
  starting transfers between devices  0.45 us (2%)
    all_to_all x1, blocking collectives, per_device(): lax.all_to_all(corr, 'win', split_axis=0, concat_axis=0, tiled=True)  18.2 us
    unnamed x4, local copies, waits for them, and re-layouts  3.3 us
    pallas_call x1, Pallas kernels, correlate(): pl.pallas_call(functools.partial(correlate_kernel, peers=len(blocks), chu...  2.5 us
    pallas_call x1, Pallas kernels, stack_blocks(): pl.pallas_call(functools.partial(stack_kernel, win_count=win_count), out_...  1.67 us
    ppermute x1, waiting for transfers between devices, per_device(): lax.ppermute(spectra, 'rcv', [(i, (i + step) % peers) for i in range(peer...  1.07 us
    add x1, other arithmetic, per_device(): source_rows = back * chan_count + source_channel % chan_count  0.68 us
  transfers between devices with their start and end apart: 1, of which 1 were waited for; matrix products, arithmetic and copies ran while one was open for 2% of the time, Pallas kernels for 0%

commit v1 on v0

--- a/solution.py
+++ b/solution.py
@@ -35,6 +35,7 @@
     win_count, _, chan_count, bin_count = block_refs[0].shape
     source_count = rows_ref.shape[0]
     half = out_ref.shape[0] // 2
+    own_ref = block_refs[0]
     for start in range(0, bin_count, chunk):
         bins = slice(start, start + chunk)
         for k in range(peers):
@@ -45,8 +46,8 @@
                     ].astype(jnp.float32)
         reals, imags = [], []
         for w in range(win_count):
-            real_p = float_ref[w, 0, :chan_count, bins]
-            imag_q = float_ref[w, 1, :chan_count, bins]
+            real_p = own_ref[w, 0, :, bins]
+            imag_q = own_ref[w, 1, :, bins]
             for s in range(source_count):
                 real_a = float_ref[w, 0, pl.ds(rows_ref[s], 1), bins]
                 imag_b = float_ref[w, 1, pl.ds(rows_ref[s], 1), bins]
@@ -77,12 +78,11 @@
     out_ref[:half, :] = first.astype(jnp.bfloat16)
 
 
-def correlate(blocks, source_rows):
+def correlate(table, blocks, source_rows):
     win_count, _, chan_count, bin_count = blocks[0].shape
     source_count = source_rows.shape[0]
-    rows = L // 2 + 16
+    rows = table.shape[1]
     chunk = min(512, bin_count)
-    table = make_tables(bin_count, L, rows)
     width = win_count * source_count * chan_count
     vmem = pl.BlockSpec(memory_space=pltpu.VMEM)
     return pl.pallas_call(
@@ -98,6 +98,27 @@
         compiler_params=pltpu.CompilerParams(vmem_limit_bytes=40 * 2**20),
         name="correlate",
     )(source_rows, table, *blocks)
+
+
+def widen_kernel(table_ref, own_ref, out_ref):
+    for w in range(own_ref.shape[0]):
+        for part in range(2):
+            out_ref[w, part] = own_ref[w, part].astype(jnp.float32)
+
+
+def widen(table, own):
+    vmem = pl.BlockSpec(memory_space=pltpu.VMEM)
+    return pl.pallas_call(
+        widen_kernel,
+        out_shape=jax.ShapeDtypeStruct(own.shape, jnp.float32),
+        in_specs=[vmem, vmem],
+        out_specs=vmem,
+        compiler_params=pltpu.CompilerParams(vmem_limit_bytes=16 * 2**20),
+        cost_estimate=pl.CostEstimate(
+            flops=0, bytes_accessed=2 * table.size + 6 * own.size, transcendentals=0
+        ),
+        name="widen",
+    )(table, own)
 
 
 def stack_kernel(x_ref, out_ref, y_ref, *, win_count):
@@ -159,12 +180,14 @@
     source_count = source_channel.shape[0]
     peers = lax.axis_size("rcv")
     me = lax.axis_index("rcv")
-    blocks = [spectra]
+    table = make_tables(spectra.shape[3], L, L // 2 + 16)
+    own = widen(table, spectra)
+    blocks = [own]
     for step in range(1, peers):
         blocks.append(lax.ppermute(spectra, "rcv", [(i, (i + step) % peers) for i in range(peers)]))
     back = (me - source_channel // chan_count + peers) % peers
     source_rows = back * chan_count + source_channel % chan_count
-    corr = correlate(blocks, source_rows)
+    corr = correlate(table, blocks, source_rows)
     parts = lax.axis_size("win")
     corr = corr.reshape(parts, L // parts, corr.shape[1])
     regrouped = lax.all_to_all(corr, "win", split_axis=0, concat_axis=0, tiled=True)

time: 28.1 us -> 28.5 us (1.014)
  local copies, waits for them, and re-layouts: 3.3 us -> 5.45 us
  waiting for transfers between devices: 1.07 us -> 0.01 us
  other arithmetic: 0.68 us -> 0.02 us
    unnamed x4 -> x8, local copies, waits for them, and re-layouts: 3.3 us -> 5.45 us
    ppermute x1, waiting for transfers between devices: 1.07 us -> 0.01 us  [per_device(): lax.ppermute(spectra, 'rcv', [(i, (i + step) % peers) for i in range(peer...]
    add x1, other arithmetic: 0.68 us -> 0.02 us  [per_device(): source_rows = back * chan_count + source_channel % chan_count]
  transfers between devices with their start and end apart: 1 -> 1, of which waited for: 1 -> 0; matrix products, arithmetic and copies ran while one was open for 2% -> 0% of each run, Pallas kernels for 0% -> 0%
where the time goes in v1:
time: 28.5 us; the launch traced here: 28.2 us
  blocking collectives  18.2 us (64%)
  local copies, waits for them, and re-layouts  5.45 us (19%)
  Pallas kernels  4.09 us (14%)
  starting transfers between devices  0.45 us (2%)
    all_to_all x1, blocking collectives, per_device(): lax.all_to_all(corr, 'win', split_axis=0, concat_axis=0, tiled=True)  18.2 us
    unnamed x8, local copies, waits for them, and re-layouts  5.45 us
    pallas_call x1, Pallas kernels, correlate(): pl.pallas_call(functools.partial(correlate_kernel, peers=len(blocks), chu...  2.35 us
    pallas_call x1, Pallas kernels, stack_blocks(): pl.pallas_call(functools.partial(stack_kernel, win_count=win_count), out_...  1.67 us
  transfers between devices with their start and end apart: 1, of which 0 were waited for; matrix products, arithmetic and copies ran while one was open for 0% of the time, Pallas kernels for 0%

profile of v1, /device:TPU:0, one launch (start us, length us, event | category | flops | bytes accessed | tf_op | source)
XLA Modules:
  0.0 28.2 jit_solution(13199163169856695913)
XLA Ops:
  0.0 0.0 copy-start.3
  0.0 0.5 %collective-permute-start = (bf16[2,2,16,4096]{3,2,1,0:T(8,128)(2,1)}, bf16[2,2,16,4096]{3,2,1,0:T(8,128)(2,1)S(1)}, u32[]{:S(2)}, u32[]{:S(2)}) collective-permute-start(bf16[2,2,16,4096]{3,2,1,0:T(8,128)(2,1)} %own_ref.1), channel_id=1, source_target_pairs={{0,1},{1,0},{2,3},{3,2},{4,5},{5,4},{6,7},{7,6},{8,9},{9,8},{10,11... | collective-permute-start | bytes 1572872 | tf_op jit(solution)/shard_map/ppermute | solution.py:187
  0.5 0.0 copy-start
  0.5 2.3 %copy-done = bf16[2,272,4096]{2,1,0:T(8,128)(2,1)S(1)} copy-done((bf16[2,272,4096]{2,1,0:T(8,128)(2,1)S(1)}, bf16[2,272,4096]{2,1,0:T(8,128)(2,1)}, u32[]{:S(2)}) %copy-start) | copy-done | bytes 4456472
  2.7 0.0 copy-start.2
  2.7 1.0 %copy-done.2 = bf16[2,2,16,4096]{3,2,1,0:T(8,128)(2,1)S(1)} copy-done((bf16[2,2,16,4096]{3,2,1,0:T(8,128)(2,1)S(1)}, bf16[2,2,16,4096]{3,2,1,0:T(8,128)(2,1)}, u32[]{:S(2)}) %copy-start.2) | copy-done | bytes 524312
  3.8 0.0 copy-start.1
  3.8 0.1 widen.1.refs_2_
  3.8 0.0 copy-done.3
  3.9 0.0 collective-permute-done.refs_3_
  3.9 2.1 %copy-done.1 = bf16[2,272,4096]{2,1,0:T(8,128)(2,1)S(1)} copy-done((bf16[2,272,4096]{2,1,0:T(8,128)(2,1)S(1)}, bf16[2,272,4096]{2,1,0:T(8,128)(2,1)}, u32[]{:S(2)}) %copy-start.1) | copy-done | bytes 4456472
  6.0 2.3 %correlate.1 = bf16[512,256]{1,0:T(8,128)(2,1)S(1)} custom-call(s32[8]{0:T(128)S(1)} %fusion.refs_0_, bf16[2,272,4096]{2,1,0:T(8,128)(2,1)S(1)} %copy-done.1, f32[2,2,16,4096]{3,2,1,0:T(8,128)S(1)} %widen.1.refs_2_, bf16[2,2,16,4096]{3,2,1,0:T(8,128)(2,1)S(1)} %collective-permute-done.refs_3_), custom_call_target="tpu_custom_call" | custom-call | tf_op jit(solution)/shard_map/correlate/pallas_call | solution.py:88
  8.4 18.2 %all_to_all.5.x_ref = bf16[16,32,256]{2,1,0:T(8,128)(2,1)S(1)} all-to-all(bf16[16,32,256]{2,1,0:T(8,128)(2,1)S(1)} %bitcast.4), channel_id=1, replica_groups=mesh['win'=16,'rcv'=2] {'win'}, dimensions={0} | all-to-all | bytes 524288 | tf_op jit(solution)/shard_map/all_to_all | solution.py:193
  26.6 1.7 %bisquare_stack.1 = f32[128,32]{1,0:T(8,128)} custom-call(bf16[16,32,256]{2,1,0:T(8,128)(2,1)S(1)} %all_to_all.5.x_ref), custom_call_target="tpu_custom_call" | custom-call | tf_op jit(solution)/shard_map/bisquare_stack/pallas_call | solution.py:165
  (1 shorter events, 0.0 us)
Async XLA Ops:
  0.0 3.8 %copy-start.3 = (s32[8]{0:T(128)S(1)}, s32[8]{0:T(128)}, u32[]{:S(2)}) copy-start(s32[8]{0:T(128)} %param.4) | copy-start | bytes 100
  0.0 3.9 %collective-permute-start = (bf16[2,2,16,4096]{3,2,1,0:T(8,128)(2,1)}, bf16[2,2,16,4096]{3,2,1,0:T(8,128)(2,1)S(1)}, u32[]{:S(2)}, u32[]{:S(2)}) collective-permute-start(bf16[2,2,16,4096]{3,2,1,0:T(8,128)(2,1)} %own_ref.1), channel_id=1, source_target_pairs={{0,1},{1,0},{2,3},{3,2},{4,5},{5,4},{6,7},{7,6},{8,9},{9,8},{10,11... | collective-permute-start | bytes 1572872 | tf_op jit(solution)/shard_map/ppermute | solution.py:187
  0.5 2.3 %copy-start = (bf16[2,272,4096]{2,1,0:T(8,128)(2,1)S(1)}, bf16[2,272,4096]{2,1,0:T(8,128)(2,1)}, u32[]{:S(2)}) copy-start(bf16[2,272,4096]{2,1,0:T(8,128)(2,1)} %constant.46.clone.table_ref.refs_1_) | copy-start | bytes 13369348
  2.7 1.0 %copy-start.2 = (bf16[2,2,16,4096]{3,2,1,0:T(8,128)(2,1)S(1)}, bf16[2,2,16,4096]{3,2,1,0:T(8,128)(2,1)}, u32[]{:S(2)}) copy-start(bf16[2,2,16,4096]{3,2,1,0:T(8,128)(2,1)} %own_ref.1) | copy-start | bytes 1572868
  3.8 2.3 %copy-start.1 = (bf16[2,272,4096]{2,1,0:T(8,128)(2,1)S(1)}, bf16[2,272,4096]{2,1,0:T(8,128)(2,1)}, u32[]{:S(2)}) copy-start(bf16[2,272,4096]{2,1,0:T(8,128)(2,1)} %constant.46.clone.table_ref.refs_1_) | copy-start | bytes 13369348

commit v2 on v0

--- a/solution.py
+++ b/solution.py
@@ -10,6 +10,7 @@
 
 L = 512
 ITERS = 5
+VMEM_LIMIT = 24 * 2**20
 
 
 TUKEY = 4.685
@@ -77,12 +78,11 @@
     out_ref[:half, :] = first.astype(jnp.bfloat16)
 
 
-def correlate(blocks, source_rows):
+def correlate(table, blocks, source_rows):
     win_count, _, chan_count, bin_count = blocks[0].shape
     source_count = source_rows.shape[0]
-    rows = L // 2 + 16
+    rows = table.shape[1]
     chunk = min(512, bin_count)
-    table = make_tables(bin_count, L, rows)
     width = win_count * source_count * chan_count
     vmem = pl.BlockSpec(memory_space=pltpu.VMEM)
     return pl.pallas_call(
@@ -95,9 +95,31 @@
             pltpu.VMEM((rows, width), jnp.float32),
             pltpu.VMEM((win_count, 2, len(blocks) * chan_count, bin_count), jnp.float32),
         ],
-        compiler_params=pltpu.CompilerParams(vmem_limit_bytes=40 * 2**20),
+        compiler_params=pltpu.CompilerParams(vmem_limit_bytes=VMEM_LIMIT),
         name="correlate",
     )(source_rows, table, *blocks)
+
+
+def places_kernel(me_ref, channel_ref, out_ref, *, peers, chan_count):
+    for s in range(channel_ref.shape[0]):
+        channel = channel_ref[s]
+        owner = lax.div(channel, chan_count)
+        step = lax.rem(me_ref[0] - owner + peers, peers)
+        out_ref[s] = step * chan_count + channel - owner * chan_count
+
+
+def find_places(source_channel, peers, chan_count, meanwhile):
+    me = lax.axis_index("rcv").astype(jnp.int32)
+    smem = pl.BlockSpec(memory_space=pltpu.SMEM)
+    return pl.pallas_call(
+        functools.partial(places_kernel, peers=peers, chan_count=chan_count),
+        out_shape=jax.ShapeDtypeStruct(source_channel.shape, jnp.int32),
+        in_specs=[smem, smem],
+        out_specs=smem,
+        compiler_params=pltpu.CompilerParams(vmem_limit_bytes=VMEM_LIMIT),
+        cost_estimate=pl.CostEstimate(flops=0, bytes_accessed=meanwhile, transcendentals=0),
+        name="places",
+    )(me[None], source_channel)
 
 
 def stack_kernel(x_ref, out_ref, y_ref, *, win_count):
@@ -147,7 +169,7 @@
         in_specs=[pl.BlockSpec(memory_space=pltpu.VMEM)],
         out_specs=pl.BlockSpec(memory_space=pltpu.VMEM),
         scratch_shapes=[pltpu.VMEM((parts * win_count, block, pairs), jnp.float32)],
-        compiler_params=pltpu.CompilerParams(vmem_limit_bytes=16 * 2**20),
+        compiler_params=pltpu.CompilerParams(vmem_limit_bytes=VMEM_LIMIT),
         name="bisquare_stack",
     )(regrouped)
     return result.reshape(source_count, pairs // source_count, block).transpose(2, 0, 1)
@@ -158,13 +180,12 @@
     chan_count = spectra.shape[2]
     source_count = source_channel.shape[0]
     peers = lax.axis_size("rcv")
-    me = lax.axis_index("rcv")
+    table = make_tables(spectra.shape[3], L, L // 2 + 16)
+    source_rows = find_places(source_channel, peers, chan_count, 4 * (table.size + spectra.size))
     blocks = [spectra]
     for step in range(1, peers):
         blocks.append(lax.ppermute(spectra, "rcv", [(i, (i + step) % peers) for i in range(peers)]))
-    back = (me - source_channel // chan_count + peers) % peers
-    source_rows = back * chan_count + source_channel % chan_count
-    corr = correlate(blocks, source_rows)
+    corr = correlate(table, blocks, source_rows)
     parts = lax.axis_size("win")
     corr = corr.reshape(parts, L // parts, corr.shape[1])
     regrouped = lax.all_to_all(corr, "win", split_axis=0, concat_axis=0, tiled=True)

time: 28.1 us -> 28.2 us (level)
  Pallas kernels: 4.17 us -> 5.35 us
  waiting for transfers between devices: 1.07 us -> 0.01 us
  other arithmetic: 0.68 us -> 0 us
  local copies, waits for them, and re-layouts: 3.3 us -> 3.95 us
    pallas_call x0 -> x1, Pallas kernels: none -> 1.18 us  [find_places(): pl.pallas_call(functools.partial(places_kernel, peers=peers, chan_count=c...]
    ppermute x1, waiting for transfers between devices: 1.07 us -> 0.01 us  [per_device(): lax.ppermute(spectra, 'rcv', [(i, (i + step) % peers) for i in range(peer...]
    add x1 -> x0, other arithmetic: 0.68 us -> none  [per_device(): source_rows = back * chan_count + source_channel % chan_count]
    unnamed x4 -> x6, local copies, waits for them, and re-layouts: 3.3 us -> 3.95 us
  transfers between devices with their start and end apart: 1 -> 1, of which waited for: 1 -> 0; matrix products, arithmetic and copies ran while one was open for 2% -> 0% of each run, Pallas kernels for 0% -> 4%
where the time goes in v2:
time: 28.2 us; the launch traced here: 28 us
  blocking collectives  18.2 us (65%)
  Pallas kernels  5.35 us (19%)
  local copies, waits for them, and re-layouts  3.95 us (14%)
  starting transfers between devices  0.45 us (2%)
    all_to_all x1, blocking collectives, per_device(): lax.all_to_all(corr, 'win', split_axis=0, concat_axis=0, tiled=True)  18.2 us
    unnamed x6, local copies, waits for them, and re-layouts  3.95 us
    pallas_call x1, Pallas kernels, correlate(): pl.pallas_call(functools.partial(correlate_kernel, peers=len(blocks), chu...  2.5 us
    pallas_call x1, Pallas kernels, stack_blocks(): pl.pallas_call(functools.partial(stack_kernel, win_count=win_count), out_...  1.67 us
    pallas_call x1, Pallas kernels, find_places(): pl.pallas_call(functools.partial(places_kernel, peers=peers, chan_count=c...  1.18 us
  transfers between devices with their start and end apart: 1, of which 0 were waited for; matrix products, arithmetic and copies ran while one was open for 0% of the time, Pallas kernels for 4%

profile of v2, /device:TPU:0, one launch (start us, length us, event | category | flops | bytes accessed | tf_op | source)
XLA Modules:
  0.0 28.0 jit_solution(4222316281428913772)
XLA Ops:
  0.0 0.5 %collective-permute-start = (bf16[2,2,16,4096]{3,2,1,0:T(8,128)(2,1)}, bf16[2,2,16,4096]{3,2,1,0:T(8,128)(2,1)S(1)}, u32[]{:S(2)}, u32[]{:S(2)}) collective-permute-start(bf16[2,2,16,4096]{3,2,1,0:T(8,128)(2,1)} %refs_2_.1), channel_id=1, source_target_pairs={{0,1},{1,0},{2,3},{3,2},{4,5},{5,4},{6,7},{7,6},{8,9},{9,8},{10,11... | collective-permute-start | bytes 1572872 | tf_op jit(solution)/shard_map/ppermute | solution.py:187
  0.5 0.0 copy-start.2
  0.5 0.7 %copy-done.2 = s32[8]{0:T(128)S(1)} copy-done((s32[8]{0:T(128)S(1)}, s32[8]{0:T(128)}, u32[]{:S(2)}) %copy-start.2) | copy-done | bytes 56
  1.1 1.2 %places.1.refs_0_ = s32[8]{0:T(128)S(1)} custom-call(s32[1]{0:T(128)} %bitcast.me_ref, s32[8]{0:T(128)S(1)} %copy-done.2), custom_call_target="tpu_custom_call" | custom-call | bytes 9961472 | tf_op jit(solution)/shard_map/places/pallas_call | solution.py:114
  2.3 0.0 collective-permute-done.refs_3_
  2.3 0.0 copy-start
  2.3 2.3 %copy-done = bf16[2,272,4096]{2,1,0:T(8,128)(2,1)S(1)} copy-done((bf16[2,272,4096]{2,1,0:T(8,128)(2,1)S(1)}, bf16[2,272,4096]{2,1,0:T(8,128)(2,1)}, u32[]{:S(2)}) %copy-start) | copy-done | bytes 4456472
  4.6 0.0 copy-start.1
  4.6 1.0 %copy-done.1 = bf16[2,2,16,4096]{3,2,1,0:T(8,128)(2,1)S(1)} copy-done((bf16[2,2,16,4096]{3,2,1,0:T(8,128)(2,1)S(1)}, bf16[2,2,16,4096]{3,2,1,0:T(8,128)(2,1)}, u32[]{:S(2)}) %copy-start.1) | copy-done | bytes 524312
  5.6 2.5 %correlate.1 = bf16[512,256]{1,0:T(8,128)(2,1)S(1)} custom-call(s32[8]{0:T(128)S(1)} %places.1.refs_0_, bf16[2,272,4096]{2,1,0:T(8,128)(2,1)S(1)} %copy-done, bf16[2,2,16,4096]{3,2,1,0:T(8,128)(2,1)S(1)} %copy-done.1, bf16[2,2,16,4096]{3,2,1,0:T(8,128)(2,1)S(1)} %collective-permute-done.refs_3_), custom_call_target="tpu_custom_call" | custom-call | tf_op jit(solution)/shard_map/correlate/pallas_call | solution.py:88
  8.1 18.2 %all_to_all.5.x_ref = bf16[16,32,256]{2,1,0:T(8,128)(2,1)S(1)} all-to-all(bf16[16,32,256]{2,1,0:T(8,128)(2,1)S(1)} %bitcast.5), channel_id=1, replica_groups=mesh['win'=16,'rcv'=2] {'win'}, dimensions={0} | all-to-all | bytes 524288 | tf_op jit(solution)/shard_map/all_to_all | solution.py:191
  26.3 1.7 %bisquare_stack.1 = f32[128,32]{1,0:T(8,128)} custom-call(bf16[16,32,256]{2,1,0:T(8,128)(2,1)S(1)} %all_to_all.5.x_ref), custom_call_target="tpu_custom_call" | custom-call | tf_op jit(solution)/shard_map/bisquare_stack/pallas_call | solution.py:166
Async XLA Ops:
  0.0 2.3 %collective-permute-start = (bf16[2,2,16,4096]{3,2,1,0:T(8,128)(2,1)}, bf16[2,2,16,4096]{3,2,1,0:T(8,128)(2,1)S(1)}, u32[]{:S(2)}, u32[]{:S(2)}) collective-permute-start(bf16[2,2,16,4096]{3,2,1,0:T(8,128)(2,1)} %refs_2_.1), channel_id=1, source_target_pairs={{0,1},{1,0},{2,3},{3,2},{4,5},{5,4},{6,7},{7,6},{8,9},{9,8},{10,11... | collective-permute-start | bytes 1572872 | tf_op jit(solution)/shard_map/ppermute | solution.py:187
  0.5 0.7 %copy-start.2 = (s32[8]{0:T(128)S(1)}, s32[8]{0:T(128)}, u32[]{:S(2)}) copy-start(s32[8]{0:T(128)} %channel_ref.1) | copy-start | bytes 100
  2.3 2.3 %copy-start = (bf16[2,272,4096]{2,1,0:T(8,128)(2,1)S(1)}, bf16[2,272,4096]{2,1,0:T(8,128)(2,1)}, u32[]{:S(2)}) copy-start(bf16[2,272,4096]{2,1,0:T(8,128)(2,1)} %constant.6.clone.refs_1_) | copy-start | bytes 13369348
  4.6 1.0 %copy-start.1 = (bf16[2,2,16,4096]{3,2,1,0:T(8,128)(2,1)S(1)}, bf16[2,2,16,4096]{3,2,1,0:T(8,128)(2,1)}, u32[]{:S(2)}) copy-start(bf16[2,2,16,4096]{3,2,1,0:T(8,128)(2,1)} %refs_2_.1) | copy-start | bytes 1572868

commit v3 on v2

--- a/solution.py
+++ b/solution.py
@@ -117,7 +117,7 @@
         in_specs=[smem, smem],
         out_specs=smem,
         compiler_params=pltpu.CompilerParams(vmem_limit_bytes=VMEM_LIMIT),
-        cost_estimate=pl.CostEstimate(flops=0, bytes_accessed=meanwhile, transcendentals=0),
+        cost_estimate=pl.CostEstimate(flops=meanwhile, bytes_accessed=0, transcendentals=0),
         name="places",
     )(me[None], source_channel)
 
@@ -181,7 +181,7 @@
     source_count = source_channel.shape[0]
     peers = lax.axis_size("rcv")
     table = make_tables(spectra.shape[3], L, L // 2 + 16)
-    source_rows = find_places(source_channel, peers, chan_count, 4 * (table.size + spectra.size))
+    source_rows = find_places(source_channel, peers, chan_count, 2000 * table.size)
     blocks = [spectra]
     for step in range(1, peers):
         blocks.append(lax.ppermute(spectra, "rcv", [(i, (i + step) % peers) for i in range(peers)]))

time: 28.2 us -> 26.1 us (0.926)
  local copies, waits for them, and re-layouts: 3.95 us -> 1.84 us
    unnamed x6, local copies, waits for them, and re-layouts: 3.95 us -> 1.84 us
  transfers between devices with their start and end apart: 1 -> 1, of which waited for: 0 -> 0; matrix products, arithmetic and copies ran while one was open for 0% -> 0% of each run, Pallas kernels for 4% -> 5%
where the time goes in v3:
time: 26.1 us; the launch traced here: 25.9 us
  blocking collectives  18.2 us (70%)
  Pallas kernels  5.35 us (20%)
  local copies, waits for them, and re-layouts  1.84 us (7%)
  starting transfers between devices  0.45 us (2%)
    all_to_all x1, blocking collectives, per_device(): lax.all_to_all(corr, 'win', split_axis=0, concat_axis=0, tiled=True)  18.2 us
    pallas_call x1, Pallas kernels, correlate(): pl.pallas_call(functools.partial(correlate_kernel, peers=len(blocks), chu...  2.51 us
    unnamed x6, local copies, waits for them, and re-layouts  1.84 us
    pallas_call x1, Pallas kernels, stack_blocks(): pl.pallas_call(functools.partial(stack_kernel, win_count=win_count), out_...  1.67 us
    pallas_call x1, Pallas kernels, find_places(): pl.pallas_call(functools.partial(places_kernel, peers=peers, chan_count=c...  1.18 us
  transfers between devices with their start and end apart: 1, of which 0 were waited for; matrix products, arithmetic and copies ran while one was open for 0% of the time, Pallas kernels for 5%

profile of v3, /device:TPU:0, one launch (start us, length us, event | category | flops | bytes accessed | tf_op | source)
XLA Modules:
  0.0 25.9 jit_solution(7998325940760225654)
XLA Ops:
  0.0 0.5 %collective-permute-start = (bf16[2,2,16,4096]{3,2,1,0:T(8,128)(2,1)}, bf16[2,2,16,4096]{3,2,1,0:T(8,128)(2,1)S(1)}, u32[]{:S(2)}, u32[]{:S(2)}) collective-permute-start(bf16[2,2,16,4096]{3,2,1,0:T(8,128)(2,1)} %refs_2_.1), channel_id=1, source_target_pairs={{0,1},{1,0},{2,3},{3,2},{4,5},{5,4},{6,7},{7,6},{8,9},{9,8},{10,11... | collective-permute-start | bytes 1572872 | tf_op jit(solution)/shard_map/ppermute | solution.py:187
  0.5 0.0 copy-start.2
  0.5 0.7 %copy-done.2 = s32[8]{0:T(128)S(1)} copy-done((s32[8]{0:T(128)S(1)}, s32[8]{0:T(128)}, u32[]{:S(2)}) %copy-start.2) | copy-done | bytes 56
  1.1 0.0 copy-start
  1.1 0.0 copy-start.1
  1.1 1.2 %places.1.refs_0_ = s32[8]{0:T(128)S(1)} custom-call(s32[1]{0:T(128)} %bitcast.me_ref, s32[8]{0:T(128)S(1)} %copy-done.2), custom_call_target="tpu_custom_call" | custom-call | flops 4456448000 | tf_op jit(solution)/shard_map/places/pallas_call | solution.py:114
  2.3 0.0 collective-permute-done.refs_3_
  2.3 1.1 %copy-done = bf16[2,272,4096]{2,1,0:T(8,128)(2,1)S(1)} copy-done((bf16[2,272,4096]{2,1,0:T(8,128)(2,1)S(1)}, bf16[2,272,4096]{2,1,0:T(8,128)(2,1)}, u32[]{:S(2)}) %copy-start) | copy-done | bytes 4456472
  3.4 0.1 copy-done.1
  3.5 2.5 %correlate.1 = bf16[512,256]{1,0:T(8,128)(2,1)S(1)} custom-call(s32[8]{0:T(128)S(1)} %places.1.refs_0_, bf16[2,272,4096]{2,1,0:T(8,128)(2,1)S(1)} %copy-done, bf16[2,2,16,4096]{3,2,1,0:T(8,128)(2,1)S(1)} %copy-done.1, bf16[2,2,16,4096]{3,2,1,0:T(8,128)(2,1)S(1)} %collective-permute-done.refs_3_), custom_call_target="tpu_custom_call" | custom-call | tf_op jit(solution)/shard_map/correlate/pallas_call | solution.py:88
  6.0 18.2 %all_to_all.5.x_ref = bf16[16,32,256]{2,1,0:T(8,128)(2,1)S(1)} all-to-all(bf16[16,32,256]{2,1,0:T(8,128)(2,1)S(1)} %bitcast.5), channel_id=1, replica_groups=mesh['win'=16,'rcv'=2] {'win'}, dimensions={0} | all-to-all | bytes 524288 | tf_op jit(solution)/shard_map/all_to_all | solution.py:191
  24.2 1.7 %bisquare_stack.1 = f32[128,32]{1,0:T(8,128)} custom-call(bf16[16,32,256]{2,1,0:T(8,128)(2,1)S(1)} %all_to_all.5.x_ref), custom_call_target="tpu_custom_call" | custom-call | tf_op jit(solution)/shard_map/bisquare_stack/pallas_call | solution.py:166
Async XLA Ops:
  0.0 2.3 %collective-permute-start = (bf16[2,2,16,4096]{3,2,1,0:T(8,128)(2,1)}, bf16[2,2,16,4096]{3,2,1,0:T(8,128)(2,1)S(1)}, u32[]{:S(2)}, u32[]{:S(2)}) collective-permute-start(bf16[2,2,16,4096]{3,2,1,0:T(8,128)(2,1)} %refs_2_.1), channel_id=1, source_target_pairs={{0,1},{1,0},{2,3},{3,2},{4,5},{5,4},{6,7},{7,6},{8,9},{9,8},{10,11... | collective-permute-start | bytes 1572872 | tf_op jit(solution)/shard_map/ppermute | solution.py:187
  0.5 0.7 %copy-start.2 = (s32[8]{0:T(128)S(1)}, s32[8]{0:T(128)}, u32[]{:S(2)}) copy-start(s32[8]{0:T(128)} %channel_ref.1) | copy-start | bytes 100
  1.1 2.3 %copy-start = (bf16[2,272,4096]{2,1,0:T(8,128)(2,1)S(1)}, bf16[2,272,4096]{2,1,0:T(8,128)(2,1)}, u32[]{:S(2)}) copy-start(bf16[2,272,4096]{2,1,0:T(8,128)(2,1)} %constant.6.clone.refs_1_) | copy-start | bytes 13369348
  1.1 2.4 %copy-start.1 = (bf16[2,2,16,4096]{3,2,1,0:T(8,128)(2,1)S(1)}, bf16[2,2,16,4096]{3,2,1,0:T(8,128)(2,1)}, u32[]{:S(2)}) copy-start(bf16[2,2,16,4096]{3,2,1,0:T(8,128)(2,1)} %refs_2_.1) | copy-start | bytes 1572868

commit v4 on v0

--- a/solution.py
+++ b/solution.py
@@ -10,6 +10,7 @@
 
 L = 512
 ITERS = 5
+VMEM_LIMIT = 24 * 2**20
 
 
 TUKEY = 4.685
@@ -29,12 +30,18 @@
 
 
 def correlate_kernel(*refs, peers, chunk):
-    rows_ref, table_ref = refs[:2]
-    block_refs = refs[2 : 2 + peers]
-    out_ref, even_ref, odd_ref, float_ref = refs[2 + peers :]
+    channel_ref, table_ref, flip_ref = refs[:3]
+    block_refs = refs[3 : 3 + peers]
+    out_ref, even_ref, odd_ref, float_ref = refs[3 + peers :]
     win_count, _, chan_count, bin_count = block_refs[0].shape
-    source_count = rows_ref.shape[0]
+    source_count = channel_ref.shape[0]
     half = out_ref.shape[0] // 2
+    me = lax.axis_index("rcv")
+    rows = []
+    for s in range(source_count):
+        owner = lax.div(channel_ref[s], chan_count)
+        place = lax.rem(me - owner + peers, peers) * chan_count
+        rows.append(place + lax.rem(channel_ref[s], chan_count))
     for start in range(0, bin_count, chunk):
         bins = slice(start, start + chunk)
         for k in range(peers):
@@ -48,8 +55,8 @@
             real_p = float_ref[w, 0, :chan_count, bins]
             imag_q = float_ref[w, 1, :chan_count, bins]
             for s in range(source_count):
-                real_a = float_ref[w, 0, pl.ds(rows_ref[s], 1), bins]
-                imag_b = float_ref[w, 1, pl.ds(rows_ref[s], 1), bins]
+                real_a = float_ref[w, 0, pl.ds(rows[s], 1), bins]
+                imag_b = float_ref[w, 1, pl.ds(rows[s], 1), bins]
                 reals.append((real_a * real_p + imag_b * imag_q).astype(jnp.bfloat16))
                 imags.append((imag_b * real_p - real_a * imag_q).astype(jnp.bfloat16))
         for index, parts, sum_ref in ((0, reals, even_ref), (1, imags, odd_ref)):
@@ -65,10 +72,7 @@
                 sum_ref[...] += term
     out_ref[half:, :] = (even_ref[:half, :] + odd_ref[:half, :]).astype(jnp.bfloat16)
     back = (even_ref[...] - odd_ref[...]).astype(jnp.bfloat16)
-    lag = lax.broadcasted_iota(jnp.int32, (half, half), 0)
-    shift = lax.broadcasted_iota(jnp.int32, (half, half), 1)
-    flip = (lag + shift == half).astype(jnp.bfloat16)
-    turned = jnp.dot(flip, back[:half], preferred_element_type=jnp.float32)
+    turned = jnp.dot(flip_ref[...], back[:half], preferred_element_type=jnp.float32)
     first = jnp.where(
         lax.broadcasted_iota(jnp.int32, turned.shape, 0) == 0,
         back[half : half + 16].astype(jnp.float32)[:1],
@@ -77,27 +81,43 @@
     out_ref[:half, :] = first.astype(jnp.bfloat16)
 
 
-def correlate(blocks, source_rows):
+def correlate(source_channel, table, flip, blocks):
     win_count, _, chan_count, bin_count = blocks[0].shape
-    source_count = source_rows.shape[0]
-    rows = L // 2 + 16
+    source_count = source_channel.shape[0]
+    rows = table.shape[1]
     chunk = min(512, bin_count)
-    table = make_tables(bin_count, L, rows)
     width = win_count * source_count * chan_count
     vmem = pl.BlockSpec(memory_space=pltpu.VMEM)
     return pl.pallas_call(
         functools.partial(correlate_kernel, peers=len(blocks), chunk=chunk),
         out_shape=jax.ShapeDtypeStruct((L, width), jnp.bfloat16),
-        in_specs=[pl.BlockSpec(memory_space=pltpu.SMEM), vmem] + [vmem] * len(blocks),
+        in_specs=[pl.BlockSpec(memory_space=pltpu.SMEM), vmem, vmem] + [vmem] * len(blocks),
         out_specs=vmem,
         scratch_shapes=[
             pltpu.VMEM((rows, width), jnp.float32),
             pltpu.VMEM((rows, width), jnp.float32),
             pltpu.VMEM((win_count, 2, len(blocks) * chan_count, bin_count), jnp.float32),
         ],
-        compiler_params=pltpu.CompilerParams(vmem_limit_bytes=40 * 2**20),
+        compiler_params=pltpu.CompilerParams(vmem_limit_bytes=VMEM_LIMIT),
         name="correlate",
-    )(source_rows, table, *blocks)
+    )(source_channel, table, flip, *blocks)
+
+
+def flip_kernel(out_ref):
+    lag = lax.broadcasted_iota(jnp.int32, out_ref.shape, 0)
+    shift = lax.broadcasted_iota(jnp.int32, out_ref.shape, 1)
+    out_ref[...] = (lag + shift == out_ref.shape[0]).astype(jnp.float32).astype(jnp.bfloat16)
+
+
+def make_flip(half, meanwhile):
+    return pl.pallas_call(
+        flip_kernel,
+        out_shape=jax.ShapeDtypeStruct((half, half), jnp.bfloat16),
+        out_specs=pl.BlockSpec(memory_space=pltpu.VMEM),
+        compiler_params=pltpu.CompilerParams(vmem_limit_bytes=VMEM_LIMIT),
+        cost_estimate=pl.CostEstimate(flops=meanwhile, bytes_accessed=0, transcendentals=0),
+        name="make_flip",
+    )()
 
 
 def stack_kernel(x_ref, out_ref, y_ref, *, win_count):
@@ -147,7 +167,7 @@
         in_specs=[pl.BlockSpec(memory_space=pltpu.VMEM)],
         out_specs=pl.BlockSpec(memory_space=pltpu.VMEM),
         scratch_shapes=[pltpu.VMEM((parts * win_count, block, pairs), jnp.float32)],
-        compiler_params=pltpu.CompilerParams(vmem_limit_bytes=16 * 2**20),
+        compiler_params=pltpu.CompilerParams(vmem_limit_bytes=VMEM_LIMIT),
         name="bisquare_stack",
     )(regrouped)
     return result.reshape(source_count, pairs // source_count, block).transpose(2, 0, 1)
@@ -155,16 +175,14 @@
 
 def per_device(spectra, source_channel):
     win_count = spectra.shape[0]
-    chan_count = spectra.shape[2]
     source_count = source_channel.shape[0]
     peers = lax.axis_size("rcv")
-    me = lax.axis_index("rcv")
+    table = make_tables(spectra.shape[3], L, L // 2 + 16)
+    flip = make_flip(L // 2, 2000 * table.size)
     blocks = [spectra]
     for step in range(1, peers):
         blocks.append(lax.ppermute(spectra, "rcv", [(i, (i + step) % peers) for i in range(peers)]))
-    back = (me - source_channel // chan_count + peers) % peers
-    source_rows = back * chan_count + source_channel % chan_count
-    corr = correlate(blocks, source_rows)
+    corr = correlate(source_channel, table, flip, blocks)
     parts = lax.axis_size("win")
     corr = corr.reshape(parts, L // parts, corr.shape[1])
     regrouped = lax.all_to_all(corr, "win", split_axis=0, concat_axis=0, tiled=True)

time: 28.1 us -> 24.9 us (0.89)
  local copies, waits for them, and re-layouts: 3.3 us -> 0.11 us
  other arithmetic: 0.68 us -> 0 us
  waiting for transfers between devices: 1.07 us -> 1.72 us
    unnamed x4 -> x6, local copies, waits for them, and re-layouts: 3.3 us -> 0.11 us
    add x1 -> x0, other arithmetic: 0.68 us -> none  [per_device(): source_rows = back * chan_count + source_channel % chan_count]
    ppermute x1, waiting for transfers between devices: 1.07 us -> 1.72 us  [per_device(): lax.ppermute(spectra, 'rcv', [(i, (i + step) % peers) for i in range(peer...]
  transfers between devices with their start and end apart: 1 -> 1, of which waited for: 1 -> 1; matrix products, arithmetic and copies ran while one was open for 2% -> 0% of each run, Pallas kernels for 0% -> 0%
where the time goes in v4:
time: 24.9 us; the launch traced here: 24.7 us
  blocking collectives  18.1 us (73%)
  Pallas kernels  4.23 us (17%)
  waiting for transfers between devices  1.72 us (7%)
  starting transfers between devices  0.52 us (2%)
    all_to_all x1, blocking collectives, per_device(): lax.all_to_all(corr, 'win', split_axis=0, concat_axis=0, tiled=True)  18.1 us
    pallas_call x1, Pallas kernels, correlate(): pl.pallas_call(functools.partial(correlate_kernel, peers=len(blocks), chu...  2.53 us
    ppermute x1, waiting for transfers between devices, per_device(): lax.ppermute(spectra, 'rcv', [(i, (i + step) % peers) for i in range(peer...  1.72 us
    pallas_call x1, Pallas kernels, stack_blocks(): pl.pallas_call(functools.partial(stack_kernel, win_count=win_count), out_...  1.67 us
    ppermute x1, starting transfers between devices, per_device(): lax.ppermute(spectra, 'rcv', [(i, (i + step) % peers) for i in range(peer...  0.52 us
  transfers between devices with their start and end apart: 1, of which 1 were waited for; matrix products, arithmetic and copies ran while one was open for 0% of the time, Pallas kernels for 0%

profile of v4, /device:TPU:0, one launch (start us, length us, event | category | flops | bytes accessed | tf_op | source)
XLA Modules:
  0.0 24.7 jit_solution(15882791132627312987)
XLA Ops:
  0.0 0.0 copy-start
  0.0 0.0 copy-start.1
  0.0 0.0 copy-start.2
  0.0 0.5 %collective-permute-start = (bf16[2,2,16,4096]{3,2,1,0:T(8,128)(2,1)}, bf16[2,2,16,4096]{3,2,1,0:T(8,128)(2,1)S(1)}, u32[]{:S(2)}, u32[]{:S(2)}) collective-permute-start(bf16[2,2,16,4096]{3,2,1,0:T(8,128)(2,1)} %refs_3_.1), channel_id=1, source_target_pairs={{0,1},{1,0},{2,3},{3,2},{4,5},{5,4},{6,7},{7,6},{8,9},{9,8},{10,11... | collective-permute-start | bytes 1572872 | tf_op jit(solution)/shard_map/ppermute | solution.py:184
  0.6 1.7 %collective-permute-done.refs_4_ = bf16[2,2,16,4096]{3,2,1,0:T(8,128)(2,1)S(1)} collective-permute-done((bf16[2,2,16,4096]{3,2,1,0:T(8,128)(2,1)}, bf16[2,2,16,4096]{3,2,1,0:T(8,128)(2,1)S(1)}, u32[]{:S(2)}, u32[]{:S(2)}) %collective-permute-start) | collective-permute-done | bytes 524320 | tf_op jit(solution)/shard_map/ppermute | solution.py:184
  2.3 0.0 copy-done
  2.3 0.1 copy-done.1
  2.4 0.0 copy-done.2
  2.4 2.5 %correlate.1 = bf16[512,256]{1,0:T(8,128)(2,1)S(1)} custom-call(s32[8]{0:T(128)S(1)} %copy-done.2, bf16[2,272,4096]{2,1,0:T(8,128)(2,1)S(1)} %copy-done, bf16[256,256]{1,0:T(8,128)(2,1)S(1)} %make_flip.1.refs_2_, bf16[2,2,16,4096]{3,2,1,0:T(8,128)(2,1)S(1)} %copy-done.1, bf16[2,2,16,4096]{3,2,1,0:T(8,128)(2,1)S(1)} %collective-permute-done.refs_4_), custom_call_target="tpu_custom_call" | custom-call | tf_op jit(solution)/shard_map/correlate/pallas_call | solution.py:91
  4.9 18.1 %all_to_all.5.x_ref = bf16[16,32,256]{2,1,0:T(8,128)(2,1)S(1)} all-to-all(bf16[16,32,256]{2,1,0:T(8,128)(2,1)S(1)} %bitcast.4), channel_id=1, replica_groups=mesh['win'=16,'rcv'=2] {'win'}, dimensions={0} | all-to-all | bytes 524288 | tf_op jit(solution)/shard_map/all_to_all | solution.py:188
  23.0 1.7 %bisquare_stack.1 = f32[128,32]{1,0:T(8,128)} custom-call(bf16[16,32,256]{2,1,0:T(8,128)(2,1)S(1)} %all_to_all.5.x_ref), custom_call_target="tpu_custom_call" | custom-call | tf_op jit(solution)/shard_map/bisquare_stack/pallas_call | solution.py:164
  (1 shorter events, 0.0 us)
Async XLA Ops:
  0.0 2.3 %copy-start = (bf16[2,272,4096]{2,1,0:T(8,128)(2,1)S(1)}, bf16[2,272,4096]{2,1,0:T(8,128)(2,1)}, u32[]{:S(2)}) copy-start(bf16[2,272,4096]{2,1,0:T(8,128)(2,1)} %constant.2.clone.refs_1_) | copy-start | bytes 13369348
  0.0 2.4 %copy-start.1 = (bf16[2,2,16,4096]{3,2,1,0:T(8,128)(2,1)S(1)}, bf16[2,2,16,4096]{3,2,1,0:T(8,128)(2,1)}, u32[]{:S(2)}) copy-start(bf16[2,2,16,4096]{3,2,1,0:T(8,128)(2,1)} %refs_3_.1) | copy-start | bytes 1572868
  0.0 2.4 %copy-start.2 = (s32[8]{0:T(128)S(1)}, s32[8]{0:T(128)}, u32[]{:S(2)}) copy-start(s32[8]{0:T(128)} %refs_0_.1) | copy-start | bytes 100
  0.0 2.3 %collective-permute-start = (bf16[2,2,16,4096]{3,2,1,0:T(8,128)(2,1)}, bf16[2,2,16,4096]{3,2,1,0:T(8,128)(2,1)S(1)}, u32[]{:S(2)}, u32[]{:S(2)}) collective-permute-start(bf16[2,2,16,4096]{3,2,1,0:T(8,128)(2,1)} %refs_3_.1), channel_id=1, source_target_pairs={{0,1},{1,0},{2,3},{3,2},{4,5},{5,4},{6,7},{7,6},{8,9},{9,8},{10,11... | collective-permute-start | bytes 1572872 | tf_op jit(solution)/shard_map/ppermute | solution.py:184

commit v5 on v4

--- a/solution.py
+++ b/solution.py
@@ -29,11 +29,11 @@
     return jnp.asarray(table.astype(jnp.bfloat16))
 
 
-def correlate_kernel(*refs, peers, chunk):
+def correlate_kernel(*refs, peers, chunk, window):
     channel_ref, table_ref, flip_ref = refs[:3]
     block_refs = refs[3 : 3 + peers]
     out_ref, even_ref, odd_ref, float_ref = refs[3 + peers :]
-    win_count, _, chan_count, bin_count = block_refs[0].shape
+    _, _, chan_count, bin_count = block_refs[0].shape
     source_count = channel_ref.shape[0]
     half = out_ref.shape[0] // 2
     me = lax.axis_index("rcv")
@@ -45,20 +45,18 @@
     for start in range(0, bin_count, chunk):
         bins = slice(start, start + chunk)
         for k in range(peers):
-            for w in range(win_count):
-                for part in range(2):
-                    float_ref[w, part, k * chan_count : (k + 1) * chan_count, bins] = block_refs[k][
-                        w, part, :, bins
-                    ].astype(jnp.float32)
+            for part in range(2):
+                float_ref[part, k * chan_count : (k + 1) * chan_count, bins] = block_refs[k][
+                    window, part, :, bins
+                ].astype(jnp.float32)
         reals, imags = [], []
-        for w in range(win_count):
-            real_p = float_ref[w, 0, :chan_count, bins]
-            imag_q = float_ref[w, 1, :chan_count, bins]
-            for s in range(source_count):
-                real_a = float_ref[w, 0, pl.ds(rows[s], 1), bins]
-                imag_b = float_ref[w, 1, pl.ds(rows[s], 1), bins]
-                reals.append((real_a * real_p + imag_b * imag_q).astype(jnp.bfloat16))
-                imags.append((imag_b * real_p - real_a * imag_q).astype(jnp.bfloat16))
+        real_p = float_ref[0, :chan_count, bins]
+        imag_q = float_ref[1, :chan_count, bins]
+        for s in range(source_count):
+            real_a = float_ref[0, pl.ds(rows[s], 1), bins]
+            imag_b = float_ref[1, pl.ds(rows[s], 1), bins]
+            reals.append((real_a * real_p + imag_b * imag_q).astype(jnp.bfloat16))
+            imags.append((imag_b * real_p - real_a * imag_q).astype(jnp.bfloat16))
         for index, parts, sum_ref in ((0, reals, even_ref), (1, imags, odd_ref)):
             term = lax.dot_general(
                 table_ref[index, :, bins],
@@ -81,22 +79,22 @@
     out_ref[:half, :] = first.astype(jnp.bfloat16)
 
 
-def correlate(source_channel, table, flip, blocks):
-    win_count, _, chan_count, bin_count = blocks[0].shape
+def correlate(source_channel, table, flip, blocks, window):
+    _, _, chan_count, bin_count = blocks[0].shape
     source_count = source_channel.shape[0]
     rows = table.shape[1]
     chunk = min(512, bin_count)
-    width = win_count * source_count * chan_count
+    width = source_count * chan_count
     vmem = pl.BlockSpec(memory_space=pltpu.VMEM)
     return pl.pallas_call(
-        functools.partial(correlate_kernel, peers=len(blocks), chunk=chunk),
+        functools.partial(correlate_kernel, peers=len(blocks), chunk=chunk, window=window),
         out_shape=jax.ShapeDtypeStruct((L, width), jnp.bfloat16),
         in_specs=[pl.BlockSpec(memory_space=pltpu.SMEM), vmem, vmem] + [vmem] * len(blocks),
         out_specs=vmem,
         scratch_shapes=[
             pltpu.VMEM((rows, width), jnp.float32),
             pltpu.VMEM((rows, width), jnp.float32),
-            pltpu.VMEM((win_count, 2, len(blocks) * chan_count, bin_count), jnp.float32),
+            pltpu.VMEM((2, len(blocks) * chan_count, bin_count), jnp.float32),
         ],
         compiler_params=pltpu.CompilerParams(vmem_limit_bytes=VMEM_LIMIT),
         name="correlate",
@@ -120,14 +118,13 @@
     )()
 
 
-def stack_kernel(x_ref, out_ref, y_ref, *, win_count):
-    parts, block, width = x_ref.shape
-    pairs = width // win_count
-    count = parts * win_count
-    for part in range(parts):
-        both = x_ref[part].astype(jnp.float32)
-        for w in range(win_count):
-            y_ref[part * win_count + w] = both[:, w * pairs : (w + 1) * pairs]
+def stack_kernel(*refs):
+    window_refs, out_ref, y_ref = refs[:-2], refs[-2], refs[-1]
+    parts, block, pairs = window_refs[0].shape
+    count = parts * len(window_refs)
+    for w, x_ref in enumerate(window_refs):
+        for part in range(parts):
+            y_ref[w * parts + part] = x_ref[part].astype(jnp.float32)
     rows = 8
     centers = []
     for start in range(0, block, rows):
@@ -158,18 +155,18 @@
     return (sums[0] + sums[1]) + (sums[2] + sums[3])
 
 
-def stack_blocks(regrouped, win_count, source_count):
-    parts, block, width = regrouped.shape
-    pairs = width // win_count
+def stack_blocks(received, source_count):
+    win_count = len(received)
+    parts, block, pairs = received[0].shape
     result = pl.pallas_call(
-        functools.partial(stack_kernel, win_count=win_count),
+        stack_kernel,
         out_shape=jax.ShapeDtypeStruct((pairs, block), jnp.float32),
-        in_specs=[pl.BlockSpec(memory_space=pltpu.VMEM)],
+        in_specs=[pl.BlockSpec(memory_space=pltpu.VMEM)] * win_count,
         out_specs=pl.BlockSpec(memory_space=pltpu.VMEM),
         scratch_shapes=[pltpu.VMEM((parts * win_count, block, pairs), jnp.float32)],
         compiler_params=pltpu.CompilerParams(vmem_limit_bytes=VMEM_LIMIT),
         name="bisquare_stack",
-    )(regrouped)
+    )(*received)
     return result.reshape(source_count, pairs // source_count, block).transpose(2, 0, 1)
 
 
@@ -182,11 +179,13 @@
     blocks = [spectra]
     for step in range(1, peers):
         blocks.append(lax.ppermute(spectra, "rcv", [(i, (i + step) % peers) for i in range(peers)]))
-    corr = correlate(source_channel, table, flip, blocks)
     parts = lax.axis_size("win")
-    corr = corr.reshape(parts, L // parts, corr.shape[1])
-    regrouped = lax.all_to_all(corr, "win", split_axis=0, concat_axis=0, tiled=True)
-    return stack_blocks(regrouped, win_count, source_count)
+    received = []
+    for window in range(win_count):
+        corr = correlate(source_channel, table, flip, blocks, window)
+        corr = corr.reshape(parts, L // parts, corr.shape[1])
+        received.append(lax.all_to_all(corr, "win", split_axis=0, concat_axis=0, tiled=True))
+    return stack_blocks(received, source_count)
 
 
 def solution(mesh):

time: 24.9 us -> 34.5 us (1.39)
  starting transfers between devices: 0.52 us -> 8.83 us
  blocking collectives: 18.1 us -> 11.2 us
  waiting for transfers between devices: 1.72 us -> 5.04 us
  Pallas kernels: 4.23 us -> 6.76 us
  local copies, waits for them, and re-layouts: 0.11 us -> 2.37 us
    all_to_all x0 -> x1, starting transfers between devices: none -> 8.31 us  [per_device(): lax.all_to_all(corr, 'win', split_axis=0, concat_axis=0, tiled=True)]
    all_to_all x1, blocking collectives: 18.1 us -> 11.2 us  [per_device(): lax.all_to_all(corr, 'win', split_axis=0, concat_axis=0, tiled=True)]
    all_to_all x0 -> x1, waiting for transfers between devices: none -> 3.33 us  [per_device(): lax.all_to_all(corr, 'win', split_axis=0, concat_axis=0, tiled=True)]
    pallas_call x1 -> x2, Pallas kernels: 2.53 us -> 5.06 us  [correlate(): pl.pallas_call(functools.partial(correlate_kernel, peers=len(blocks), chu...]
    unnamed x6 -> x8, local copies, waits for them, and re-layouts: 0.11 us -> 2.37 us
  transfers between devices with their start and end apart: 1 -> 2, of which waited for: 1 -> 2; matrix products, arithmetic and copies ran while one was open for 0% -> 0% of each run, Pallas kernels for 0% -> 7%
where the time goes in v5:
time: 34.5 us; the launch traced here: 34.2 us
  blocking collectives  11.2 us (32%)
  starting transfers between devices  8.83 us (26%)
  Pallas kernels  6.76 us (20%)
  waiting for transfers between devices  5.04 us (15%)
  local copies, waits for them, and re-layouts  2.37 us (7%)
    all_to_all x1, blocking collectives, per_device(): lax.all_to_all(corr, 'win', split_axis=0, concat_axis=0, tiled=True)  11.2 us
    all_to_all x1, starting transfers between devices, per_device(): lax.all_to_all(corr, 'win', split_axis=0, concat_axis=0, tiled=True)  8.31 us
    pallas_call x2, Pallas kernels, correlate(): pl.pallas_call(functools.partial(correlate_kernel, peers=len(blocks), chu...  5.06 us
    all_to_all x1, waiting for transfers between devices, per_device(): lax.all_to_all(corr, 'win', split_axis=0, concat_axis=0, tiled=True)  3.33 us
    unnamed x8, local copies, waits for them, and re-layouts  2.37 us
    ppermute x1, waiting for transfers between devices, per_device(): lax.ppermute(spectra, 'rcv', [(i, (i + step) % peers) for i in range(peer...  1.72 us
    pallas_call x1, Pallas kernels, stack_blocks(): pl.pallas_call(stack_kernel, out_shape=jax.ShapeDtypeStruct((pairs, block...  1.67 us
  transfers between devices with their start and end apart: 2, of which 2 were waited for; matrix products, arithmetic and copies ran while one was open for 0% of the time, Pallas kernels for 7%

profile of v5, /device:TPU:0, one launch (start us, length us, event | category | flops | bytes accessed | tf_op | source)
XLA Modules:
  0.0 34.2 jit_solution(17752331030911533979)
XLA Ops:
  0.0 0.0 copy-start
  0.0 0.0 copy-start.2
  0.0 0.0 copy-start.3
  0.0 0.5 %collective-permute-start = (bf16[2,2,16,4096]{3,2,1,0:T(8,128)(2,1)}, bf16[2,2,16,4096]{3,2,1,0:T(8,128)(2,1)S(1)}, u32[]{:S(2)}, u32[]{:S(2)}) collective-permute-start(bf16[2,2,16,4096]{3,2,1,0:T(8,128)(2,1)} %refs_3_.3), channel_id=1, source_target_pairs={{0,1},{1,0},{2,3},{3,2},{4,5},{5,4},{6,7},{7,6},{8,9},{9,8},{10,11... | collective-permute-start | bytes 1572872 | tf_op jit(solution)/shard_map/ppermute | solution.py:181
  0.6 1.7 %collective-permute-done.refs_4_ = bf16[2,2,16,4096]{3,2,1,0:T(8,128)(2,1)S(1)} collective-permute-done((bf16[2,2,16,4096]{3,2,1,0:T(8,128)(2,1)}, bf16[2,2,16,4096]{3,2,1,0:T(8,128)(2,1)S(1)}, u32[]{:S(2)}, u32[]{:S(2)}) %collective-permute-start) | collective-permute-done | bytes 524320 | tf_op jit(solution)/shard_map/ppermute | solution.py:181
  2.3 0.0 copy-done
  2.3 0.1 copy-done.2
  2.4 0.0 copy-done.3
  2.4 2.9 %correlate.3 = bf16[512,128]{1,0:T(8,128)(2,1)} custom-call(s32[8]{0:T(128)S(1)} %copy-done.3, bf16[2,272,4096]{2,1,0:T(8,128)(2,1)S(1)} %copy-done, bf16[256,256]{1,0:T(8,128)(2,1)S(1)} %make_flip.1.refs_2_, bf16[2,2,16,4096]{3,2,1,0:T(8,128)(2,1)S(1)} %copy-done.2, bf16[2,2,16,4096]{3,2,1,0:T(8,128)(2,1)S(1)} %collective-permute-done.refs_4_), custom_call_target="tpu_custom_call" | custom-call | tf_op jit(solution)/shard_map/correlate/pallas_call | solution.py:89
  5.2 8.3 %all-to-all-start.1 = ((bf16[16,32,128]{2,1,0:T(8,128)(2,1)}), bf16[16,32,128]{2,1,0:T(8,128)(2,1)S(1)}, u32[]{:S(2)}, u32[]{:S(2)}) async-start(bf16[16,32,128]{2,1,0:T(8,128)(2,1)} %bitcast.1), calls=%async_computation.1 | async-start | bytes 262144 | tf_op jit(solution)/shard_map/all_to_all | solution.py:187
  13.6 0.0 copy-start.1
  13.6 2.3 %copy-done.1 = bf16[2,272,4096]{2,1,0:T(8,128)(2,1)S(1)} copy-done((bf16[2,272,4096]{2,1,0:T(8,128)(2,1)S(1)}, bf16[2,272,4096]{2,1,0:T(8,128)(2,1)}, u32[]{:S(2)}) %copy-start.1) | copy-done | bytes 4456472
  15.8 2.2 %correlate.2 = bf16[512,128]{1,0:T(8,128)(2,1)S(1)} custom-call(s32[8]{0:T(128)S(1)} %copy-done.3, bf16[2,272,4096]{2,1,0:T(8,128)(2,1)S(1)} %copy-done.1, bf16[256,256]{1,0:T(8,128)(2,1)S(1)} %make_flip.1.refs_2_, bf16[2,2,16,4096]{3,2,1,0:T(8,128)(2,1)S(1)} %copy-done.2, bf16[2,2,16,4096]{3,2,1,0:T(8,128)(2,1)S(1)} %collective-permute-done.refs_4_), custom_call_target="tpu_custom_call" | custom-call | tf_op jit(solution)/shard_map/correlate/pallas_call | solution.py:89
  18.0 3.3 %all-to-all-done.1.refs_1_ = bf16[16,32,128]{2,1,0:T(8,128)(2,1)S(1)} async-done(((bf16[16,32,128]{2,1,0:T(8,128)(2,1)}), bf16[16,32,128]{2,1,0:T(8,128)(2,1)S(1)}, u32[]{:S(2)}, u32[]{:S(2)}) %all-to-all-start.1) | async-done | bytes 131104 | tf_op jit(solution)/shard_map/all_to_all | solution.py:187
  21.4 11.2 %all_to_all.10.refs_0_ = bf16[16,32,128]{2,1,0:T(8,128)(2,1)S(1)} all-to-all(bf16[16,32,128]{2,1,0:T(8,128)(2,1)S(1)} %bitcast.5), channel_id=1, replica_groups=mesh['win'=16,'rcv'=2] {'win'}, dimensions={0} | all-to-all | bytes 262144 | tf_op jit(solution)/shard_map/all_to_all | solution.py:187
  32.6 1.7 %bisquare_stack.1 = f32[128,32]{1,0:T(8,128)} custom-call(bf16[16,32,128]{2,1,0:T(8,128)(2,1)S(1)} %all_to_all.10.refs_0_, bf16[16,32,128]{2,1,0:T(8,128)(2,1)S(1)} %all-to-all-done.1.refs_1_), custom_call_target="tpu_custom_call" | custom-call | tf_op jit(solution)/shard_map/bisquare_stack/pallas_call | solution.py:161
  (1 shorter events, 0.0 us)
Async XLA Ops:
  0.0 2.3 %copy-start = (bf16[2,272,4096]{2,1,0:T(8,128)(2,1)S(1)}, bf16[2,272,4096]{2,1,0:T(8,128)(2,1)}, u32[]{:S(2)}) copy-start(bf16[2,272,4096]{2,1,0:T(8,128)(2,1)} %constant.2.clone.refs_1_) | copy-start | bytes 13369348
  0.0 2.4 %copy-start.2 = (bf16[2,2,16,4096]{3,2,1,0:T(8,128)(2,1)S(1)}, bf16[2,2,16,4096]{3,2,1,0:T(8,128)(2,1)}, u32[]{:S(2)}) copy-start(bf16[2,2,16,4096]{3,2,1,0:T(8,128)(2,1)} %refs_3_.3) | copy-start | bytes 1572868
  0.0 2.4 %copy-start.3 = (s32[8]{0:T(128)S(1)}, s32[8]{0:T(128)}, u32[]{:S(2)}) copy-start(s32[8]{0:T(128)} %refs_0_.3) | copy-start | bytes 100
  0.0 2.3 %collective-permute-start = (bf16[2,2,16,4096]{3,2,1,0:T(8,128)(2,1)}, bf16[2,2,16,4096]{3,2,1,0:T(8,128)(2,1)S(1)}, u32[]{:S(2)}, u32[]{:S(2)}) collective-permute-start(bf16[2,2,16,4096]{3,2,1,0:T(8,128)(2,1)} %refs_3_.3), channel_id=1, source_target_pairs={{0,1},{1,0},{2,3},{3,2},{4,5},{5,4},{6,7},{7,6},{8,9},{9,8},{10,11... | collective-permute-start | bytes 1572872 | tf_op jit(solution)/shard_map/ppermute | solution.py:181
  5.2 16.1 %all-to-all-start.1 = ((bf16[16,32,128]{2,1,0:T(8,128)(2,1)}), bf16[16,32,128]{2,1,0:T(8,128)(2,1)S(1)}, u32[]{:S(2)}, u32[]{:S(2)}) async-start(bf16[16,32,128]{2,1,0:T(8,128)(2,1)} %bitcast.1), calls=%async_computation.1 | async-start | bytes 262144 | tf_op jit(solution)/shard_map/all_to_all | solution.py:187
  13.6 2.3 %copy-start.1 = (bf16[2,272,4096]{2,1,0:T(8,128)(2,1)S(1)}, bf16[2,272,4096]{2,1,0:T(8,128)(2,1)}, u32[]{:S(2)}) copy-start(bf16[2,272,4096]{2,1,0:T(8,128)(2,1)} %constant.2.clone.refs_1_) | copy-start | bytes 13369348

commit v6 on v0

v6 whole, which is shorter than its diff:
```python
import functools

import jax
import jax.numpy as jnp
import numpy as np
from jax import lax
from jax.experimental import pallas as pl
from jax.experimental.pallas import tpu as pltpu
from jax.sharding import PartitionSpec as P

L = 512
ITERS = 5
VMEM_LIMIT = 24 * 2**20


TUKEY = 4.685
EPSILON = 1e-06


def make_tables(bin_count, lag_count, rows):
    freq = np.arange(bin_count, dtype=np.int64)
    shifts = np.arange(lag_count // 2 + 1, dtype=np.int64)
    phase = shifts[:, None] * freq[None, :] % (2 * bin_count)
    angle = phase * (2.0 * np.pi / (2 * bin_count))
    factor = np.where(freq == 0, 1.0, 2.0) / np.sqrt(8.0 * bin_count)
    table = np.zeros((2, rows, bin_count), np.float32)
    table[0, : len(shifts)] = np.cos(angle) * factor
    table[1, : len(shifts)] = -np.sin(angle) * factor
    return jnp.asarray(table.astype(jnp.bfloat16))


def flip_kernel(out_ref):
    lag = lax.broadcasted_iota(jnp.int32, out_ref.shape, 0)
    shift = lax.broadcasted_iota(jnp.int32, out_ref.shape, 1)
    out_ref[...] = (lag + shift == out_ref.shape[0]).astype(jnp.float32).astype(jnp.bfloat16)


def make_flip(half, meanwhile):
    return pl.pallas_call(
        flip_kernel,
        out_shape=jax.ShapeDtypeStruct((half, half), jnp.bfloat16),
        out_specs=pl.BlockSpec(memory_space=pltpu.VMEM),
        compiler_params=pltpu.CompilerParams(vmem_limit_bytes=VMEM_LIMIT),
        cost_estimate=pl.CostEstimate(flops=meanwhile, bytes_accessed=0, transcendentals=0),
        name="make_flip",
    )()


def share(win_count, source_count, peers):
    items = win_count * source_count // peers
    assert items * peers == win_count * source_count
    assert items % source_count == 0 or source_count % items == 0
    return items


def correlate_kernel(*refs, peers, chunk):
    channel_ref, table_ref, flip_ref = refs[:3]
    block_refs = refs[3 : 3 + peers]
    out_ref, lags_ref, even_ref, odd_ref, float_ref = refs[3 + peers :]
    win_count, _, chan_count, bin_count = block_refs[0].shape
    source_count = channel_ref.shape[0]
    items = share(win_count, source_count, peers)
    windows = float_ref.shape[0]
    parts, _, block, width = out_ref.shape
    half = flip_ref.shape[0]
    me = lax.axis_index("rcv")
    first = lax.div(me * items, source_count)
    rows = []
    for t in range(items):
        channel = channel_ref[lax.rem(me * items + t, source_count)]
        owner = lax.div(channel, chan_count)
        place = lax.rem(me - owner + peers, peers) * chan_count
        rows.append(place + lax.rem(channel, chan_count))
    for start in range(0, bin_count, chunk):
        bins = slice(start, start + chunk)
        for k in range(peers):
            for w in range(windows):
                for part in range(2):
                    float_ref[w, part, k * chan_count : (k + 1) * chan_count, bins] = block_refs[k][
                        first + w, part, :, bins
                    ].astype(jnp.float32)
        reals, imags = [], []
        for k in range(peers):
            receivers = slice(k * chan_count, (k + 1) * chan_count)
            for t in range(items):
                w = t // source_count
                real_p = float_ref[w, 0, receivers, bins]
                imag_q = float_ref[w, 1, receivers, bins]
                real_a = float_ref[w, 0, pl.ds(rows[t], 1), bins]
                imag_b = float_ref[w, 1, pl.ds(rows[t], 1), bins]
                reals.append((real_a * real_p + imag_b * imag_q).astype(jnp.bfloat16))
                imags.append((imag_b * real_p - real_a * imag_q).astype(jnp.bfloat16))
        for index, terms, sum_ref in ((0, reals, even_ref), (1, imags, odd_ref)):
            term = lax.dot_general(
                table_ref[index, :, bins],
                jnp.concatenate(terms, axis=0),
                (((1,), (1,)), ((), ())),
                preferred_element_type=jnp.float32,
            )
            if start == 0:
                sum_ref[...] = term
            else:
                sum_ref[...] += term
    lags_ref[half:, :] = even_ref[:half, :] + odd_ref[:half, :]
    back = (even_ref[...] - odd_ref[...]).astype(jnp.bfloat16)
    turned = jnp.dot(flip_ref[...], back[:half], preferred_element_type=jnp.float32)
    lags_ref[:half, :] = jnp.where(
        lax.broadcasted_iota(jnp.int32, turned.shape, 0) == 0,
        back[half : half + 16].astype(jnp.float32)[:1],
        turned,
    )
    for k in range(peers):
        owner = lax.rem(me - k + peers, peers)
        for part in range(parts):
            out_ref[part, owner] = lags_ref[
                part * block : (part + 1) * block, k * width : (k + 1) * width
            ].astype(jnp.bfloat16)


def correlate(source_channel, table, flip, blocks, parts):
    win_count, _, chan_count, bin_count = blocks[0].shape
    source_count = source_channel.shape[0]
    peers = len(blocks)
    items = share(win_count, source_count, peers)
    rows = table.shape[1]
    chunk = min(512, bin_count)
    width = items * chan_count
    vmem = pl.BlockSpec(memory_space=pltpu.VMEM)
    return pl.pallas_call(
        functools.partial(correlate_kernel, peers=peers, chunk=chunk),
        out_shape=jax.ShapeDtypeStruct((parts, peers, L // parts, width), jnp.bfloat16),
        in_specs=[pl.BlockSpec(memory_space=pltpu.SMEM), vmem, vmem] + [vmem] * peers,
        out_specs=vmem,
        scratch_shapes=[
            pltpu.VMEM((L, peers * width), jnp.float32),
            pltpu.VMEM((rows, peers * width), jnp.float32),
            pltpu.VMEM((rows, peers * width), jnp.float32),
            pltpu.VMEM((max(1, items // source_count), 2, peers * chan_count, bin_count), jnp.float32),
        ],
        compiler_params=pltpu.CompilerParams(vmem_limit_bytes=VMEM_LIMIT),
        name="correlate",
    )(source_channel, table, flip, *blocks)


def stack_kernel(x_ref, out_ref, y_ref):
    count, block, pairs = x_ref.shape
    for n in range(count):
        y_ref[n] = x_ref[n].astype(jnp.float32)
    rows = 8
    centers = []
    for start in range(0, block, rows):
        raw = [y_ref[n, start : start + rows, :] for n in range(count)]
        mean = tree_sum(raw) * (1.0 / count)
        samples = [x - mean for x in raw]
        variance = tree_sum([x * x for x in samples]) * (1.0 / count)
        center = jnp.zeros_like(mean)
        for iteration in range(ITERS):
            scale_two = variance + center * center + EPSILON
            inverse = 1.0 / (TUKEY * TUKEY * scale_two)
            weights, products = [], []
            for x in samples:
                deviation = x - center
                kept = jnp.maximum(1.0 - deviation * deviation * inverse, 0.0)
                weight = kept * kept
                weights.append(weight)
                products.append(weight * x)
            center = tree_sum(products) / tree_sum(weights)
        centers.append(center + mean)
    out_ref[...] = jnp.concatenate(centers, axis=0).T


def tree_sum(terms):
    sums = list(terms[:4])
    for index, term in enumerate(terms[4:]):
        sums[index % 4] = sums[index % 4] + term
    return (sums[0] + sums[1]) + (sums[2] + sums[3])


def stack_blocks(samples, source_count):
    count, block, pairs = samples.shape
    result = pl.pallas_call(
        stack_kernel,
        out_shape=jax.ShapeDtypeStruct((pairs, block), jnp.float32),
        in_specs=[pl.BlockSpec(memory_space=pltpu.VMEM)],
        out_specs=pl.BlockSpec(memory_space=pltpu.VMEM),
        scratch_shapes=[pltpu.VMEM((count, block, pairs), jnp.float32)],
        compiler_params=pltpu.CompilerParams(vmem_limit_bytes=VMEM_LIMIT),
        name="bisquare_stack",
    )(samples)
    return result.reshape(source_count, pairs // source_count, block).transpose(2, 0, 1)


def per_device(spectra, source_channel):
    win_count, _, chan_count, bin_count = spectra.shape
    source_count = source_channel.shape[0]
    peers = lax.axis_size("rcv")
    parts = lax.axis_size("win")
    block = L // parts
    items = share(win_count, source_count, peers)
    table = make_tables(bin_count, L, L // 2 + 16)
    flip = make_flip(L // 2, 2000 * table.size)
    blocks = [spectra]
    for step in range(1, peers):
        blocks.append(lax.ppermute(spectra, "rcv", [(i, (i + step) % peers) for i in range(peers)]))
    corr = correlate(source_channel, table, flip, blocks, parts)
    corr = corr.reshape(parts * peers, block, items * chan_count)
    moved = lax.all_to_all(corr, ("win", "rcv"), split_axis=0, concat_axis=0, tiled=True)
    if items != source_count:
        moved = moved.reshape(parts * peers, block, items, chan_count).transpose(0, 2, 1, 3)
        moved = moved.reshape(parts * win_count, source_count, block, chan_count).transpose(0, 2, 1, 3)
        moved = moved.reshape(parts * win_count, block, source_count * chan_count)
    return stack_blocks(moved, source_count)


def solution(mesh):
    return jax.shard_map(
        per_device,
        mesh=mesh,
        in_specs=(P("win", None, "rcv", None), P()),
        out_specs=P("win", None, "rcv"),
        check_vma=False,
    )
```

time: 28.1 us -> 24.3 us (0.86)
  local copies, waits for them, and re-layouts: 3.3 us -> 0.11 us
  other arithmetic: 0.68 us -> 0 us
  waiting for transfers between devices: 1.07 us -> 1.72 us
  blocking collectives: 18.2 us -> 17.7 us
    unnamed x4 -> x6, local copies, waits for them, and re-layouts: 3.3 us -> 0.11 us
    add x1 -> x0, other arithmetic: 0.68 us -> none  [per_device(): source_rows = back * chan_count + source_channel % chan_count]
    ppermute x1, waiting for transfers between devices: 1.07 us -> 1.72 us  [per_device(): lax.ppermute(spectra, 'rcv', [(i, (i + step) % peers) for i in range(peer...]
    all_to_all x1, blocking collectives: 18.2 us -> 17.7 us  [per_device(): lax.all_to_all(corr, ('win', 'rcv'), split_axis=0, concat_axis=0, tiled=T...]
    pallas_call x2 -> x3, Pallas kernels: 4.17 us -> 4.06 us  [the longest x1 2.36 us: correlate(): pl.pallas_call(functools.partial(correlate_kernel, peers=peers, chunk=chu...]
  transfers between devices with their start and end apart: 1 -> 1, of which waited for: 1 -> 1; matrix products, arithmetic and copies ran while one was open for 2% -> 0% of each run, Pallas kernels for 0% -> 0%
where the time goes in v6:
time: 24.3 us; the launch traced here: 24.1 us
  blocking collectives  17.7 us (73%)
  Pallas kernels  4.06 us (17%)
  waiting for transfers between devices  1.72 us (7%)
  starting transfers between devices  0.52 us (2%)
    all_to_all x1, blocking collectives, per_device(): lax.all_to_all(corr, ('win', 'rcv'), split_axis=0, concat_axis=0, tiled=T...  17.7 us
    pallas_call x1, Pallas kernels, correlate(): pl.pallas_call(functools.partial(correlate_kernel, peers=peers, chunk=chu...  2.36 us
    ppermute x1, waiting for transfers between devices, per_device(): lax.ppermute(spectra, 'rcv', [(i, (i + step) % peers) for i in range(peer...  1.72 us
    pallas_call x1, Pallas kernels, stack_blocks(): pl.pallas_call(stack_kernel, out_shape=jax.ShapeDtypeStruct((pairs, block...  1.67 us
    ppermute x1, starting transfers between devices, per_device(): lax.ppermute(spectra, 'rcv', [(i, (i + step) % peers) for i in range(peer...  0.52 us
  transfers between devices with their start and end apart: 1, of which 1 were waited for; matrix products, arithmetic and copies ran while one was open for 0% of the time, Pallas kernels for 0%

profile of v6, /device:TPU:0, one launch (start us, length us, event | category | flops | bytes accessed | tf_op | source)
XLA Modules:
  0.0 24.1 jit_solution(13989441237334691317)
XLA Ops:
  0.0 0.0 copy-start
  0.0 0.0 copy-start.1
  0.0 0.0 copy-start.2
  0.0 0.5 %collective-permute-start = (bf16[2,2,16,4096]{3,2,1,0:T(8,128)(2,1)}, bf16[2,2,16,4096]{3,2,1,0:T(8,128)(2,1)S(1)}, u32[]{:S(2)}, u32[]{:S(2)}) collective-permute-start(bf16[2,2,16,4096]{3,2,1,0:T(8,128)(2,1)} %refs_3_.1), channel_id=1, source_target_pairs={{0,1},{1,0},{2,3},{3,2},{4,5},{5,4},{6,7},{7,6},{8,9},{9,8},{10,11... | collective-permute-start | bytes 1572872 | tf_op jit(solution)/shard_map/ppermute | solution.py:204
  0.6 1.7 %collective-permute-done.refs_4_ = bf16[2,2,16,4096]{3,2,1,0:T(8,128)(2,1)S(1)} collective-permute-done((bf16[2,2,16,4096]{3,2,1,0:T(8,128)(2,1)}, bf16[2,2,16,4096]{3,2,1,0:T(8,128)(2,1)S(1)}, u32[]{:S(2)}, u32[]{:S(2)}) %collective-permute-start) | collective-permute-done | bytes 524320 | tf_op jit(solution)/shard_map/ppermute | solution.py:204
  2.3 0.0 copy-done
  2.3 0.1 copy-done.1
  2.4 0.0 copy-done.2
  2.4 2.4 %correlate.1 = bf16[16,2,32,128]{3,2,1,0:T(8,128)(2,1)S(1)} custom-call(s32[8]{0:T(128)S(1)} %copy-done.2, bf16[2,272,4096]{2,1,0:T(8,128)(2,1)S(1)} %copy-done, bf16[256,256]{1,0:T(8,128)(2,1)S(1)} %make_flip.1.refs_2_, bf16[2,2,16,4096]{3,2,1,0:T(8,128)(2,1)S(1)} %copy-done.1, bf16[2,2,16,4096]{3,2,1,0:T(8,128)(2,1)S(1)} %collective-permute-done.refs_4_), custom_call_target="tpu_custom_call" | custom-call | tf_op jit(solution)/shard_map/correlate/pallas_call | solution.py:129
  4.8 17.7 %all_to_all.5.x_ref = bf16[32,32,128]{2,1,0:T(8,128)(2,1)S(1)} all-to-all(bf16[32,32,128]{2,1,0:T(8,128)(2,1)S(1)} %bitcast.4), channel_id=1, replica_groups=mesh['win'=16,'rcv'=2] {'win','rcv'}, dimensions={0} | all-to-all | bytes 524288 | tf_op jit(solution)/shard_map/all_to_all | solution.py:207
  22.5 1.7 %bisquare_stack.1 = f32[128,32]{1,0:T(8,128)} custom-call(bf16[32,32,128]{2,1,0:T(8,128)(2,1)S(1)} %all_to_all.5.x_ref), custom_call_target="tpu_custom_call" | custom-call | tf_op jit(solution)/shard_map/bisquare_stack/pallas_call | solution.py:181
  (1 shorter events, 0.0 us)
Async XLA Ops:
  0.0 2.3 %copy-start = (bf16[2,272,4096]{2,1,0:T(8,128)(2,1)S(1)}, bf16[2,272,4096]{2,1,0:T(8,128)(2,1)}, u32[]{:S(2)}) copy-start(bf16[2,272,4096]{2,1,0:T(8,128)(2,1)} %constant.2.clone.refs_1_) | copy-start | bytes 13369348
  0.0 2.4 %copy-start.1 = (bf16[2,2,16,4096]{3,2,1,0:T(8,128)(2,1)S(1)}, bf16[2,2,16,4096]{3,2,1,0:T(8,128)(2,1)}, u32[]{:S(2)}) copy-start(bf16[2,2,16,4096]{3,2,1,0:T(8,128)(2,1)} %refs_3_.1) | copy-start | bytes 1572868
  0.0 2.4 %copy-start.2 = (s32[8]{0:T(128)S(1)}, s32[8]{0:T(128)}, u32[]{:S(2)}) copy-start(s32[8]{0:T(128)} %refs_0_.1) | copy-start | bytes 100
  0.0 2.3 %collective-permute-start = (bf16[2,2,16,4096]{3,2,1,0:T(8,128)(2,1)}, bf16[2,2,16,4096]{3,2,1,0:T(8,128)(2,1)S(1)}, u32[]{:S(2)}, u32[]{:S(2)}) collective-permute-start(bf16[2,2,16,4096]{3,2,1,0:T(8,128)(2,1)} %refs_3_.1), channel_id=1, source_target_pairs={{0,1},{1,0},{2,3},{3,2},{4,5},{5,4},{6,7},{7,6},{8,9},{9,8},{10,11... | collective-permute-start | bytes 1572872 | tf_op jit(solution)/shard_map/ppermute | solution.py:204

commit v7 on v6

--- a/solution.py
+++ b/solution.py
@@ -80,16 +80,17 @@
                         first + w, part, :, bins
                     ].astype(jnp.float32)
         reals, imags = [], []
-        for k in range(peers):
-            receivers = slice(k * chan_count, (k + 1) * chan_count)
-            for t in range(items):
-                w = t // source_count
-                real_p = float_ref[w, 0, receivers, bins]
-                imag_q = float_ref[w, 1, receivers, bins]
-                real_a = float_ref[w, 0, pl.ds(rows[t], 1), bins]
-                imag_b = float_ref[w, 1, pl.ds(rows[t], 1), bins]
-                reals.append((real_a * real_p + imag_b * imag_q).astype(jnp.bfloat16))
-                imags.append((imag_b * real_p - real_a * imag_q).astype(jnp.bfloat16))
+        for t in range(items):
+            w = t // source_count
+            real_p = float_ref[w, 0, :, bins]
+            imag_q = float_ref[w, 1, :, bins]
+            real_a = float_ref[w, 0, pl.ds(rows[t], 1), bins]
+            imag_b = float_ref[w, 1, pl.ds(rows[t], 1), bins]
+            reals.append((real_a * real_p + imag_b * imag_q).astype(jnp.bfloat16))
+            imags.append((imag_b * real_p - real_a * imag_q).astype(jnp.bfloat16))
+        receivers = [slice(k * chan_count, (k + 1) * chan_count) for k in range(peers)]
+        reals = [term[part] for part in receivers for term in reals]
+        imags = [term[part] for part in receivers for term in imags]
         for index, terms, sum_ref in ((0, reals, even_ref), (1, imags, odd_ref)):
             term = lax.dot_general(
                 table_ref[index, :, bins],
@@ -123,7 +124,7 @@
     peers = len(blocks)
     items = share(win_count, source_count, peers)
     rows = table.shape[1]
-    chunk = min(512, bin_count)
+    chunk = min(1024, bin_count)
     width = items * chan_count
     vmem = pl.BlockSpec(memory_space=pltpu.VMEM)
     return pl.pallas_call(
@@ -146,34 +147,34 @@
     count, block, pairs = x_ref.shape
     for n in range(count):
         y_ref[n] = x_ref[n].astype(jnp.float32)
-    rows = 8
-    centers = []
-    for start in range(0, block, rows):
-        raw = [y_ref[n, start : start + rows, :] for n in range(count)]
-        mean = tree_sum(raw) * (1.0 / count)
-        samples = [x - mean for x in raw]
-        variance = tree_sum([x * x for x in samples]) * (1.0 / count)
-        center = jnp.zeros_like(mean)
-        for iteration in range(ITERS):
-            scale_two = variance + center * center + EPSILON
-            inverse = 1.0 / (TUKEY * TUKEY * scale_two)
-            weights, products = [], []
-            for x in samples:
-                deviation = x - center
-                kept = jnp.maximum(1.0 - deviation * deviation * inverse, 0.0)
-                weight = kept * kept
-                weights.append(weight)
-                products.append(weight * x)
-            center = tree_sum(products) / tree_sum(weights)
-        centers.append(center + mean)
-    out_ref[...] = jnp.concatenate(centers, axis=0).T
+    mean = tree_sum([y_ref[n] for n in range(count)]) * (1.0 / count)
+    squares = []
+    for n in range(count):
+        sample = y_ref[n] - mean
+        y_ref[n] = sample
+        squares.append(sample * sample)
+    variance = tree_sum(squares) * (1.0 / count)
+    center = jnp.zeros_like(mean)
+    for iteration in range(ITERS):
+        scale_two = variance + center * center + EPSILON
+        inverse = 1.0 / (TUKEY * TUKEY * scale_two)
+        weights, products = [], []
+        for n in range(count):
+            sample = y_ref[n]
+            deviation = sample - center
+            kept = jnp.maximum(1.0 - deviation * deviation * inverse, 0.0)
+            weight = kept * kept
+            weights.append(weight)
+            products.append(weight * sample)
+        center = tree_sum(products) / tree_sum(weights)
+    out_ref[...] = (center + mean).T
 
 
 def tree_sum(terms):
-    sums = list(terms[:4])
-    for index, term in enumerate(terms[4:]):
-        sums[index % 4] = sums[index % 4] + term
-    return (sums[0] + sums[1]) + (sums[2] + sums[3])
+    sums = list(terms[:2])
+    for index, term in enumerate(terms[2:]):
+        sums[index % 2] = sums[index % 2] + term
+    return sums[0] + sums[1]
 
 
 def stack_blocks(samples, source_count):

time: 24.3 us -> 24.4 us (level)
  no operation moved by 1% of the time
where the time goes in v7:
time: 24.4 us; the launch traced here: 24.2 us
  blocking collectives  17.7 us (73%)
  Pallas kernels  4.14 us (17%)
  waiting for transfers between devices  1.72 us (7%)
  starting transfers between devices  0.52 us (2%)
    all_to_all x1, blocking collectives, per_device(): lax.all_to_all(corr, ('win', 'rcv'), split_axis=0, concat_axis=0, tiled=T...  17.7 us
    pallas_call x1, Pallas kernels, correlate(): pl.pallas_call(functools.partial(correlate_kernel, peers=peers, chunk=chu...  2.43 us
    ppermute x1, waiting for transfers between devices, per_device(): lax.ppermute(spectra, 'rcv', [(i, (i + step) % peers) for i in range(peer...  1.72 us
    pallas_call x1, Pallas kernels, stack_blocks(): pl.pallas_call(stack_kernel, out_shape=jax.ShapeDtypeStruct((pairs, block...  1.68 us
    ppermute x1, starting transfers between devices, per_device(): lax.ppermute(spectra, 'rcv', [(i, (i + step) % peers) for i in range(peer...  0.52 us
  transfers between devices with their start and end apart: 1, of which 1 were waited for; matrix products, arithmetic and copies ran while one was open for 0% of the time, Pallas kernels for 0%

profile of v7, /device:TPU:0, one launch (start us, length us, event | category | flops | bytes accessed | tf_op | source)
XLA Modules:
  0.0 24.2 jit_solution(8096126800874214393)
XLA Ops:
  0.0 0.0 copy-start
  0.0 0.0 copy-start.1
  0.0 0.0 copy-start.2
  0.0 0.5 %collective-permute-start = (bf16[2,2,16,4096]{3,2,1,0:T(8,128)(2,1)}, bf16[2,2,16,4096]{3,2,1,0:T(8,128)(2,1)S(1)}, u32[]{:S(2)}, u32[]{:S(2)}) collective-permute-start(bf16[2,2,16,4096]{3,2,1,0:T(8,128)(2,1)} %refs_3_.1), channel_id=1, source_target_pairs={{0,1},{1,0},{2,3},{3,2},{4,5},{5,4},{6,7},{7,6},{8,9},{9,8},{10,11... | collective-permute-start | bytes 1572872 | tf_op jit(solution)/shard_map/ppermute | solution.py:205
  0.6 1.7 %collective-permute-done.refs_4_ = bf16[2,2,16,4096]{3,2,1,0:T(8,128)(2,1)S(1)} collective-permute-done((bf16[2,2,16,4096]{3,2,1,0:T(8,128)(2,1)}, bf16[2,2,16,4096]{3,2,1,0:T(8,128)(2,1)S(1)}, u32[]{:S(2)}, u32[]{:S(2)}) %collective-permute-start) | collective-permute-done | bytes 524320 | tf_op jit(solution)/shard_map/ppermute | solution.py:205
  2.3 0.0 copy-done
  2.3 0.1 copy-done.1
  2.4 0.0 copy-done.2
  2.4 2.4 %correlate.1 = bf16[16,2,32,128]{3,2,1,0:T(8,128)(2,1)S(1)} custom-call(s32[8]{0:T(128)S(1)} %copy-done.2, bf16[2,272,4096]{2,1,0:T(8,128)(2,1)S(1)} %copy-done, bf16[256,256]{1,0:T(8,128)(2,1)S(1)} %make_flip.1.refs_2_, bf16[2,2,16,4096]{3,2,1,0:T(8,128)(2,1)S(1)} %copy-done.1, bf16[2,2,16,4096]{3,2,1,0:T(8,128)(2,1)S(1)} %collective-permute-done.refs_4_), custom_call_target="tpu_custom_call" | custom-call | tf_op jit(solution)/shard_map/correlate/pallas_call | solution.py:130
  4.8 17.7 %all_to_all.5.x_ref = bf16[32,32,128]{2,1,0:T(8,128)(2,1)S(1)} all-to-all(bf16[32,32,128]{2,1,0:T(8,128)(2,1)S(1)} %bitcast.4), channel_id=1, replica_groups=mesh['win'=16,'rcv'=2] {'win','rcv'}, dimensions={0} | all-to-all | bytes 524288 | tf_op jit(solution)/shard_map/all_to_all | solution.py:208
  22.5 1.7 %bisquare_stack.1 = f32[128,32]{1,0:T(8,128)} custom-call(bf16[32,32,128]{2,1,0:T(8,128)(2,1)S(1)} %all_to_all.5.x_ref), custom_call_target="tpu_custom_call" | custom-call | tf_op jit(solution)/shard_map/bisquare_stack/pallas_call | solution.py:182
  (1 shorter events, 0.0 us)
Async XLA Ops:
  0.0 2.3 %copy-start = (bf16[2,272,4096]{2,1,0:T(8,128)(2,1)S(1)}, bf16[2,272,4096]{2,1,0:T(8,128)(2,1)}, u32[]{:S(2)}) copy-start(bf16[2,272,4096]{2,1,0:T(8,128)(2,1)} %constant.2.clone.refs_1_) | copy-start | bytes 13369348
  0.0 2.4 %copy-start.1 = (bf16[2,2,16,4096]{3,2,1,0:T(8,128)(2,1)S(1)}, bf16[2,2,16,4096]{3,2,1,0:T(8,128)(2,1)}, u32[]{:S(2)}) copy-start(bf16[2,2,16,4096]{3,2,1,0:T(8,128)(2,1)} %refs_3_.1) | copy-start | bytes 1572868
  0.0 2.4 %copy-start.2 = (s32[8]{0:T(128)S(1)}, s32[8]{0:T(128)}, u32[]{:S(2)}) copy-start(s32[8]{0:T(128)} %refs_0_.1) | copy-start | bytes 100
  0.0 2.3 %collective-permute-start = (bf16[2,2,16,4096]{3,2,1,0:T(8,128)(2,1)}, bf16[2,2,16,4096]{3,2,1,0:T(8,128)(2,1)S(1)}, u32[]{:S(2)}, u32[]{:S(2)}) collective-permute-start(bf16[2,2,16,4096]{3,2,1,0:T(8,128)(2,1)} %refs_3_.1), channel_id=1, source_target_pairs={{0,1},{1,0},{2,3},{3,2},{4,5},{5,4},{6,7},{7,6},{8,9},{9,8},{10,11... | collective-permute-start | bytes 1572872 | tf_op jit(solution)/shard_map/ppermute | solution.py:205

commit v8 on v7

--- a/solution.py
+++ b/solution.py
@@ -56,7 +56,7 @@
 def correlate_kernel(*refs, peers, chunk):
     channel_ref, table_ref, flip_ref = refs[:3]
     block_refs = refs[3 : 3 + peers]
-    out_ref, lags_ref, even_ref, odd_ref, float_ref = refs[3 + peers :]
+    out_ref, lags_ref, even_ref, odd_ref, cross_ref, float_ref = refs[3 + peers :]
     win_count, _, chan_count, bin_count = block_refs[0].shape
     source_count = channel_ref.shape[0]
     items = share(win_count, source_count, peers)
@@ -71,37 +71,46 @@
         owner = lax.div(channel, chan_count)
         place = lax.rem(me - owner + peers, peers) * chan_count
         rows.append(place + lax.rem(channel, chan_count))
-    for start in range(0, bin_count, chunk):
-        bins = slice(start, start + chunk)
+    def form_cross(bins):
         for k in range(peers):
             for w in range(windows):
                 for part in range(2):
                     float_ref[w, part, k * chan_count : (k + 1) * chan_count, bins] = block_refs[k][
                         first + w, part, :, bins
                     ].astype(jnp.float32)
-        reals, imags = [], []
         for t in range(items):
             w = t // source_count
             real_p = float_ref[w, 0, :, bins]
             imag_q = float_ref[w, 1, :, bins]
             real_a = float_ref[w, 0, pl.ds(rows[t], 1), bins]
             imag_b = float_ref[w, 1, pl.ds(rows[t], 1), bins]
-            reals.append((real_a * real_p + imag_b * imag_q).astype(jnp.bfloat16))
-            imags.append((imag_b * real_p - real_a * imag_q).astype(jnp.bfloat16))
-        receivers = [slice(k * chan_count, (k + 1) * chan_count) for k in range(peers)]
-        reals = [term[part] for part in receivers for term in reals]
-        imags = [term[part] for part in receivers for term in imags]
-        for index, terms, sum_ref in ((0, reals, even_ref), (1, imags, odd_ref)):
+            real = (real_a * real_p + imag_b * imag_q).astype(jnp.bfloat16)
+            imag = (imag_b * real_p - real_a * imag_q).astype(jnp.bfloat16)
+            for k in range(peers):
+                receivers = slice(k * chan_count, (k + 1) * chan_count)
+                pairs = slice(k * width + t * chan_count, k * width + (t + 1) * chan_count)
+                cross_ref[0, pairs, bins] = real[receivers]
+                cross_ref[1, pairs, bins] = imag[receivers]
+
+    def add_products(bins):
+        for index, sum_ref in ((0, even_ref), (1, odd_ref)):
             term = lax.dot_general(
                 table_ref[index, :, bins],
-                jnp.concatenate(terms, axis=0),
+                cross_ref[index, :, bins],
                 (((1,), (1,)), ((), ())),
                 preferred_element_type=jnp.float32,
             )
-            if start == 0:
+            if bins.start == 0:
                 sum_ref[...] = term
             else:
                 sum_ref[...] += term
+
+    chunks = [slice(start, start + chunk) for start in range(0, bin_count, chunk)]
+    form_cross(chunks[0])
+    for index, bins in enumerate(chunks):
+        if index + 1 < len(chunks):
+            form_cross(chunks[index + 1])
+        add_products(bins)
     lags_ref[half:, :] = even_ref[:half, :] + odd_ref[:half, :]
     back = (even_ref[...] - odd_ref[...]).astype(jnp.bfloat16)
     turned = jnp.dot(flip_ref[...], back[:half], preferred_element_type=jnp.float32)
@@ -124,7 +133,7 @@
     peers = len(blocks)
     items = share(win_count, source_count, peers)
     rows = table.shape[1]
-    chunk = min(1024, bin_count)
+    chunk = min(512, bin_count)
     width = items * chan_count
     vmem = pl.BlockSpec(memory_space=pltpu.VMEM)
     return pl.pallas_call(
@@ -136,6 +145,7 @@
             pltpu.VMEM((L, peers * width), jnp.float32),
             pltpu.VMEM((rows, peers * width), jnp.float32),
             pltpu.VMEM((rows, peers * width), jnp.float32),
+            pltpu.VMEM((2, peers * width, bin_count), jnp.bfloat16),
             pltpu.VMEM((max(1, items // source_count), 2, peers * chan_count, bin_count), jnp.float32),
         ],
         compiler_params=pltpu.CompilerParams(vmem_limit_bytes=VMEM_LIMIT),
@@ -156,13 +166,12 @@
     variance = tree_sum(squares) * (1.0 / count)
     center = jnp.zeros_like(mean)
     for iteration in range(ITERS):
-        scale_two = variance + center * center + EPSILON
-        inverse = 1.0 / (TUKEY * TUKEY * scale_two)
+        limit = TUKEY * TUKEY * (variance + center * center + EPSILON)
         weights, products = [], []
         for n in range(count):
             sample = y_ref[n]
             deviation = sample - center
-            kept = jnp.maximum(1.0 - deviation * deviation * inverse, 0.0)
+            kept = jnp.maximum(limit - deviation * deviation, 0.0)
             weight = kept * kept
             weights.append(weight)
             products.append(weight * sample)

time: 24.4 us -> 24.2 us (level)
  no operation moved by 1% of the time
where the time goes in v8:
time: 24.2 us; the launch traced here: 24 us
  blocking collectives  17.7 us (73%)
  Pallas kernels  3.96 us (16%)
  waiting for transfers between devices  1.72 us (7%)
  starting transfers between devices  0.52 us (2%)
    all_to_all x1, blocking collectives, per_device(): lax.all_to_all(corr, ('win', 'rcv'), split_axis=0, concat_axis=0, tiled=T...  17.7 us
    pallas_call x1, Pallas kernels, correlate(): pl.pallas_call(functools.partial(correlate_kernel, peers=peers, chunk=chu...  2.35 us
    ppermute x1, waiting for transfers between devices, per_device(): lax.ppermute(spectra, 'rcv', [(i, (i + step) % peers) for i in range(peer...  1.72 us
    pallas_call x1, Pallas kernels, stack_blocks(): pl.pallas_call(stack_kernel, out_shape=jax.ShapeDtypeStruct((pairs, block...  1.57 us
    ppermute x1, starting transfers between devices, per_device(): lax.ppermute(spectra, 'rcv', [(i, (i + step) % peers) for i in range(peer...  0.52 us
  transfers between devices with their start and end apart: 1, of which 1 were waited for; matrix products, arithmetic and copies ran while one was open for 0% of the time, Pallas kernels for 0%

profile of v8, /device:TPU:0, one launch (start us, length us, event | category | flops | bytes accessed | tf_op | source)
XLA Modules:
  0.0 24.0 jit_solution(18137856201607201672)
XLA Ops:
  0.0 0.0 copy-start
  0.0 0.0 copy-start.1
  0.0 0.0 copy-start.2
  0.0 0.5 %collective-permute-start = (bf16[2,2,16,4096]{3,2,1,0:T(8,128)(2,1)}, bf16[2,2,16,4096]{3,2,1,0:T(8,128)(2,1)S(1)}, u32[]{:S(2)}, u32[]{:S(2)}) collective-permute-start(bf16[2,2,16,4096]{3,2,1,0:T(8,128)(2,1)} %refs_3_.1), channel_id=1, source_target_pairs={{0,1},{1,0},{2,3},{3,2},{4,5},{5,4},{6,7},{7,6},{8,9},{9,8},{10,11... | collective-permute-start | bytes 1572872 | tf_op jit(solution)/shard_map/ppermute | solution.py:214
  0.6 1.7 %collective-permute-done.refs_4_ = bf16[2,2,16,4096]{3,2,1,0:T(8,128)(2,1)S(1)} collective-permute-done((bf16[2,2,16,4096]{3,2,1,0:T(8,128)(2,1)}, bf16[2,2,16,4096]{3,2,1,0:T(8,128)(2,1)S(1)}, u32[]{:S(2)}, u32[]{:S(2)}) %collective-permute-start) | collective-permute-done | bytes 524320 | tf_op jit(solution)/shard_map/ppermute | solution.py:214
  2.3 0.0 copy-done
  2.3 0.1 copy-done.1
  2.4 0.0 copy-done.2
  2.4 2.4 %correlate.1 = bf16[16,2,32,128]{3,2,1,0:T(8,128)(2,1)S(1)} custom-call(s32[8]{0:T(128)S(1)} %copy-done.2, bf16[2,272,4096]{2,1,0:T(8,128)(2,1)S(1)} %copy-done, bf16[256,256]{1,0:T(8,128)(2,1)S(1)} %make_flip.1.refs_2_, bf16[2,2,16,4096]{3,2,1,0:T(8,128)(2,1)S(1)} %copy-done.1, bf16[2,2,16,4096]{3,2,1,0:T(8,128)(2,1)S(1)} %collective-permute-done.refs_4_), custom_call_target="tpu_custom_call" | custom-call | tf_op jit(solution)/shard_map/correlate/pallas_call | solution.py:139
  4.7 17.7 %all_to_all.5.x_ref = bf16[32,32,128]{2,1,0:T(8,128)(2,1)S(1)} all-to-all(bf16[32,32,128]{2,1,0:T(8,128)(2,1)S(1)} %bitcast.4), channel_id=1, replica_groups=mesh['win'=16,'rcv'=2] {'win','rcv'}, dimensions={0} | all-to-all | bytes 524288 | tf_op jit(solution)/shard_map/all_to_all | solution.py:217
  22.5 1.6 %bisquare_stack.1 = f32[128,32]{1,0:T(8,128)} custom-call(bf16[32,32,128]{2,1,0:T(8,128)(2,1)S(1)} %all_to_all.5.x_ref), custom_call_target="tpu_custom_call" | custom-call | tf_op jit(solution)/shard_map/bisquare_stack/pallas_call | solution.py:191
  (1 shorter events, 0.0 us)
Async XLA Ops:
  0.0 2.3 %copy-start = (bf16[2,272,4096]{2,1,0:T(8,128)(2,1)S(1)}, bf16[2,272,4096]{2,1,0:T(8,128)(2,1)}, u32[]{:S(2)}) copy-start(bf16[2,272,4096]{2,1,0:T(8,128)(2,1)} %constant.2.clone.refs_1_) | copy-start | bytes 13369348
  0.0 2.4 %copy-start.1 = (bf16[2,2,16,4096]{3,2,1,0:T(8,128)(2,1)S(1)}, bf16[2,2,16,4096]{3,2,1,0:T(8,128)(2,1)}, u32[]{:S(2)}) copy-start(bf16[2,2,16,4096]{3,2,1,0:T(8,128)(2,1)} %refs_3_.1) | copy-start | bytes 1572868
  0.0 2.4 %copy-start.2 = (s32[8]{0:T(128)S(1)}, s32[8]{0:T(128)}, u32[]{:S(2)}) copy-start(s32[8]{0:T(128)} %refs_0_.1) | copy-start | bytes 100
  0.0 2.3 %collective-permute-start = (bf16[2,2,16,4096]{3,2,1,0:T(8,128)(2,1)}, bf16[2,2,16,4096]{3,2,1,0:T(8,128)(2,1)S(1)}, u32[]{:S(2)}, u32[]{:S(2)}) collective-permute-start(bf16[2,2,16,4096]{3,2,1,0:T(8,128)(2,1)} %refs_3_.1), channel_id=1, source_target_pairs={{0,1},{1,0},{2,3},{3,2},{4,5},{5,4},{6,7},{7,6},{8,9},{9,8},{10,11... | collective-permute-start | bytes 1572872 | tf_op jit(solution)/shard_map/ppermute | solution.py:214

commit v9 on v8

--- a/solution.py
+++ b/solution.py
@@ -17,32 +17,38 @@
 EPSILON = 1e-06
 
 
-def make_tables(bin_count, lag_count, rows):
+def make_tables(bin_count, lag_count):
     freq = np.arange(bin_count, dtype=np.int64)
-    shifts = np.arange(lag_count // 2 + 1, dtype=np.int64)
-    phase = shifts[:, None] * freq[None, :] % (2 * bin_count)
+    shifts = np.arange(lag_count // 2, dtype=np.int64) + 1
+    phase = freq[:, None] * shifts[None, :] % (2 * bin_count)
     angle = phase * (2.0 * np.pi / (2 * bin_count))
-    factor = np.where(freq == 0, 1.0, 2.0) / np.sqrt(8.0 * bin_count)
-    table = np.zeros((2, rows, bin_count), np.float32)
-    table[0, : len(shifts)] = np.cos(angle) * factor
-    table[1, : len(shifts)] = -np.sin(angle) * factor
-    return jnp.asarray(table.astype(jnp.bfloat16))
-
-
-def flip_kernel(out_ref):
-    lag = lax.broadcasted_iota(jnp.int32, out_ref.shape, 0)
-    shift = lax.broadcasted_iota(jnp.int32, out_ref.shape, 1)
-    out_ref[...] = (lag + shift == out_ref.shape[0]).astype(jnp.float32).astype(jnp.bfloat16)
-
-
-def make_flip(half, meanwhile):
+    factor = np.where(freq == 0, 1.0, 2.0)[:, None] / np.sqrt(8.0 * bin_count)
+    table = np.stack([np.cos(angle) * factor, -np.sin(angle) * factor])
+    return jnp.asarray(table.astype(np.float32).astype(jnp.bfloat16))
+
+
+def level_at_zero(bin_count):
+    return float(np.float32(2.0 / np.sqrt(8.0 * bin_count)).astype(jnp.bfloat16))
+
+
+def order_kernel(out_ref):
+    half = out_ref.shape[1]
+    lag = lax.broadcasted_iota(jnp.int32, (half, half), 0)
+    column = lax.broadcasted_iota(jnp.int32, (half, half), 1)
+    behind = lag + column == half - 1
+    ahead = lag == jnp.where(column == half - 1, 0, column + 1)
+    out_ref[0] = behind.astype(jnp.float32).astype(jnp.bfloat16)
+    out_ref[1] = ahead.astype(jnp.float32).astype(jnp.bfloat16)
+
+
+def make_order(half, meanwhile):
     return pl.pallas_call(
-        flip_kernel,
-        out_shape=jax.ShapeDtypeStruct((half, half), jnp.bfloat16),
+        order_kernel,
+        out_shape=jax.ShapeDtypeStruct((2, half, half), jnp.bfloat16),
         out_specs=pl.BlockSpec(memory_space=pltpu.VMEM),
         compiler_params=pltpu.CompilerParams(vmem_limit_bytes=VMEM_LIMIT),
         cost_estimate=pl.CostEstimate(flops=meanwhile, bytes_accessed=0, transcendentals=0),
-        name="make_flip",
+        name="make_order",
     )()
 
 
@@ -54,15 +60,15 @@
 
 
 def correlate_kernel(*refs, peers, chunk):
-    channel_ref, table_ref, flip_ref = refs[:3]
+    channel_ref, table_ref, order_ref = refs[:3]
     block_refs = refs[3 : 3 + peers]
-    out_ref, lags_ref, even_ref, odd_ref, cross_ref, float_ref = refs[3 + peers :]
+    out_ref, lags_ref, even_ref, odd_ref, zero_ref, cross_ref, float_ref = refs[3 + peers :]
     win_count, _, chan_count, bin_count = block_refs[0].shape
     source_count = channel_ref.shape[0]
     items = share(win_count, source_count, peers)
     windows = float_ref.shape[0]
     parts, _, block, width = out_ref.shape
-    half = flip_ref.shape[0]
+    half = order_ref.shape[1]
     me = lax.axis_index("rcv")
     first = lax.div(me * items, source_count)
     rows = []
@@ -91,14 +97,16 @@
                 pairs = slice(k * width + t * chan_count, k * width + (t + 1) * chan_count)
                 cross_ref[0, pairs, bins] = real[receivers]
                 cross_ref[1, pairs, bins] = imag[receivers]
+                level = sum_lanes(real[receivers].astype(jnp.float32))
+                if bins.start == 0:
+                    zero_ref[pairs, :] = level
+                else:
+                    zero_ref[pairs, :] += level
 
     def add_products(bins):
         for index, sum_ref in ((0, even_ref), (1, odd_ref)):
-            term = lax.dot_general(
-                table_ref[index, :, bins],
-                cross_ref[index, :, bins],
-                (((1,), (1,)), ((), ())),
-                preferred_element_type=jnp.float32,
+            term = jnp.dot(
+                cross_ref[index, :, bins], table_ref[index, bins, :], preferred_element_type=jnp.float32
             )
             if bins.start == 0:
                 sum_ref[...] = term
@@ -111,14 +119,18 @@
         if index + 1 < len(chunks):
             form_cross(chunks[index + 1])
         add_products(bins)
-    lags_ref[half:, :] = even_ref[:half, :] + odd_ref[:half, :]
-    back = (even_ref[...] - odd_ref[...]).astype(jnp.bfloat16)
-    turned = jnp.dot(flip_ref[...], back[:half], preferred_element_type=jnp.float32)
-    lags_ref[:half, :] = jnp.where(
-        lax.broadcasted_iota(jnp.int32, turned.shape, 0) == 0,
-        back[half : half + 16].astype(jnp.float32)[:1],
-        turned,
-    )
+    first_bin = cross_ref[0, :, :128].astype(jnp.float32)[:, :1]
+    level = jnp.sum(zero_ref[...], axis=1, keepdims=True) - 0.5 * first_bin
+    at_zero = level * level_at_zero(bin_count)
+    column = lax.broadcasted_iota(jnp.int32, even_ref.shape, 1)
+    ahead = jnp.where(column == half - 1, at_zero, even_ref[...] + odd_ref[...])
+    for index, side in ((0, even_ref[...] - odd_ref[...]), (1, ahead)):
+        lags_ref[index * half : (index + 1) * half, :] = lax.dot_general(
+            order_ref[index],
+            side.astype(jnp.bfloat16),
+            (((1,), (1,)), ((), ())),
+            preferred_element_type=jnp.float32,
+        )
     for k in range(peers):
         owner = lax.rem(me - k + peers, peers)
         for part in range(parts):
@@ -127,12 +139,17 @@
             ].astype(jnp.bfloat16)
 
 
-def correlate(source_channel, table, flip, blocks, parts):
+def sum_lanes(values):
+    tiles = [values[:, start : start + 128] for start in range(0, values.shape[1], 128)]
+    return tree_sum(tiles)
+
+
+def correlate(source_channel, table, order, blocks, parts):
     win_count, _, chan_count, bin_count = blocks[0].shape
     source_count = source_channel.shape[0]
     peers = len(blocks)
     items = share(win_count, source_count, peers)
-    rows = table.shape[1]
+    half = table.shape[2]
     chunk = min(512, bin_count)
     width = items * chan_count
     vmem = pl.BlockSpec(memory_space=pltpu.VMEM)
@@ -143,14 +160,15 @@
         out_specs=vmem,
         scratch_shapes=[
             pltpu.VMEM((L, peers * width), jnp.float32),
-            pltpu.VMEM((rows, peers * width), jnp.float32),
-            pltpu.VMEM((rows, peers * width), jnp.float32),
+            pltpu.VMEM((peers * width, half), jnp.float32),
+            pltpu.VMEM((peers * width, half), jnp.float32),
+            pltpu.VMEM((peers * width, 128), jnp.float32),
             pltpu.VMEM((2, peers * width, bin_count), jnp.bfloat16),
             pltpu.VMEM((max(1, items // source_count), 2, peers * chan_count, bin_count), jnp.float32),
         ],
         compiler_params=pltpu.CompilerParams(vmem_limit_bytes=VMEM_LIMIT),
         name="correlate",
-    )(source_channel, table, flip, *blocks)
+    )(source_channel, table, order, *blocks)
 
 
 def stack_kernel(x_ref, out_ref, y_ref):
@@ -207,12 +225,12 @@
     parts = lax.axis_size("win")
     block = L // parts
     items = share(win_count, source_count, peers)
-    table = make_tables(bin_count, L, L // 2 + 16)
-    flip = make_flip(L // 2, 2000 * table.size)
+    table = make_tables(bin_count, L)
+    order = make_order(L // 2, 2000 * table.size)
     blocks = [spectra]
     for step in range(1, peers):
         blocks.append(lax.ppermute(spectra, "rcv", [(i, (i + step) % peers) for i in range(peers)]))
-    corr = correlate(source_channel, table, flip, blocks, parts)
+    corr = correlate(source_channel, table, order, blocks, parts)
     corr = corr.reshape(parts * peers, block, items * chan_count)
     moved = lax.all_to_all(corr, ("win", "rcv"), split_axis=0, concat_axis=0, tiled=True)
     if items != source_count:

time: 24.2 us -> 24.5 us (1.012)
  Pallas kernels: 3.96 us -> 4.34 us
    pallas_call x1, Pallas kernels: 2.35 us -> 2.72 us  [correlate(): pl.pallas_call(functools.partial(correlate_kernel, peers=peers, chunk=chu...]
where the time goes in v9:
time: 24.5 us; the launch traced here: 24.3 us
  blocking collectives  17.7 us (72%)
  Pallas kernels  4.34 us (18%)
  waiting for transfers between devices  1.7 us (7%)
  starting transfers between devices  0.52 us (2%)
    all_to_all x1, blocking collectives, per_device(): lax.all_to_all(corr, ('win', 'rcv'), split_axis=0, concat_axis=0, tiled=T...  17.7 us
    pallas_call x1, Pallas kernels, correlate(): pl.pallas_call(functools.partial(correlate_kernel, peers=peers, chunk=chu...  2.72 us
    ppermute x1, waiting for transfers between devices, per_device(): lax.ppermute(spectra, 'rcv', [(i, (i + step) % peers) for i in range(peer...  1.7 us
    pallas_call x1, Pallas kernels, stack_blocks(): pl.pallas_call(stack_kernel, out_shape=jax.ShapeDtypeStruct((pairs, block...  1.57 us
    ppermute x1, starting transfers between devices, per_device(): lax.ppermute(spectra, 'rcv', [(i, (i + step) % peers) for i in range(peer...  0.52 us
  transfers between devices with their start and end apart: 1, of which 1 were waited for; matrix products, arithmetic and copies ran while one was open for 0% of the time, Pallas kernels for 0%

profile of v9, /device:TPU:0, one launch (start us, length us, event | category | flops | bytes accessed | tf_op | source)
XLA Modules:
  0.0 24.3 jit_solution(2896207244394502139)
XLA Ops:
  0.0 0.0 copy-start
  0.0 0.0 copy-start.1
  0.0 0.0 copy-start.2
  0.0 0.5 %collective-permute-start = (bf16[2,2,16,4096]{3,2,1,0:T(8,128)(2,1)}, bf16[2,2,16,4096]{3,2,1,0:T(8,128)(2,1)S(1)}, u32[]{:S(2)}, u32[]{:S(2)}) collective-permute-start(bf16[2,2,16,4096]{3,2,1,0:T(8,128)(2,1)} %refs_3_.1), channel_id=1, source_target_pairs={{0,1},{1,0},{2,3},{3,2},{4,5},{5,4},{6,7},{7,6},{8,9},{9,8},{10,11... | collective-permute-start | bytes 1572872 | tf_op jit(solution)/shard_map/ppermute | solution.py:232
  0.6 1.7 %collective-permute-done.refs_4_ = bf16[2,2,16,4096]{3,2,1,0:T(8,128)(2,1)S(1)} collective-permute-done((bf16[2,2,16,4096]{3,2,1,0:T(8,128)(2,1)}, bf16[2,2,16,4096]{3,2,1,0:T(8,128)(2,1)S(1)}, u32[]{:S(2)}, u32[]{:S(2)}) %collective-permute-start) | collective-permute-done | bytes 524320 | tf_op jit(solution)/shard_map/ppermute | solution.py:232
  2.3 0.0 copy-done
  2.3 0.0 copy-done.1
  2.3 0.0 copy-done.2
  2.3 2.7 %correlate.1 = bf16[16,2,32,128]{3,2,1,0:T(8,128)(2,1)S(1)} custom-call(s32[8]{0:T(128)S(1)} %copy-done.2, bf16[2,4096,256]{2,1,0:T(8,128)(2,1)S(1)} %copy-done, bf16[2,256,256]{2,1,0:T(8,128)(2,1)S(1)} %make_order.1.refs_2_, bf16[2,2,16,4096]{3,2,1,0:T(8,128)(2,1)S(1)} %copy-done.1, bf16[2,2,16,4096]{3,2,1,0:T(8,128)(2,1)S(1)} %collective-permute-done.refs_4_), custom_call_target="tpu_custom_call" | custom-call | tf_op jit(solution)/shard_map/correlate/pallas_call | solution.py:156
  5.0 17.7 %all_to_all.5.x_ref = bf16[32,32,128]{2,1,0:T(8,128)(2,1)S(1)} all-to-all(bf16[32,32,128]{2,1,0:T(8,128)(2,1)S(1)} %bitcast.4), channel_id=1, replica_groups=mesh['win'=16,'rcv'=2] {'win','rcv'}, dimensions={0} | all-to-all | bytes 524288 | tf_op jit(solution)/shard_map/all_to_all | solution.py:235
  22.7 1.6 %bisquare_stack.1 = f32[128,32]{1,0:T(8,128)} custom-call(bf16[32,32,128]{2,1,0:T(8,128)(2,1)S(1)} %all_to_all.5.x_ref), custom_call_target="tpu_custom_call" | custom-call | tf_op jit(solution)/shard_map/bisquare_stack/pallas_call | solution.py:209
  (1 shorter events, 0.0 us)
Async XLA Ops:
  0.0 2.3 %copy-start = (bf16[2,4096,256]{2,1,0:T(8,128)(2,1)S(1)}, bf16[2,4096,256]{2,1,0:T(8,128)(2,1)}, u32[]{:S(2)}) copy-start(bf16[2,4096,256]{2,1,0:T(8,128)(2,1)} %constant.2.clone.refs_1_) | copy-start | bytes 12582916
  0.0 2.3 %copy-start.1 = (bf16[2,2,16,4096]{3,2,1,0:T(8,128)(2,1)S(1)}, bf16[2,2,16,4096]{3,2,1,0:T(8,128)(2,1)}, u32[]{:S(2)}) copy-start(bf16[2,2,16,4096]{3,2,1,0:T(8,128)(2,1)} %refs_3_.1) | copy-start | bytes 1572868
  0.0 2.3 %copy-start.2 = (s32[8]{0:T(128)S(1)}, s32[8]{0:T(128)}, u32[]{:S(2)}) copy-start(s32[8]{0:T(128)} %refs_0_.1) | copy-start | bytes 100
  0.0 2.3 %collective-permute-start = (bf16[2,2,16,4096]{3,2,1,0:T(8,128)(2,1)}, bf16[2,2,16,4096]{3,2,1,0:T(8,128)(2,1)S(1)}, u32[]{:S(2)}, u32[]{:S(2)}) collective-permute-start(bf16[2,2,16,4096]{3,2,1,0:T(8,128)(2,1)} %refs_3_.1), channel_id=1, source_target_pairs={{0,1},{1,0},{2,3},{3,2},{4,5},{5,4},{6,7},{7,6},{8,9},{9,8},{10,11... | collective-permute-start | bytes 1572872 | tf_op jit(solution)/shard_map/ppermute | solution.py:232

commit v10 on v8

--- a/solution.py
+++ b/solution.py
@@ -53,7 +53,7 @@
     return items
 
 
-def correlate_kernel(*refs, peers, chunk):
+def correlate_kernel(*refs, peers, chunk, piece):
     channel_ref, table_ref, flip_ref = refs[:3]
     block_refs = refs[3 : 3 + peers]
     out_ref, lags_ref, even_ref, odd_ref, cross_ref, float_ref = refs[3 + peers :]
@@ -72,25 +72,24 @@
         place = lax.rem(me - owner + peers, peers) * chan_count
         rows.append(place + lax.rem(channel, chan_count))
     def form_cross(bins):
-        for k in range(peers):
-            for w in range(windows):
-                for part in range(2):
-                    float_ref[w, part, k * chan_count : (k + 1) * chan_count, bins] = block_refs[k][
-                        first + w, part, :, bins
-                    ].astype(jnp.float32)
-        for t in range(items):
-            w = t // source_count
-            real_p = float_ref[w, 0, :, bins]
-            imag_q = float_ref[w, 1, :, bins]
-            real_a = float_ref[w, 0, pl.ds(rows[t], 1), bins]
-            imag_b = float_ref[w, 1, pl.ds(rows[t], 1), bins]
-            real = (real_a * real_p + imag_b * imag_q).astype(jnp.bfloat16)
-            imag = (imag_b * real_p - real_a * imag_q).astype(jnp.bfloat16)
-            for k in range(peers):
-                receivers = slice(k * chan_count, (k + 1) * chan_count)
-                pairs = slice(k * width + t * chan_count, k * width + (t + 1) * chan_count)
-                cross_ref[0, pairs, bins] = real[receivers]
-                cross_ref[1, pairs, bins] = imag[receivers]
+        for w in range(windows):
+            sides = []
+            for part in range(2):
+                pieces = [block_refs[k][first + w, part, :, bins] for k in range(peers)]
+                side = jnp.concatenate(pieces, axis=0).astype(jnp.float32)
+                float_ref[w, part, :, bins] = side
+                sides.append(side)
+            real_p, imag_q = sides
+            for t in range(w * source_count, min(items, (w + 1) * source_count)):
+                real_a = float_ref[w, 0, pl.ds(rows[t], 1), bins]
+                imag_b = float_ref[w, 1, pl.ds(rows[t], 1), bins]
+                real = (real_a * real_p + imag_b * imag_q).astype(jnp.bfloat16)
+                imag = (imag_b * real_p - real_a * imag_q).astype(jnp.bfloat16)
+                for k in range(peers):
+                    receivers = slice(k * chan_count, (k + 1) * chan_count)
+                    pairs = slice(k * width + t * chan_count, k * width + (t + 1) * chan_count)
+                    cross_ref[0, pairs, bins] = real[receivers]
+                    cross_ref[1, pairs, bins] = imag[receivers]
 
     def add_products(bins):
         for index, sum_ref in ((0, even_ref), (1, odd_ref)):
@@ -106,11 +105,12 @@
                 sum_ref[...] += term
 
     chunks = [slice(start, start + chunk) for start in range(0, bin_count, chunk)]
-    form_cross(chunks[0])
-    for index, bins in enumerate(chunks):
-        if index + 1 < len(chunks):
-            form_cross(chunks[index + 1])
-        add_products(bins)
+    for index in range(len(chunks) + 1):
+        if index < len(chunks):
+            for start in range(chunks[index].start, chunks[index].stop, piece):
+                form_cross(slice(start, start + piece))
+        if index > 0:
+            add_products(chunks[index - 1])
     lags_ref[half:, :] = even_ref[:half, :] + odd_ref[:half, :]
     back = (even_ref[...] - odd_ref[...]).astype(jnp.bfloat16)
     turned = jnp.dot(flip_ref[...], back[:half], preferred_element_type=jnp.float32)
@@ -133,11 +133,11 @@
     peers = len(blocks)
     items = share(win_count, source_count, peers)
     rows = table.shape[1]
-    chunk = min(512, bin_count)
+    chunk = min(1024, bin_count)
     width = items * chan_count
     vmem = pl.BlockSpec(memory_space=pltpu.VMEM)
     return pl.pallas_call(
-        functools.partial(correlate_kernel, peers=peers, chunk=chunk),
+        functools.partial(correlate_kernel, peers=peers, chunk=chunk, piece=min(256, chunk)),
         out_shape=jax.ShapeDtypeStruct((parts, peers, L // parts, width), jnp.bfloat16),
         in_specs=[pl.BlockSpec(memory_space=pltpu.SMEM), vmem, vmem] + [vmem] * peers,
         out_specs=vmem,

time: 24.2 us -> 24.4 us (level)
  no operation moved by 1% of the time
where the time goes in v10:
time: 24.4 us; the launch traced here: 24.3 us
  blocking collectives  17.7 us (73%)
  Pallas kernels  4.17 us (17%)
  waiting for transfers between devices  1.72 us (7%)
  starting transfers between devices  0.52 us (2%)
    all_to_all x1, blocking collectives, per_device(): lax.all_to_all(corr, ('win', 'rcv'), split_axis=0, concat_axis=0, tiled=T...  17.7 us
    pallas_call x1, Pallas kernels, correlate(): pl.pallas_call(functools.partial(correlate_kernel, peers=peers, chunk=chu...  2.57 us
    ppermute x1, waiting for transfers between devices, per_device(): lax.ppermute(spectra, 'rcv', [(i, (i + step) % peers) for i in range(peer...  1.72 us
    pallas_call x1, Pallas kernels, stack_blocks(): pl.pallas_call(stack_kernel, out_shape=jax.ShapeDtypeStruct((pairs, block...  1.57 us
    ppermute x1, starting transfers between devices, per_device(): lax.ppermute(spectra, 'rcv', [(i, (i + step) % peers) for i in range(peer...  0.52 us
  transfers between devices with their start and end apart: 1, of which 1 were waited for; matrix products, arithmetic and copies ran while one was open for 0% of the time, Pallas kernels for 0%

profile of v10, /device:TPU:0, one launch (start us, length us, event | category | flops | bytes accessed | tf_op | source)
XLA Modules:
  0.0 24.3 jit_solution(8615689811483079390)
XLA Ops:
  0.0 0.0 copy-start
  0.0 0.0 copy-start.1
  0.0 0.0 copy-start.2
  0.0 0.5 %collective-permute-start = (bf16[2,2,16,4096]{3,2,1,0:T(8,128)(2,1)}, bf16[2,2,16,4096]{3,2,1,0:T(8,128)(2,1)S(1)}, u32[]{:S(2)}, u32[]{:S(2)}) collective-permute-start(bf16[2,2,16,4096]{3,2,1,0:T(8,128)(2,1)} %refs_3_.1), channel_id=1, source_target_pairs={{0,1},{1,0},{2,3},{3,2},{4,5},{5,4},{6,7},{7,6},{8,9},{9,8},{10,11... | collective-permute-start | bytes 1572872 | tf_op jit(solution)/shard_map/ppermute | solution.py:214
  0.6 1.7 %collective-permute-done.refs_4_ = bf16[2,2,16,4096]{3,2,1,0:T(8,128)(2,1)S(1)} collective-permute-done((bf16[2,2,16,4096]{3,2,1,0:T(8,128)(2,1)}, bf16[2,2,16,4096]{3,2,1,0:T(8,128)(2,1)S(1)}, u32[]{:S(2)}, u32[]{:S(2)}) %collective-permute-start) | collective-permute-done | bytes 524320 | tf_op jit(solution)/shard_map/ppermute | solution.py:214
  2.3 0.0 copy-done
  2.3 0.1 copy-done.1
  2.4 0.0 copy-done.2
  2.4 2.6 %correlate.1 = bf16[16,2,32,128]{3,2,1,0:T(8,128)(2,1)S(1)} custom-call(s32[8]{0:T(128)S(1)} %copy-done.2, bf16[2,272,4096]{2,1,0:T(8,128)(2,1)S(1)} %copy-done, bf16[256,256]{1,0:T(8,128)(2,1)S(1)} %make_flip.1.refs_2_, bf16[2,2,16,4096]{3,2,1,0:T(8,128)(2,1)S(1)} %copy-done.1, bf16[2,2,16,4096]{3,2,1,0:T(8,128)(2,1)S(1)} %collective-permute-done.refs_4_), custom_call_target="tpu_custom_call" | custom-call | tf_op jit(solution)/shard_map/correlate/pallas_call | solution.py:139
  5.0 17.7 %all_to_all.5.x_ref = bf16[32,32,128]{2,1,0:T(8,128)(2,1)S(1)} all-to-all(bf16[32,32,128]{2,1,0:T(8,128)(2,1)S(1)} %bitcast.4), channel_id=1, replica_groups=mesh['win'=16,'rcv'=2] {'win','rcv'}, dimensions={0} | all-to-all | bytes 524288 | tf_op jit(solution)/shard_map/all_to_all | solution.py:217
  22.7 1.6 %bisquare_stack.1 = f32[128,32]{1,0:T(8,128)} custom-call(bf16[32,32,128]{2,1,0:T(8,128)(2,1)S(1)} %all_to_all.5.x_ref), custom_call_target="tpu_custom_call" | custom-call | tf_op jit(solution)/shard_map/bisquare_stack/pallas_call | solution.py:191
  (1 shorter events, 0.0 us)
Async XLA Ops:
  0.0 2.3 %copy-start = (bf16[2,272,4096]{2,1,0:T(8,128)(2,1)S(1)}, bf16[2,272,4096]{2,1,0:T(8,128)(2,1)}, u32[]{:S(2)}) copy-start(bf16[2,272,4096]{2,1,0:T(8,128)(2,1)} %constant.2.clone.refs_1_) | copy-start | bytes 13369348
  0.0 2.4 %copy-start.1 = (bf16[2,2,16,4096]{3,2,1,0:T(8,128)(2,1)S(1)}, bf16[2,2,16,4096]{3,2,1,0:T(8,128)(2,1)}, u32[]{:S(2)}) copy-start(bf16[2,2,16,4096]{3,2,1,0:T(8,128)(2,1)} %refs_3_.1) | copy-start | bytes 1572868
  0.0 2.4 %copy-start.2 = (s32[8]{0:T(128)S(1)}, s32[8]{0:T(128)}, u32[]{:S(2)}) copy-start(s32[8]{0:T(128)} %refs_0_.1) | copy-start | bytes 100
  0.0 2.3 %collective-permute-start = (bf16[2,2,16,4096]{3,2,1,0:T(8,128)(2,1)}, bf16[2,2,16,4096]{3,2,1,0:T(8,128)(2,1)S(1)}, u32[]{:S(2)}, u32[]{:S(2)}) collective-permute-start(bf16[2,2,16,4096]{3,2,1,0:T(8,128)(2,1)} %refs_3_.1), channel_id=1, source_target_pairs={{0,1},{1,0},{2,3},{3,2},{4,5},{5,4},{6,7},{7,6},{8,9},{9,8},{10,11... | collective-permute-start | bytes 1572872 | tf_op jit(solution)/shard_map/ppermute | solution.py:214

commit v11 on v8

--- a/solution.py
+++ b/solution.py
@@ -71,14 +71,16 @@
         owner = lax.div(channel, chan_count)
         place = lax.rem(me - owner + peers, peers) * chan_count
         rows.append(place + lax.rem(channel, chan_count))
-    def form_cross(bins):
+    def widen(bins):
         for k in range(peers):
             for w in range(windows):
                 for part in range(2):
                     float_ref[w, part, k * chan_count : (k + 1) * chan_count, bins] = block_refs[k][
                         first + w, part, :, bins
                     ].astype(jnp.float32)
-        for t in range(items):
+
+    def form_cross(bins, some):
+        for t in some:
             w = t // source_count
             real_p = float_ref[w, 0, :, bins]
             imag_q = float_ref[w, 1, :, bins]
@@ -92,25 +94,29 @@
                 cross_ref[0, pairs, bins] = real[receivers]
                 cross_ref[1, pairs, bins] = imag[receivers]
 
-    def add_products(bins):
-        for index, sum_ref in ((0, even_ref), (1, odd_ref)):
-            term = lax.dot_general(
-                table_ref[index, :, bins],
-                cross_ref[index, :, bins],
-                (((1,), (1,)), ((), ())),
-                preferred_element_type=jnp.float32,
-            )
-            if bins.start == 0:
-                sum_ref[...] = term
-            else:
-                sum_ref[...] += term
+    def add_product(bins, index, sum_ref):
+        term = lax.dot_general(
+            table_ref[index, :, bins],
+            cross_ref[index, :, bins],
+            (((1,), (1,)), ((), ())),
+            preferred_element_type=jnp.float32,
+        )
+        if bins.start == 0:
+            sum_ref[...] = term
+        else:
+            sum_ref[...] += term
 
     chunks = [slice(start, start + chunk) for start in range(0, bin_count, chunk)]
-    form_cross(chunks[0])
-    for index, bins in enumerate(chunks):
-        if index + 1 < len(chunks):
-            form_cross(chunks[index + 1])
-        add_products(bins)
+    for index in range(len(chunks) + 1):
+        if index < len(chunks):
+            widen(chunks[index])
+            form_cross(chunks[index], range(items // 2))
+        if index > 0:
+            add_product(chunks[index - 1], 0, even_ref)
+        if index < len(chunks):
+            form_cross(chunks[index], range(items // 2, items))
+        if index > 0:
+            add_product(chunks[index - 1], 1, odd_ref)
     lags_ref[half:, :] = even_ref[:half, :] + odd_ref[:half, :]
     back = (even_ref[...] - odd_ref[...]).astype(jnp.bfloat16)
     turned = jnp.dot(flip_ref[...], back[:half], preferred_element_type=jnp.float32)
@@ -133,7 +139,7 @@
     peers = len(blocks)
     items = share(win_count, source_count, peers)
     rows = table.shape[1]
-    chunk = min(512, bin_count)
+    chunk = min(256, bin_count)
     width = items * chan_count
     vmem = pl.BlockSpec(memory_space=pltpu.VMEM)
     return pl.pallas_call(

time: 24.2 us -> 24.1 us (level)
  no operation moved by 1% of the time
where the time goes in v11:
time: 24.1 us; the launch traced here: 23.9 us
  blocking collectives  17.7 us (73%)
  Pallas kernels  3.83 us (16%)
  waiting for transfers between devices  1.72 us (7%)
  starting transfers between devices  0.52 us (2%)
    all_to_all x1, blocking collectives, per_device(): lax.all_to_all(corr, ('win', 'rcv'), split_axis=0, concat_axis=0, tiled=T...  17.7 us
    pallas_call x1, Pallas kernels, correlate(): pl.pallas_call(functools.partial(correlate_kernel, peers=peers, chunk=chu...  2.23 us
    ppermute x1, waiting for transfers between devices, per_device(): lax.ppermute(spectra, 'rcv', [(i, (i + step) % peers) for i in range(peer...  1.72 us
    pallas_call x1, Pallas kernels, stack_blocks(): pl.pallas_call(stack_kernel, out_shape=jax.ShapeDtypeStruct((pairs, block...  1.57 us
    ppermute x1, starting transfers between devices, per_device(): lax.ppermute(spectra, 'rcv', [(i, (i + step) % peers) for i in range(peer...  0.52 us
  transfers between devices with their start and end apart: 1, of which 1 were waited for; matrix products, arithmetic and copies ran while one was open for 0% of the time, Pallas kernels for 0%

profile of v11, /device:TPU:0, one launch (start us, length us, event | category | flops | bytes accessed | tf_op | source)
XLA Modules:
  0.0 23.9 jit_solution(7190483064746163575)
XLA Ops:
  0.0 0.0 copy-start
  0.0 0.0 copy-start.1
  0.0 0.0 copy-start.2
  0.0 0.5 %collective-permute-start = (bf16[2,2,16,4096]{3,2,1,0:T(8,128)(2,1)}, bf16[2,2,16,4096]{3,2,1,0:T(8,128)(2,1)S(1)}, u32[]{:S(2)}, u32[]{:S(2)}) collective-permute-start(bf16[2,2,16,4096]{3,2,1,0:T(8,128)(2,1)} %refs_3_.1), channel_id=1, source_target_pairs={{0,1},{1,0},{2,3},{3,2},{4,5},{5,4},{6,7},{7,6},{8,9},{9,8},{10,11... | collective-permute-start | bytes 1572872 | tf_op jit(solution)/shard_map/ppermute | solution.py:220
  0.6 1.7 %collective-permute-done.refs_4_ = bf16[2,2,16,4096]{3,2,1,0:T(8,128)(2,1)S(1)} collective-permute-done((bf16[2,2,16,4096]{3,2,1,0:T(8,128)(2,1)}, bf16[2,2,16,4096]{3,2,1,0:T(8,128)(2,1)S(1)}, u32[]{:S(2)}, u32[]{:S(2)}) %collective-permute-start) | collective-permute-done | bytes 524320 | tf_op jit(solution)/shard_map/ppermute | solution.py:220
  2.3 0.0 copy-done
  2.3 0.1 copy-done.1
  2.4 0.0 copy-done.2
  2.4 2.2 %correlate.1 = bf16[16,2,32,128]{3,2,1,0:T(8,128)(2,1)S(1)} custom-call(s32[8]{0:T(128)S(1)} %copy-done.2, bf16[2,272,4096]{2,1,0:T(8,128)(2,1)S(1)} %copy-done, bf16[256,256]{1,0:T(8,128)(2,1)S(1)} %make_flip.1.refs_2_, bf16[2,2,16,4096]{3,2,1,0:T(8,128)(2,1)S(1)} %copy-done.1, bf16[2,2,16,4096]{3,2,1,0:T(8,128)(2,1)S(1)} %collective-permute-done.refs_4_), custom_call_target="tpu_custom_call" | custom-call | tf_op jit(solution)/shard_map/correlate/pallas_call | solution.py:145
  4.6 17.7 %all_to_all.5.x_ref = bf16[32,32,128]{2,1,0:T(8,128)(2,1)S(1)} all-to-all(bf16[32,32,128]{2,1,0:T(8,128)(2,1)S(1)} %bitcast.4), channel_id=1, replica_groups=mesh['win'=16,'rcv'=2] {'win','rcv'}, dimensions={0} | all-to-all | bytes 524288 | tf_op jit(solution)/shard_map/all_to_all | solution.py:223
  22.3 1.6 %bisquare_stack.1 = f32[128,32]{1,0:T(8,128)} custom-call(bf16[32,32,128]{2,1,0:T(8,128)(2,1)S(1)} %all_to_all.5.x_ref), custom_call_target="tpu_custom_call" | custom-call | tf_op jit(solution)/shard_map/bisquare_stack/pallas_call | solution.py:197
  (1 shorter events, 0.0 us)
Async XLA Ops:
  0.0 2.3 %copy-start = (bf16[2,272,4096]{2,1,0:T(8,128)(2,1)S(1)}, bf16[2,272,4096]{2,1,0:T(8,128)(2,1)}, u32[]{:S(2)}) copy-start(bf16[2,272,4096]{2,1,0:T(8,128)(2,1)} %constant.2.clone.refs_1_) | copy-start | bytes 13369348
  0.0 2.4 %copy-start.1 = (bf16[2,2,16,4096]{3,2,1,0:T(8,128)(2,1)S(1)}, bf16[2,2,16,4096]{3,2,1,0:T(8,128)(2,1)}, u32[]{:S(2)}) copy-start(bf16[2,2,16,4096]{3,2,1,0:T(8,128)(2,1)} %refs_3_.1) | copy-start | bytes 1572868
  0.0 2.4 %copy-start.2 = (s32[8]{0:T(128)S(1)}, s32[8]{0:T(128)}, u32[]{:S(2)}) copy-start(s32[8]{0:T(128)} %refs_0_.1) | copy-start | bytes 100
  0.0 2.3 %collective-permute-start = (bf16[2,2,16,4096]{3,2,1,0:T(8,128)(2,1)}, bf16[2,2,16,4096]{3,2,1,0:T(8,128)(2,1)S(1)}, u32[]{:S(2)}, u32[]{:S(2)}) collective-permute-start(bf16[2,2,16,4096]{3,2,1,0:T(8,128)(2,1)} %refs_3_.1), channel_id=1, source_target_pairs={{0,1},{1,0},{2,3},{3,2},{4,5},{5,4},{6,7},{7,6},{8,9},{9,8},{10,11... | collective-permute-start | bytes 1572872 | tf_op jit(solution)/shard_map/ppermute | solution.py:220

commit v12 on v11

--- a/solution.py
+++ b/solution.py
@@ -29,23 +29,6 @@
     return jnp.asarray(table.astype(jnp.bfloat16))
 
 
-def flip_kernel(out_ref):
-    lag = lax.broadcasted_iota(jnp.int32, out_ref.shape, 0)
-    shift = lax.broadcasted_iota(jnp.int32, out_ref.shape, 1)
-    out_ref[...] = (lag + shift == out_ref.shape[0]).astype(jnp.float32).astype(jnp.bfloat16)
-
-
-def make_flip(half, meanwhile):
-    return pl.pallas_call(
-        flip_kernel,
-        out_shape=jax.ShapeDtypeStruct((half, half), jnp.bfloat16),
-        out_specs=pl.BlockSpec(memory_space=pltpu.VMEM),
-        compiler_params=pltpu.CompilerParams(vmem_limit_bytes=VMEM_LIMIT),
-        cost_estimate=pl.CostEstimate(flops=meanwhile, bytes_accessed=0, transcendentals=0),
-        name="make_flip",
-    )()
-
-
 def share(win_count, source_count, peers):
     items = win_count * source_count // peers
     assert items * peers == win_count * source_count
@@ -53,30 +36,27 @@
     return items
 
 
-def correlate_kernel(*refs, peers, chunk):
-    channel_ref, table_ref, flip_ref = refs[:3]
-    block_refs = refs[3 : 3 + peers]
-    out_ref, lags_ref, even_ref, odd_ref, cross_ref, float_ref = refs[3 + peers :]
-    win_count, _, chan_count, bin_count = block_refs[0].shape
+def correlate_kernel(
+    channel_ref, table_ref, block_ref, out_ref, lags_ref, even_ref, odd_ref, cross_ref, float_ref, *, chunk, items
+):
+    peers, held, _, chan_count, bin_count = block_ref.shape
     source_count = channel_ref.shape[0]
-    items = share(win_count, source_count, peers)
     windows = float_ref.shape[0]
     parts, _, block, width = out_ref.shape
-    half = flip_ref.shape[0]
-    me = lax.axis_index("rcv")
-    first = lax.div(me * items, source_count)
-    rows = []
-    for t in range(items):
-        channel = channel_ref[lax.rem(me * items + t, source_count)]
-        owner = lax.div(channel, chan_count)
-        place = lax.rem(me - owner + peers, peers) * chan_count
-        rows.append(place + lax.rem(channel, chan_count))
+    half = lags_ref.shape[0] // 2
+    if held == windows and items % source_count == 0:
+        first, rows = 0, [channel_ref[t % source_count] for t in range(items)]
+    else:
+        start = lax.axis_index("rcv") * items
+        first = lax.div(start, source_count)
+        rows = [channel_ref[lax.rem(start + t, source_count)] for t in range(items)]
+
     def widen(bins):
         for k in range(peers):
             for w in range(windows):
                 for part in range(2):
-                    float_ref[w, part, k * chan_count : (k + 1) * chan_count, bins] = block_refs[k][
-                        first + w, part, :, bins
+                    float_ref[w, part, k * chan_count : (k + 1) * chan_count, bins] = block_ref[
+                        k, first + w, part, :, bins
                     ].astype(jnp.float32)
 
     def form_cross(bins, some):
@@ -119,33 +99,33 @@
             add_product(chunks[index - 1], 1, odd_ref)
     lags_ref[half:, :] = even_ref[:half, :] + odd_ref[:half, :]
     back = (even_ref[...] - odd_ref[...]).astype(jnp.bfloat16)
-    turned = jnp.dot(flip_ref[...], back[:half], preferred_element_type=jnp.float32)
+    lag = lax.broadcasted_iota(jnp.int32, (half, half), 0)
+    column = lax.broadcasted_iota(jnp.int32, (half, half), 1)
+    flip = (lag + column == half).astype(jnp.float32).astype(jnp.bfloat16)
+    turned = jnp.dot(flip, back[:half], preferred_element_type=jnp.float32)
     lags_ref[:half, :] = jnp.where(
         lax.broadcasted_iota(jnp.int32, turned.shape, 0) == 0,
         back[half : half + 16].astype(jnp.float32)[:1],
         turned,
     )
     for k in range(peers):
-        owner = lax.rem(me - k + peers, peers)
         for part in range(parts):
-            out_ref[part, owner] = lags_ref[
+            out_ref[part, k] = lags_ref[
                 part * block : (part + 1) * block, k * width : (k + 1) * width
             ].astype(jnp.bfloat16)
 
 
-def correlate(source_channel, table, flip, blocks, parts):
-    win_count, _, chan_count, bin_count = blocks[0].shape
+def correlate(source_channel, table, blocks, parts, items):
+    peers, _, _, chan_count, bin_count = blocks.shape
     source_count = source_channel.shape[0]
-    peers = len(blocks)
-    items = share(win_count, source_count, peers)
     rows = table.shape[1]
     chunk = min(256, bin_count)
     width = items * chan_count
     vmem = pl.BlockSpec(memory_space=pltpu.VMEM)
     return pl.pallas_call(
-        functools.partial(correlate_kernel, peers=peers, chunk=chunk),
+        functools.partial(correlate_kernel, chunk=chunk, items=items),
         out_shape=jax.ShapeDtypeStruct((parts, peers, L // parts, width), jnp.bfloat16),
-        in_specs=[pl.BlockSpec(memory_space=pltpu.SMEM), vmem, vmem] + [vmem] * peers,
+        in_specs=[pl.BlockSpec(memory_space=pltpu.SMEM), vmem, vmem],
         out_specs=vmem,
         scratch_shapes=[
             pltpu.VMEM((L, peers * width), jnp.float32),
@@ -156,7 +136,7 @@
         ],
         compiler_params=pltpu.CompilerParams(vmem_limit_bytes=VMEM_LIMIT),
         name="correlate",
-    )(source_channel, table, flip, *blocks)
+    )(source_channel, table, blocks)
 
 
 def stack_kernel(x_ref, out_ref, y_ref):
@@ -214,11 +194,12 @@
     block = L // parts
     items = share(win_count, source_count, peers)
     table = make_tables(bin_count, L, L // 2 + 16)
-    flip = make_flip(L // 2, 2000 * table.size)
-    blocks = [spectra]
-    for step in range(1, peers):
-        blocks.append(lax.ppermute(spectra, "rcv", [(i, (i + step) % peers) for i in range(peers)]))
-    corr = correlate(source_channel, table, flip, blocks, parts)
+    if win_count % peers == 0:
+        blocks = lax.all_to_all(spectra, "rcv", split_axis=0, concat_axis=0, tiled=True)
+        blocks = blocks.reshape(peers, win_count // peers, 2, chan_count, bin_count)
+    else:
+        blocks = lax.all_gather(spectra, "rcv")
+    corr = correlate(source_channel, table, blocks, parts, items)
     corr = corr.reshape(parts * peers, block, items * chan_count)
     moved = lax.all_to_all(corr, ("win", "rcv"), split_axis=0, concat_axis=0, tiled=True)
     if items != source_count:

time: 24.1 us -> 29.8 us (1.24)
  blocking collectives: 17.7 us -> 22.9 us
  local copies, waits for them, and re-layouts: 0.11 us -> 2.92 us
  waiting for transfers between devices: 1.72 us -> 0 us
  starting transfers between devices: 0.52 us -> 0 us
    all_to_all x0 -> x1, blocking collectives: none -> 5.21 us  [per_device(): lax.all_to_all(spectra, 'rcv', split_axis=0, concat_axis=0, tiled=True)]
    unnamed x6 -> x4, local copies, waits for them, and re-layouts: 0.11 us -> 2.92 us
    ppermute x1 -> x0, waiting for transfers between devices: 1.72 us -> none  [per_device(): lax.ppermute(spectra, 'rcv', [(i, (i + step) % peers) for i in range(peer...]
    ppermute x1 -> x0, starting transfers between devices: 0.52 us -> none  [per_device(): lax.ppermute(spectra, 'rcv', [(i, (i + step) % peers) for i in range(peer...]
    pallas_call x2 -> x1, Pallas kernels: 2.26 us -> 2.16 us  [correlate(): pl.pallas_call(functools.partial(correlate_kernel, chunk=chunk, items=ite...]
  transfers between devices with their start and end apart: 1 -> 0, of which waited for: 1 -> 0; matrix products, arithmetic and copies ran while one was open for 0% -> 0% of each run, Pallas kernels for 0% -> 0%
where the time goes in v12:
time: 29.8 us; the launch traced here: 29.6 us
  blocking collectives  22.9 us (77%)
  Pallas kernels  3.73 us (13%)
  local copies, waits for them, and re-layouts  2.92 us (10%)
    all_to_all x1, blocking collectives, per_device(): lax.all_to_all(corr, ('win', 'rcv'), split_axis=0, concat_axis=0, tiled=T...  17.7 us
    all_to_all x1, blocking collectives, per_device(): lax.all_to_all(spectra, 'rcv', split_axis=0, concat_axis=0, tiled=True)  5.21 us
    unnamed x4, local copies, waits for them, and re-layouts  2.92 us
    pallas_call x1, Pallas kernels, correlate(): pl.pallas_call(functools.partial(correlate_kernel, chunk=chunk, items=ite...  2.16 us
    pallas_call x1, Pallas kernels, stack_blocks(): pl.pallas_call(stack_kernel, out_shape=jax.ShapeDtypeStruct((pairs, block...  1.57 us

profile of v12, /device:TPU:0, one launch (start us, length us, event | category | flops | bytes accessed | tf_op | source)
XLA Modules:
  0.0 29.6 jit_solution(11681900933155579437)
XLA Ops:
  0.0 5.2 %all_to_all.10 = bf16[2,2,16,4096]{3,2,1,0:T(8,128)(2,1)S(1)} all-to-all(bf16[2,2,16,4096]{3,2,1,0:T(8,128)(2,1)} %param.3), channel_id=1, replica_groups=mesh['win'=16,'rcv'=2] {'rcv'}, dimensions={0} | all-to-all | bytes 1048576 | tf_op jit(solution)/shard_map/all_to_all | solution.py:198
  5.2 0.0 copy-start
  5.2 2.3 %copy-done = bf16[2,272,4096]{2,1,0:T(8,128)(2,1)S(1)} copy-done((bf16[2,272,4096]{2,1,0:T(8,128)(2,1)S(1)}, bf16[2,272,4096]{2,1,0:T(8,128)(2,1)}, u32[]{:S(2)}) %copy-start) | copy-done | bytes 4456472
  7.5 0.0 copy-start.1
  7.5 0.7 %copy-done.1 = s32[8]{0:T(128)S(1)} copy-done((s32[8]{0:T(128)S(1)}, s32[8]{0:T(128)}, u32[]{:S(2)}) %copy-start.1) | copy-done | bytes 56
  8.1 2.2 %correlate.1 = bf16[16,2,32,128]{3,2,1,0:T(8,128)(2,1)S(1)} custom-call(s32[8]{0:T(128)S(1)} %copy-done.1, bf16[2,272,4096]{2,1,0:T(8,128)(2,1)S(1)} %copy-done, bf16[2,1,2,16,4096]{4,3,2,1,0:T(8,128)(2,1)S(1)} %bitcast.5), custom_call_target="tpu_custom_call" | custom-call | tf_op jit(solution)/shard_map/correlate/pallas_call | solution.py:125
  10.3 17.7 %all_to_all.11.x_ref = bf16[32,32,128]{2,1,0:T(8,128)(2,1)S(1)} all-to-all(bf16[32,32,128]{2,1,0:T(8,128)(2,1)S(1)} %bitcast.6), channel_id=1, replica_groups=mesh['win'=16,'rcv'=2] {'win','rcv'}, dimensions={0} | all-to-all | bytes 524288 | tf_op jit(solution)/shard_map/all_to_all | solution.py:204
  28.0 1.6 %bisquare_stack.1 = f32[128,32]{1,0:T(8,128)} custom-call(bf16[32,32,128]{2,1,0:T(8,128)(2,1)S(1)} %all_to_all.11.x_ref), custom_call_target="tpu_custom_call" | custom-call | tf_op jit(solution)/shard_map/bisquare_stack/pallas_call | solution.py:177
Async XLA Ops:
  5.2 2.3 %copy-start = (bf16[2,272,4096]{2,1,0:T(8,128)(2,1)S(1)}, bf16[2,272,4096]{2,1,0:T(8,128)(2,1)}, u32[]{:S(2)}) copy-start(bf16[2,272,4096]{2,1,0:T(8,128)(2,1)} %constant.2.clone.table_ref) | copy-start | bytes 13369348
  7.5 0.7 %copy-start.1 = (s32[8]{0:T(128)S(1)}, s32[8]{0:T(128)}, u32[]{:S(2)}) copy-start(s32[8]{0:T(128)} %channel_ref.1) | copy-start | bytes 100

commit v13 on v11

--- a/solution.py
+++ b/solution.py
@@ -61,7 +61,7 @@
     source_count = channel_ref.shape[0]
     items = share(win_count, source_count, peers)
     windows = float_ref.shape[0]
-    parts, _, block, width = out_ref.shape
+    lines, _, depth, block, width = out_ref.shape
     half = flip_ref.shape[0]
     me = lax.axis_index("rcv")
     first = lax.div(me * items, source_count)
@@ -106,7 +106,8 @@
         else:
             sum_ref[...] += term
 
-    chunks = [slice(start, start + chunk) for start in range(0, bin_count, chunk)]
+    edges = [0] + list(range(chunk // 2, bin_count, chunk)) + [bin_count]
+    chunks = [slice(start, stop) for start, stop in zip(edges[:-1], edges[1:])]
     for index in range(len(chunks) + 1):
         if index < len(chunks):
             widen(chunks[index])
@@ -127,24 +128,24 @@
     )
     for k in range(peers):
         owner = lax.rem(me - k + peers, peers)
-        for part in range(parts):
-            out_ref[part, owner] = lags_ref[
+        for part in range(lines * depth):
+            out_ref[part % lines, owner, part // lines] = lags_ref[
                 part * block : (part + 1) * block, k * width : (k + 1) * width
             ].astype(jnp.bfloat16)
 
 
-def correlate(source_channel, table, flip, blocks, parts):
+def correlate(source_channel, table, flip, blocks, lines, depth):
     win_count, _, chan_count, bin_count = blocks[0].shape
     source_count = source_channel.shape[0]
     peers = len(blocks)
     items = share(win_count, source_count, peers)
     rows = table.shape[1]
-    chunk = min(256, bin_count)
+    chunk = min(512, bin_count)
     width = items * chan_count
     vmem = pl.BlockSpec(memory_space=pltpu.VMEM)
     return pl.pallas_call(
         functools.partial(correlate_kernel, peers=peers, chunk=chunk),
-        out_shape=jax.ShapeDtypeStruct((parts, peers, L // parts, width), jnp.bfloat16),
+        out_shape=jax.ShapeDtypeStruct((lines, peers, depth, L // (lines * depth), width), jnp.bfloat16),
         in_specs=[pl.BlockSpec(memory_space=pltpu.SMEM), vmem, vmem] + [vmem] * peers,
         out_specs=vmem,
         scratch_shapes=[
@@ -218,11 +219,22 @@
     blocks = [spectra]
     for step in range(1, peers):
         blocks.append(lax.ppermute(spectra, "rcv", [(i, (i + step) % peers) for i in range(peers)]))
-    corr = correlate(source_channel, table, flip, blocks, parts)
+    lines = 1
+    while 4 * lines * lines <= parts:
+        lines *= 2
+    depth = parts // lines
+    assert lines * depth == parts
+    corr = correlate(source_channel, table, flip, blocks, lines, depth)
     corr = corr.reshape(parts * peers, block, items * chan_count)
-    moved = lax.all_to_all(corr, ("win", "rcv"), split_axis=0, concat_axis=0, tiled=True)
+    group = [
+        (z * lines + q) * peers + c for q in range(lines) for c in range(peers) for z in range(depth)
+    ]
+    moved = lax.all_to_all(
+        corr, ("win", "rcv"), split_axis=0, concat_axis=0, tiled=True, axis_index_groups=[group]
+    )
     if items != source_count:
-        moved = moved.reshape(parts * peers, block, items, chan_count).transpose(0, 2, 1, 3)
+        moved = moved.reshape(lines, peers, depth, block, items, chan_count)
+        moved = moved.transpose(2, 0, 1, 4, 3, 5)
         moved = moved.reshape(parts * win_count, source_count, block, chan_count).transpose(0, 2, 1, 3)
         moved = moved.reshape(parts * win_count, block, source_count * chan_count)
     return stack_blocks(moved, source_count)

time: 24.1 us -> 23.7 us (0.983)
  blocking collectives: 17.7 us -> 17.3 us
    all_to_all x1, blocking collectives: 17.7 us -> 17.3 us  [per_device(): lax.all_to_all(corr, ('win', 'rcv'), split_axis=0, concat_axis=0, tiled=T...]
where the time goes in v13:
time: 23.7 us; the launch traced here: 23.6 us
  blocking collectives  17.3 us (73%)
  Pallas kernels  3.91 us (16%)
  waiting for transfers between devices  1.72 us (7%)
  starting transfers between devices  0.52 us (2%)
    all_to_all x1, blocking collectives, per_device(): lax.all_to_all(corr, ('win', 'rcv'), split_axis=0, concat_axis=0, tiled=T...  17.3 us
    pallas_call x1, Pallas kernels, correlate(): pl.pallas_call(functools.partial(correlate_kernel, peers=peers, chunk=chu...  2.31 us
    ppermute x1, waiting for transfers between devices, per_device(): lax.ppermute(spectra, 'rcv', [(i, (i + step) % peers) for i in range(peer...  1.72 us
    pallas_call x1, Pallas kernels, stack_blocks(): pl.pallas_call(stack_kernel, out_shape=jax.ShapeDtypeStruct((pairs, block...  1.57 us
    ppermute x1, starting transfers between devices, per_device(): lax.ppermute(spectra, 'rcv', [(i, (i + step) % peers) for i in range(peer...  0.52 us
  transfers between devices with their start and end apart: 1, of which 1 were waited for; matrix products, arithmetic and copies ran while one was open for 0% of the time, Pallas kernels for 0%

profile of v13, /device:TPU:0, one launch (start us, length us, event | category | flops | bytes accessed | tf_op | source)
XLA Modules:
  0.0 23.6 jit_solution(7409258585139474974)
XLA Ops:
  0.0 0.0 copy-start
  0.0 0.0 copy-start.1
  0.0 0.0 copy-start.2
  0.0 0.5 %collective-permute-start = (bf16[2,2,16,4096]{3,2,1,0:T(8,128)(2,1)}, bf16[2,2,16,4096]{3,2,1,0:T(8,128)(2,1)S(1)}, u32[]{:S(2)}, u32[]{:S(2)}) collective-permute-start(bf16[2,2,16,4096]{3,2,1,0:T(8,128)(2,1)} %refs_3_.1), channel_id=1, source_target_pairs={{0,1},{1,0},{2,3},{3,2},{4,5},{5,4},{6,7},{7,6},{8,9},{9,8},{10,11... | collective-permute-start | bytes 1572872 | tf_op jit(solution)/shard_map/ppermute | solution.py:221
  0.6 1.7 %collective-permute-done.refs_4_ = bf16[2,2,16,4096]{3,2,1,0:T(8,128)(2,1)S(1)} collective-permute-done((bf16[2,2,16,4096]{3,2,1,0:T(8,128)(2,1)}, bf16[2,2,16,4096]{3,2,1,0:T(8,128)(2,1)S(1)}, u32[]{:S(2)}, u32[]{:S(2)}) %collective-permute-start) | collective-permute-done | bytes 524320 | tf_op jit(solution)/shard_map/ppermute | solution.py:221
  2.3 0.0 copy-done
  2.3 0.1 copy-done.1
  2.4 0.0 copy-done.2
  2.4 2.3 %correlate.1 = bf16[4,2,4,32,128]{4,3,2,1,0:T(8,128)(2,1)S(1)} custom-call(s32[8]{0:T(128)S(1)} %copy-done.2, bf16[2,272,4096]{2,1,0:T(8,128)(2,1)S(1)} %copy-done, bf16[256,256]{1,0:T(8,128)(2,1)S(1)} %make_flip.1.refs_2_, bf16[2,2,16,4096]{3,2,1,0:T(8,128)(2,1)S(1)} %copy-done.1, bf16[2,2,16,4096]{3,2,1,0:T(8,128)(2,1)S(1)} %collective-permute-done.refs_4_), custom_call_target="tpu_custom_call" | custom-call | tf_op jit(solution)/shard_map/correlate/pallas_call | solution.py:146
  4.7 17.3 %all_to_all.5.x_ref = bf16[32,32,128]{2,1,0:T(8,128)(2,1)S(1)} all-to-all(bf16[32,32,128]{2,1,0:T(8,128)(2,1)S(1)} %bitcast.4), channel_id=1, replica_groups={{0,8,16,24,1,9,17,25,2,10,18,26,3,11,19,27,4,12,20,28,5,13,21,29,6,14,2..., dimensions={0} | all-to-all | bytes 524288 | tf_op jit(solution)/shard_map/all_to_all | solution.py:232
  22.0 1.6 %bisquare_stack.1 = f32[128,32]{1,0:T(8,128)} custom-call(bf16[32,32,128]{2,1,0:T(8,128)(2,1)S(1)} %all_to_all.5.x_ref), custom_call_target="tpu_custom_call" | custom-call | tf_op jit(solution)/shard_map/bisquare_stack/pallas_call | solution.py:198
  (1 shorter events, 0.0 us)
Async XLA Ops:
  0.0 2.3 %copy-start = (bf16[2,272,4096]{2,1,0:T(8,128)(2,1)S(1)}, bf16[2,272,4096]{2,1,0:T(8,128)(2,1)}, u32[]{:S(2)}) copy-start(bf16[2,272,4096]{2,1,0:T(8,128)(2,1)} %constant.2.clone.refs_1_) | copy-start | bytes 13369348
  0.0 2.4 %copy-start.1 = (bf16[2,2,16,4096]{3,2,1,0:T(8,128)(2,1)S(1)}, bf16[2,2,16,4096]{3,2,1,0:T(8,128)(2,1)}, u32[]{:S(2)}) copy-start(bf16[2,2,16,4096]{3,2,1,0:T(8,128)(2,1)} %refs_3_.1) | copy-start | bytes 1572868
  0.0 2.4 %copy-start.2 = (s32[8]{0:T(128)S(1)}, s32[8]{0:T(128)}, u32[]{:S(2)}) copy-start(s32[8]{0:T(128)} %refs_0_.1) | copy-start | bytes 100
  0.0 2.3 %collective-permute-start = (bf16[2,2,16,4096]{3,2,1,0:T(8,128)(2,1)}, bf16[2,2,16,4096]{3,2,1,0:T(8,128)(2,1)S(1)}, u32[]{:S(2)}, u32[]{:S(2)}) collective-permute-start(bf16[2,2,16,4096]{3,2,1,0:T(8,128)(2,1)} %refs_3_.1), channel_id=1, source_target_pairs={{0,1},{1,0},{2,3},{3,2},{4,5},{5,4},{6,7},{7,6},{8,9},{9,8},{10,11... | collective-permute-start | bytes 1572872 | tf_op jit(solution)/shard_map/ppermute | solution.py:221

commit v14 on v13

--- a/solution.py
+++ b/solution.py
@@ -106,8 +106,7 @@
         else:
             sum_ref[...] += term
 
-    edges = [0] + list(range(chunk // 2, bin_count, chunk)) + [bin_count]
-    chunks = [slice(start, stop) for start, stop in zip(edges[:-1], edges[1:])]
+    chunks = [slice(start, start + chunk) for start in range(0, bin_count, chunk)]
     for index in range(len(chunks) + 1):
         if index < len(chunks):
             widen(chunks[index])
@@ -129,7 +128,7 @@
     for k in range(peers):
         owner = lax.rem(me - k + peers, peers)
         for part in range(lines * depth):
-            out_ref[part % lines, owner, part // lines] = lags_ref[
+            out_ref[lines - 1 - part % lines, peers - 1 - owner, depth - 1 - part // lines] = lags_ref[
                 part * block : (part + 1) * block, k * width : (k + 1) * width
             ].astype(jnp.bfloat16)
 
@@ -140,7 +139,7 @@
     peers = len(blocks)
     items = share(win_count, source_count, peers)
     rows = table.shape[1]
-    chunk = min(512, bin_count)
+    chunk = min(256, bin_count)
     width = items * chan_count
     vmem = pl.BlockSpec(memory_space=pltpu.VMEM)
     return pl.pallas_call(
@@ -229,11 +228,12 @@
     group = [
         (z * lines + q) * peers + c for q in range(lines) for c in range(peers) for z in range(depth)
     ]
+    group.reverse()
     moved = lax.all_to_all(
         corr, ("win", "rcv"), split_axis=0, concat_axis=0, tiled=True, axis_index_groups=[group]
     )
     if items != source_count:
-        moved = moved.reshape(lines, peers, depth, block, items, chan_count)
+        moved = moved[::-1].reshape(lines, peers, depth, block, items, chan_count)
         moved = moved.transpose(2, 0, 1, 4, 3, 5)
         moved = moved.reshape(parts * win_count, source_count, block, chan_count).transpose(0, 2, 1, 3)
         moved = moved.reshape(parts * win_count, block, source_count * chan_count)

time: 23.7 us -> 24.6 us (1.038)
  blocking collectives: 17.3 us -> 18.2 us
    all_to_all x1, blocking collectives: 17.3 us -> 18.2 us  [per_device(): lax.all_to_all(corr, ('win', 'rcv'), split_axis=0, concat_axis=0, tiled=T...]
where the time goes in v14:
time: 24.6 us; the launch traced here: 24.4 us
  blocking collectives  18.2 us (74%)
  Pallas kernels  3.81 us (15%)
  waiting for transfers between devices  1.72 us (7%)
  starting transfers between devices  0.52 us (2%)
    all_to_all x1, blocking collectives, per_device(): lax.all_to_all(corr, ('win', 'rcv'), split_axis=0, concat_axis=0, tiled=T...  18.2 us
    pallas_call x1, Pallas kernels, correlate(): pl.pallas_call(functools.partial(correlate_kernel, peers=peers, chunk=chu...  2.21 us
    ppermute x1, waiting for transfers between devices, per_device(): lax.ppermute(spectra, 'rcv', [(i, (i + step) % peers) for i in range(peer...  1.72 us
    pallas_call x1, Pallas kernels, stack_blocks(): pl.pallas_call(stack_kernel, out_shape=jax.ShapeDtypeStruct((pairs, block...  1.57 us
    ppermute x1, starting transfers between devices, per_device(): lax.ppermute(spectra, 'rcv', [(i, (i + step) % peers) for i in range(peer...  0.52 us
  transfers between devices with their start and end apart: 1, of which 1 were waited for; matrix products, arithmetic and copies ran while one was open for 0% of the time, Pallas kernels for 0%

profile of v14, /device:TPU:0, one launch (start us, length us, event | category | flops | bytes accessed | tf_op | source)
XLA Modules:
  0.0 24.4 jit_solution(12986118540139458947)
XLA Ops:
  0.0 0.0 copy-start
  0.0 0.0 copy-start.1
  0.0 0.0 copy-start.2
  0.0 0.5 %collective-permute-start = (bf16[2,2,16,4096]{3,2,1,0:T(8,128)(2,1)}, bf16[2,2,16,4096]{3,2,1,0:T(8,128)(2,1)S(1)}, u32[]{:S(2)}, u32[]{:S(2)}) collective-permute-start(bf16[2,2,16,4096]{3,2,1,0:T(8,128)(2,1)} %refs_3_.1), channel_id=1, source_target_pairs={{0,1},{1,0},{2,3},{3,2},{4,5},{5,4},{6,7},{7,6},{8,9},{9,8},{10,11... | collective-permute-start | bytes 1572872 | tf_op jit(solution)/shard_map/ppermute | solution.py:220
  0.6 1.7 %collective-permute-done.refs_4_ = bf16[2,2,16,4096]{3,2,1,0:T(8,128)(2,1)S(1)} collective-permute-done((bf16[2,2,16,4096]{3,2,1,0:T(8,128)(2,1)}, bf16[2,2,16,4096]{3,2,1,0:T(8,128)(2,1)S(1)}, u32[]{:S(2)}, u32[]{:S(2)}) %collective-permute-start) | collective-permute-done | bytes 524320 | tf_op jit(solution)/shard_map/ppermute | solution.py:220
  2.3 0.0 copy-done
  2.3 0.1 copy-done.1
  2.4 0.0 copy-done.2
  2.4 2.2 %correlate.1 = bf16[4,2,4,32,128]{4,3,2,1,0:T(8,128)(2,1)S(1)} custom-call(s32[8]{0:T(128)S(1)} %copy-done.2, bf16[2,272,4096]{2,1,0:T(8,128)(2,1)S(1)} %copy-done, bf16[256,256]{1,0:T(8,128)(2,1)S(1)} %make_flip.1.refs_2_, bf16[2,2,16,4096]{3,2,1,0:T(8,128)(2,1)S(1)} %copy-done.1, bf16[2,2,16,4096]{3,2,1,0:T(8,128)(2,1)S(1)} %collective-permute-done.refs_4_), custom_call_target="tpu_custom_call" | custom-call | tf_op jit(solution)/shard_map/correlate/pallas_call | solution.py:145
  4.6 18.2 %all_to_all.5.x_ref = bf16[32,32,128]{2,1,0:T(8,128)(2,1)S(1)} all-to-all(bf16[32,32,128]{2,1,0:T(8,128)(2,1)S(1)} %bitcast.4), channel_id=1, replica_groups={{31,23,15,7,30,22,14,6,29,21,13,5,28,20,12,4,27,19,11,3,26,18,10,2,25,1..., dimensions={0} | all-to-all | bytes 524288 | tf_op jit(solution)/shard_map/all_to_all | solution.py:232
  22.8 1.6 %bisquare_stack.1 = f32[128,32]{1,0:T(8,128)} custom-call(bf16[32,32,128]{2,1,0:T(8,128)(2,1)S(1)} %all_to_all.5.x_ref), custom_call_target="tpu_custom_call" | custom-call | tf_op jit(solution)/shard_map/bisquare_stack/pallas_call | solution.py:197
  (1 shorter events, 0.0 us)
Async XLA Ops:
  0.0 2.3 %copy-start = (bf16[2,272,4096]{2,1,0:T(8,128)(2,1)S(1)}, bf16[2,272,4096]{2,1,0:T(8,128)(2,1)}, u32[]{:S(2)}) copy-start(bf16[2,272,4096]{2,1,0:T(8,128)(2,1)} %constant.2.clone.refs_1_) | copy-start | bytes 13369348
  0.0 2.4 %copy-start.1 = (bf16[2,2,16,4096]{3,2,1,0:T(8,128)(2,1)S(1)}, bf16[2,2,16,4096]{3,2,1,0:T(8,128)(2,1)}, u32[]{:S(2)}) copy-start(bf16[2,2,16,4096]{3,2,1,0:T(8,128)(2,1)} %refs_3_.1) | copy-start | bytes 1572868
  0.0 2.4 %copy-start.2 = (s32[8]{0:T(128)S(1)}, s32[8]{0:T(128)}, u32[]{:S(2)}) copy-start(s32[8]{0:T(128)} %refs_0_.1) | copy-start | bytes 100
  0.0 2.3 %collective-permute-start = (bf16[2,2,16,4096]{3,2,1,0:T(8,128)(2,1)}, bf16[2,2,16,4096]{3,2,1,0:T(8,128)(2,1)S(1)}, u32[]{:S(2)}, u32[]{:S(2)}) collective-permute-start(bf16[2,2,16,4096]{3,2,1,0:T(8,128)(2,1)} %refs_3_.1), channel_id=1, source_target_pairs={{0,1},{1,0},{2,3},{3,2},{4,5},{5,4},{6,7},{7,6},{8,9},{9,8},{10,11... | collective-permute-start | bytes 1572872 | tf_op jit(solution)/shard_map/ppermute | solution.py:220

commit v15 on v14

--- a/solution.py
+++ b/solution.py
@@ -117,20 +117,29 @@
             form_cross(chunks[index], range(items // 2, items))
         if index > 0:
             add_product(chunks[index - 1], 1, odd_ref)
-    lags_ref[half:, :] = even_ref[:half, :] + odd_ref[:half, :]
+    ahead = (even_ref[:half, :] + odd_ref[:half, :]).astype(jnp.bfloat16)
     back = (even_ref[...] - odd_ref[...]).astype(jnp.bfloat16)
     turned = jnp.dot(flip_ref[...], back[:half], preferred_element_type=jnp.float32)
-    lags_ref[:half, :] = jnp.where(
+    behind = jnp.where(
         lax.broadcasted_iota(jnp.int32, turned.shape, 0) == 0,
         back[half : half + 16].astype(jnp.float32)[:1],
         turned,
-    )
+    ).astype(jnp.bfloat16)
+    if block % 16 != 0:
+        lags_ref[half:, :] = ahead.astype(jnp.float32)
+        lags_ref[:half, :] = behind.astype(jnp.float32)
     for k in range(peers):
         owner = lax.rem(me - k + peers, peers)
+        columns = slice(k * width, (k + 1) * width)
         for part in range(lines * depth):
-            out_ref[lines - 1 - part % lines, peers - 1 - owner, depth - 1 - part // lines] = lags_ref[
-                part * block : (part + 1) * block, k * width : (k + 1) * width
-            ].astype(jnp.bfloat16)
+            start = part * block
+            if block % 16 != 0:
+                piece = lags_ref[start : start + block, columns].astype(jnp.bfloat16)
+            elif start < half:
+                piece = behind[start : start + block, columns]
+            else:
+                piece = ahead[start - half : start - half + block, columns]
+            out_ref[part % lines, owner, part // lines] = piece
 
 
 def correlate(source_channel, table, flip, blocks, lines, depth):
@@ -163,26 +172,37 @@
     count, block, pairs = x_ref.shape
     for n in range(count):
         y_ref[n] = x_ref[n].astype(jnp.float32)
-    mean = tree_sum([y_ref[n] for n in range(count)]) * (1.0 / count)
-    squares = []
-    for n in range(count):
-        sample = y_ref[n] - mean
-        y_ref[n] = sample
-        squares.append(sample * sample)
-    variance = tree_sum(squares) * (1.0 / count)
-    center = jnp.zeros_like(mean)
+    step = max(8, block // 2)
+    halves = [slice(start, start + step) for start in range(0, block, step)]
+    means, variances, centers = [], [], []
+    for lags in halves:
+        mean = tree_sum([y_ref[n, lags, :] for n in range(count)]) * (1.0 / count)
+        squares = []
+        for n in range(count):
+            sample = y_ref[n, lags, :] - mean
+            y_ref[n, lags, :] = sample
+            squares.append(sample * sample)
+        means.append(mean)
+        variances.append(tree_sum(squares) * (1.0 / count))
+        centers.append(None)
     for iteration in range(ITERS):
-        limit = TUKEY * TUKEY * (variance + center * center + EPSILON)
-        weights, products = [], []
-        for n in range(count):
-            sample = y_ref[n]
-            deviation = sample - center
-            kept = jnp.maximum(limit - deviation * deviation, 0.0)
-            weight = kept * kept
-            weights.append(weight)
-            products.append(weight * sample)
-        center = tree_sum(products) / tree_sum(weights)
-    out_ref[...] = (center + mean).T
+        for index, lags in enumerate(halves):
+            center = centers[index]
+            limit = variances[index] + EPSILON
+            if iteration > 0:
+                limit = limit + center * center
+            limit = TUKEY * TUKEY * limit
+            weights, products = [], []
+            for n in range(count):
+                sample = y_ref[n, lags, :]
+                deviation = sample if iteration == 0 else sample - center
+                kept = jnp.maximum(limit - deviation * deviation, 0.0)
+                weight = kept * kept
+                weights.append(weight)
+                products.append(weight * sample)
+            centers[index] = tree_sum(products) / tree_sum(weights)
+    results = [center + mean for center, mean in zip(centers, means)]
+    out_ref[...] = jnp.concatenate(results, axis=0).T
 
 
 def tree_sum(terms):
@@ -228,12 +248,11 @@
     group = [
         (z * lines + q) * peers + c for q in range(lines) for c in range(peers) for z in range(depth)
     ]
-    group.reverse()
     moved = lax.all_to_all(
         corr, ("win", "rcv"), split_axis=0, concat_axis=0, tiled=True, axis_index_groups=[group]
     )
     if items != source_count:
-        moved = moved[::-1].reshape(lines, peers, depth, block, items, chan_count)
+        moved = moved.reshape(lines, peers, depth, block, items, chan_count)
         moved = moved.transpose(2, 0, 1, 4, 3, 5)
         moved = moved.reshape(parts * win_count, source_count, block, chan_count).transpose(0, 2, 1, 3)
         moved = moved.reshape(parts * win_count, block, source_count * chan_count)

time: 24.6 us -> 23.7 us (0.963)
  blocking collectives: 18.2 us -> 17.3 us
    all_to_all x1, blocking collectives: 18.2 us -> 17.3 us  [per_device(): lax.all_to_all(corr, ('win', 'rcv'), split_axis=0, concat_axis=0, tiled=T...]
where the time goes in v15:
time: 23.7 us; the launch traced here: 23.5 us
  blocking collectives  17.3 us (73%)
  Pallas kernels  3.86 us (16%)
  waiting for transfers between devices  1.72 us (7%)
  starting transfers between devices  0.52 us (2%)
    all_to_all x1, blocking collectives, per_device(): lax.all_to_all(corr, ('win', 'rcv'), split_axis=0, concat_axis=0, tiled=T...  17.3 us
    pallas_call x1, Pallas kernels, correlate(): pl.pallas_call(functools.partial(correlate_kernel, peers=peers, chunk=chu...  2.21 us
    ppermute x1, waiting for transfers between devices, per_device(): lax.ppermute(spectra, 'rcv', [(i, (i + step) % peers) for i in range(peer...  1.72 us
    pallas_call x1, Pallas kernels, stack_blocks(): pl.pallas_call(stack_kernel, out_shape=jax.ShapeDtypeStruct((pairs, block...  1.62 us
    ppermute x1, starting transfers between devices, per_device(): lax.ppermute(spectra, 'rcv', [(i, (i + step) % peers) for i in range(peer...  0.52 us
  transfers between devices with their start and end apart: 1, of which 1 were waited for; matrix products, arithmetic and copies ran while one was open for 0% of the time, Pallas kernels for 0%

profile of v15, /device:TPU:0, one launch (start us, length us, event | category | flops | bytes accessed | tf_op | source)
XLA Modules:
  0.0 23.5 jit_solution(1988310520568440685)
XLA Ops:
  0.0 0.0 copy-start
  0.0 0.0 copy-start.1
  0.0 0.0 copy-start.2
  0.0 0.5 %collective-permute-start = (bf16[2,2,16,4096]{3,2,1,0:T(8,128)(2,1)}, bf16[2,2,16,4096]{3,2,1,0:T(8,128)(2,1)S(1)}, u32[]{:S(2)}, u32[]{:S(2)}) collective-permute-start(bf16[2,2,16,4096]{3,2,1,0:T(8,128)(2,1)} %refs_3_.1), channel_id=1, source_target_pairs={{0,1},{1,0},{2,3},{3,2},{4,5},{5,4},{6,7},{7,6},{8,9},{9,8},{10,11... | collective-permute-start | bytes 1572872 | tf_op jit(solution)/shard_map/ppermute | solution.py:240
  0.6 1.7 %collective-permute-done.refs_4_ = bf16[2,2,16,4096]{3,2,1,0:T(8,128)(2,1)S(1)} collective-permute-done((bf16[2,2,16,4096]{3,2,1,0:T(8,128)(2,1)}, bf16[2,2,16,4096]{3,2,1,0:T(8,128)(2,1)S(1)}, u32[]{:S(2)}, u32[]{:S(2)}) %collective-permute-start) | collective-permute-done | bytes 524320 | tf_op jit(solution)/shard_map/ppermute | solution.py:240
  2.3 0.0 copy-done
  2.3 0.1 copy-done.1
  2.4 0.0 copy-done.2
  2.4 2.2 %correlate.1 = bf16[4,2,4,32,128]{4,3,2,1,0:T(8,128)(2,1)S(1)} custom-call(s32[8]{0:T(128)S(1)} %copy-done.2, bf16[2,272,4096]{2,1,0:T(8,128)(2,1)S(1)} %copy-done, bf16[256,256]{1,0:T(8,128)(2,1)S(1)} %make_flip.1.refs_2_, bf16[2,2,16,4096]{3,2,1,0:T(8,128)(2,1)S(1)} %copy-done.1, bf16[2,2,16,4096]{3,2,1,0:T(8,128)(2,1)S(1)} %collective-permute-done.refs_4_), custom_call_target="tpu_custom_call" | custom-call | tf_op jit(solution)/shard_map/correlate/pallas_call | solution.py:154
  4.6 17.3 %all_to_all.5.x_ref = bf16[32,32,128]{2,1,0:T(8,128)(2,1)S(1)} all-to-all(bf16[32,32,128]{2,1,0:T(8,128)(2,1)S(1)} %bitcast.4), channel_id=1, replica_groups={{0,8,16,24,1,9,17,25,2,10,18,26,3,11,19,27,4,12,20,28,5,13,21,29,6,14,2..., dimensions={0} | all-to-all | bytes 524288 | tf_op jit(solution)/shard_map/all_to_all | solution.py:251
  21.9 1.6 %bisquare_stack.1 = f32[128,32]{1,0:T(8,128)} custom-call(bf16[32,32,128]{2,1,0:T(8,128)(2,1)S(1)} %all_to_all.5.x_ref), custom_call_target="tpu_custom_call" | custom-call | tf_op jit(solution)/shard_map/bisquare_stack/pallas_call | solution.py:217
  (1 shorter events, 0.0 us)
Async XLA Ops:
  0.0 2.3 %copy-start = (bf16[2,272,4096]{2,1,0:T(8,128)(2,1)S(1)}, bf16[2,272,4096]{2,1,0:T(8,128)(2,1)}, u32[]{:S(2)}) copy-start(bf16[2,272,4096]{2,1,0:T(8,128)(2,1)} %constant.2.clone.refs_1_) | copy-start | bytes 13369348
  0.0 2.4 %copy-start.1 = (bf16[2,2,16,4096]{3,2,1,0:T(8,128)(2,1)S(1)}, bf16[2,2,16,4096]{3,2,1,0:T(8,128)(2,1)}, u32[]{:S(2)}) copy-start(bf16[2,2,16,4096]{3,2,1,0:T(8,128)(2,1)} %refs_3_.1) | copy-start | bytes 1572868
  0.0 2.4 %copy-start.2 = (s32[8]{0:T(128)S(1)}, s32[8]{0:T(128)}, u32[]{:S(2)}) copy-start(s32[8]{0:T(128)} %refs_0_.1) | copy-start | bytes 100
  0.0 2.3 %collective-permute-start = (bf16[2,2,16,4096]{3,2,1,0:T(8,128)(2,1)}, bf16[2,2,16,4096]{3,2,1,0:T(8,128)(2,1)S(1)}, u32[]{:S(2)}, u32[]{:S(2)}) collective-permute-start(bf16[2,2,16,4096]{3,2,1,0:T(8,128)(2,1)} %refs_3_.1), channel_id=1, source_target_pairs={{0,1},{1,0},{2,3},{3,2},{4,5},{5,4},{6,7},{7,6},{8,9},{9,8},{10,11... | collective-permute-start | bytes 1572872 | tf_op jit(solution)/shard_map/ppermute | solution.py:240

commit v16 on v14

--- a/solution.py
+++ b/solution.py
@@ -72,18 +72,19 @@
         place = lax.rem(me - owner + peers, peers) * chan_count
         rows.append(place + lax.rem(channel, chan_count))
     def widen(bins):
-        for k in range(peers):
-            for w in range(windows):
-                for part in range(2):
-                    float_ref[w, part, k * chan_count : (k + 1) * chan_count, bins] = block_refs[k][
-                        first + w, part, :, bins
-                    ].astype(jnp.float32)
-
-    def form_cross(bins, some):
+        sides = []
+        for w in range(windows):
+            for part in range(2):
+                pieces = [block_refs[k][first + w, part, :, bins] for k in range(peers)]
+                side = jnp.concatenate(pieces, axis=0).astype(jnp.float32)
+                float_ref[w, part, :, bins] = side
+                sides.append(side)
+        return sides
+
+    def form_cross(bins, some, sides):
         for t in some:
             w = t // source_count
-            real_p = float_ref[w, 0, :, bins]
-            imag_q = float_ref[w, 1, :, bins]
+            real_p, imag_q = sides[2 * w : 2 * w + 2]
             real_a = float_ref[w, 0, pl.ds(rows[t], 1), bins]
             imag_b = float_ref[w, 1, pl.ds(rows[t], 1), bins]
             real = (real_a * real_p + imag_b * imag_q).astype(jnp.bfloat16)
@@ -109,28 +110,37 @@
     chunks = [slice(start, start + chunk) for start in range(0, bin_count, chunk)]
     for index in range(len(chunks) + 1):
         if index < len(chunks):
-            widen(chunks[index])
-            form_cross(chunks[index], range(items // 2))
+            sides = widen(chunks[index])
+            form_cross(chunks[index], range(items // 2), sides)
         if index > 0:
             add_product(chunks[index - 1], 0, even_ref)
         if index < len(chunks):
-            form_cross(chunks[index], range(items // 2, items))
+            form_cross(chunks[index], range(items // 2, items), sides)
         if index > 0:
             add_product(chunks[index - 1], 1, odd_ref)
-    lags_ref[half:, :] = even_ref[:half, :] + odd_ref[:half, :]
+    ahead = (even_ref[:half, :] + odd_ref[:half, :]).astype(jnp.bfloat16)
     back = (even_ref[...] - odd_ref[...]).astype(jnp.bfloat16)
     turned = jnp.dot(flip_ref[...], back[:half], preferred_element_type=jnp.float32)
-    lags_ref[:half, :] = jnp.where(
+    behind = jnp.where(
         lax.broadcasted_iota(jnp.int32, turned.shape, 0) == 0,
         back[half : half + 16].astype(jnp.float32)[:1],
         turned,
-    )
+    ).astype(jnp.bfloat16)
+    if block % 16 != 0:
+        lags_ref[half:, :] = ahead.astype(jnp.float32)
+        lags_ref[:half, :] = behind.astype(jnp.float32)
     for k in range(peers):
         owner = lax.rem(me - k + peers, peers)
+        columns = slice(k * width, (k + 1) * width)
         for part in range(lines * depth):
-            out_ref[lines - 1 - part % lines, peers - 1 - owner, depth - 1 - part // lines] = lags_ref[
-                part * block : (part + 1) * block, k * width : (k + 1) * width
-            ].astype(jnp.bfloat16)
+            start = part * block
+            if block % 16 != 0:
+                piece = lags_ref[start : start + block, columns].astype(jnp.bfloat16)
+            elif start < half:
+                piece = behind[start : start + block, columns]
+            else:
+                piece = ahead[start - half : start - half + block, columns]
+            out_ref[part % lines, owner, part // lines] = piece
 
 
 def correlate(source_channel, table, flip, blocks, lines, depth):
@@ -170,13 +180,13 @@
         y_ref[n] = sample
         squares.append(sample * sample)
     variance = tree_sum(squares) * (1.0 / count)
-    center = jnp.zeros_like(mean)
     for iteration in range(ITERS):
-        limit = TUKEY * TUKEY * (variance + center * center + EPSILON)
+        shift = center * center if iteration > 0 else 0.0
+        limit = TUKEY * TUKEY * (variance + shift + EPSILON)
         weights, products = [], []
         for n in range(count):
             sample = y_ref[n]
-            deviation = sample - center
+            deviation = sample - center if iteration > 0 else sample
             kept = jnp.maximum(limit - deviation * deviation, 0.0)
             weight = kept * kept
             weights.append(weight)
@@ -228,12 +238,11 @@
     group = [
         (z * lines + q) * peers + c for q in range(lines) for c in range(peers) for z in range(depth)
     ]
-    group.reverse()
     moved = lax.all_to_all(
         corr, ("win", "rcv"), split_axis=0, concat_axis=0, tiled=True, axis_index_groups=[group]
     )
     if items != source_count:
-        moved = moved[::-1].reshape(lines, peers, depth, block, items, chan_count)
+        moved = moved.reshape(lines, peers, depth, block, items, chan_count)
         moved = moved.transpose(2, 0, 1, 4, 3, 5)
         moved = moved.reshape(parts * win_count, source_count, block, chan_count).transpose(0, 2, 1, 3)
         moved = moved.reshape(parts * win_count, block, source_count * chan_count)

time: 24.6 us -> 23.9 us (0.972)
  blocking collectives: 18.2 us -> 17.3 us
  Pallas kernels: 3.81 us -> 4.1 us
    all_to_all x1, blocking collectives: 18.2 us -> 17.3 us  [per_device(): lax.all_to_all(corr, ('win', 'rcv'), split_axis=0, concat_axis=0, tiled=T...]
    pallas_call x1, Pallas kernels: 2.21 us -> 2.5 us  [correlate(): pl.pallas_call(functools.partial(correlate_kernel, peers=peers, chunk=chu...]
where the time goes in v16:
time: 23.9 us; the launch traced here: 23.8 us
  blocking collectives  17.3 us (72%)
  Pallas kernels  4.1 us (17%)
  waiting for transfers between devices  1.72 us (7%)
  starting transfers between devices  0.52 us (2%)
    all_to_all x1, blocking collectives, per_device(): lax.all_to_all(corr, ('win', 'rcv'), split_axis=0, concat_axis=0, tiled=T...  17.3 us
    pallas_call x1, Pallas kernels, correlate(): pl.pallas_call(functools.partial(correlate_kernel, peers=peers, chunk=chu...  2.5 us
    ppermute x1, waiting for transfers between devices, per_device(): lax.ppermute(spectra, 'rcv', [(i, (i + step) % peers) for i in range(peer...  1.72 us
    pallas_call x1, Pallas kernels, stack_blocks(): pl.pallas_call(stack_kernel, out_shape=jax.ShapeDtypeStruct((pairs, block...  1.57 us
    ppermute x1, starting transfers between devices, per_device(): lax.ppermute(spectra, 'rcv', [(i, (i + step) % peers) for i in range(peer...  0.52 us
  transfers between devices with their start and end apart: 1, of which 1 were waited for; matrix products, arithmetic and copies ran while one was open for 0% of the time, Pallas kernels for 0%

profile of v16, /device:TPU:0, one launch (start us, length us, event | category | flops | bytes accessed | tf_op | source)
XLA Modules:
  0.0 23.8 jit_solution(874178517136892475)
XLA Ops:
  0.0 0.0 copy-start
  0.0 0.0 copy-start.1
  0.0 0.0 copy-start.2
  0.0 0.5 %collective-permute-start = (bf16[2,2,16,4096]{3,2,1,0:T(8,128)(2,1)}, bf16[2,2,16,4096]{3,2,1,0:T(8,128)(2,1)S(1)}, u32[]{:S(2)}, u32[]{:S(2)}) collective-permute-start(bf16[2,2,16,4096]{3,2,1,0:T(8,128)(2,1)} %refs_3_.1), channel_id=1, source_target_pairs={{0,1},{1,0},{2,3},{3,2},{4,5},{5,4},{6,7},{7,6},{8,9},{9,8},{10,11... | collective-permute-start | bytes 1572872 | tf_op jit(solution)/shard_map/ppermute | solution.py:230
  0.6 1.7 %collective-permute-done.refs_4_ = bf16[2,2,16,4096]{3,2,1,0:T(8,128)(2,1)S(1)} collective-permute-done((bf16[2,2,16,4096]{3,2,1,0:T(8,128)(2,1)}, bf16[2,2,16,4096]{3,2,1,0:T(8,128)(2,1)S(1)}, u32[]{:S(2)}, u32[]{:S(2)}) %collective-permute-start) | collective-permute-done | bytes 524320 | tf_op jit(solution)/shard_map/ppermute | solution.py:230
  2.3 0.0 copy-done
  2.3 0.1 copy-done.1
  2.4 0.0 copy-done.2
  2.4 2.5 %correlate.1 = bf16[4,2,4,32,128]{4,3,2,1,0:T(8,128)(2,1)S(1)} custom-call(s32[8]{0:T(128)S(1)} %copy-done.2, bf16[2,272,4096]{2,1,0:T(8,128)(2,1)S(1)} %copy-done, bf16[256,256]{1,0:T(8,128)(2,1)S(1)} %make_flip.1.refs_2_, bf16[2,2,16,4096]{3,2,1,0:T(8,128)(2,1)S(1)} %copy-done.1, bf16[2,2,16,4096]{3,2,1,0:T(8,128)(2,1)S(1)} %collective-permute-done.refs_4_), custom_call_target="tpu_custom_call" | custom-call | tf_op jit(solution)/shard_map/correlate/pallas_call | solution.py:155
  4.9 17.3 %all_to_all.5.x_ref = bf16[32,32,128]{2,1,0:T(8,128)(2,1)S(1)} all-to-all(bf16[32,32,128]{2,1,0:T(8,128)(2,1)S(1)} %bitcast.4), channel_id=1, replica_groups={{0,8,16,24,1,9,17,25,2,10,18,26,3,11,19,27,4,12,20,28,5,13,21,29,6,14,2..., dimensions={0} | all-to-all | bytes 524288 | tf_op jit(solution)/shard_map/all_to_all | solution.py:241
  22.2 1.6 %bisquare_stack.1 = f32[128,32]{1,0:T(8,128)} custom-call(bf16[32,32,128]{2,1,0:T(8,128)(2,1)S(1)} %all_to_all.5.x_ref), custom_call_target="tpu_custom_call" | custom-call | tf_op jit(solution)/shard_map/bisquare_stack/pallas_call | solution.py:207
  (1 shorter events, 0.0 us)
Async XLA Ops:
  0.0 2.3 %copy-start = (bf16[2,272,4096]{2,1,0:T(8,128)(2,1)S(1)}, bf16[2,272,4096]{2,1,0:T(8,128)(2,1)}, u32[]{:S(2)}) copy-start(bf16[2,272,4096]{2,1,0:T(8,128)(2,1)} %constant.2.clone.refs_1_) | copy-start | bytes 13369348
  0.0 2.4 %copy-start.1 = (bf16[2,2,16,4096]{3,2,1,0:T(8,128)(2,1)S(1)}, bf16[2,2,16,4096]{3,2,1,0:T(8,128)(2,1)}, u32[]{:S(2)}) copy-start(bf16[2,2,16,4096]{3,2,1,0:T(8,128)(2,1)} %refs_3_.1) | copy-start | bytes 1572868
  0.0 2.4 %copy-start.2 = (s32[8]{0:T(128)S(1)}, s32[8]{0:T(128)}, u32[]{:S(2)}) copy-start(s32[8]{0:T(128)} %refs_0_.1) | copy-start | bytes 100
  0.0 2.3 %collective-permute-start = (bf16[2,2,16,4096]{3,2,1,0:T(8,128)(2,1)}, bf16[2,2,16,4096]{3,2,1,0:T(8,128)(2,1)S(1)}, u32[]{:S(2)}, u32[]{:S(2)}) collective-permute-start(bf16[2,2,16,4096]{3,2,1,0:T(8,128)(2,1)} %refs_3_.1), channel_id=1, source_target_pairs={{0,1},{1,0},{2,3},{3,2},{4,5},{5,4},{6,7},{7,6},{8,9},{9,8},{10,11... | collective-permute-start | bytes 1572872 | tf_op jit(solution)/shard_map/ppermute | solution.py:230

commit v17 on v16

--- a/solution.py
+++ b/solution.py
@@ -72,28 +72,31 @@
         place = lax.rem(me - owner + peers, peers) * chan_count
         rows.append(place + lax.rem(channel, chan_count))
     def widen(bins):
-        sides = []
-        for w in range(windows):
-            for part in range(2):
-                pieces = [block_refs[k][first + w, part, :, bins] for k in range(peers)]
-                side = jnp.concatenate(pieces, axis=0).astype(jnp.float32)
-                float_ref[w, part, :, bins] = side
-                sides.append(side)
-        return sides
-
-    def form_cross(bins, some, sides):
+        for k in range(peers):
+            for w in range(windows):
+                for part in range(2):
+                    float_ref[w, part, k * chan_count : (k + 1) * chan_count, bins] = block_refs[k][
+                        first + w, part, :, bins
+                    ].astype(jnp.float32)
+
+    def form_cross(bins, some):
         for t in some:
             w = t // source_count
-            real_p, imag_q = sides[2 * w : 2 * w + 2]
-            real_a = float_ref[w, 0, pl.ds(rows[t], 1), bins]
-            imag_b = float_ref[w, 1, pl.ds(rows[t], 1), bins]
-            real = (real_a * real_p + imag_b * imag_q).astype(jnp.bfloat16)
-            imag = (imag_b * real_p - real_a * imag_q).astype(jnp.bfloat16)
-            for k in range(peers):
-                receivers = slice(k * chan_count, (k + 1) * chan_count)
-                pairs = slice(k * width + t * chan_count, k * width + (t + 1) * chan_count)
-                cross_ref[0, pairs, bins] = real[receivers]
-                cross_ref[1, pairs, bins] = imag[receivers]
+            real_row = float_ref[w, 0, pl.ds(rows[t], 1), bins]
+            imag_row = float_ref[w, 1, pl.ds(rows[t], 1), bins]
+            for start in range(bins.start, bins.stop, 128):
+                lanes = slice(start, start + 128)
+                real_a = real_row[:, start - bins.start : start - bins.start + 128]
+                imag_b = imag_row[:, start - bins.start : start - bins.start + 128]
+                for k in range(peers):
+                    receivers = slice(k * chan_count, (k + 1) * chan_count)
+                    pairs = slice(k * width + t * chan_count, k * width + (t + 1) * chan_count)
+                    real_p = float_ref[w, 0, receivers, lanes]
+                    imag_q = float_ref[w, 1, receivers, lanes]
+                    real = real_a * real_p + imag_b * imag_q
+                    imag = imag_b * real_p - real_a * imag_q
+                    cross_ref[0, pairs, lanes] = real.astype(jnp.bfloat16)
+                    cross_ref[1, pairs, lanes] = imag.astype(jnp.bfloat16)
 
     def add_product(bins, index, sum_ref):
         term = lax.dot_general(
@@ -110,12 +113,12 @@
     chunks = [slice(start, start + chunk) for start in range(0, bin_count, chunk)]
     for index in range(len(chunks) + 1):
         if index < len(chunks):
-            sides = widen(chunks[index])
-            form_cross(chunks[index], range(items // 2), sides)
+            widen(chunks[index])
+            form_cross(chunks[index], range(items // 2))
         if index > 0:
             add_product(chunks[index - 1], 0, even_ref)
         if index < len(chunks):
-            form_cross(chunks[index], range(items // 2, items), sides)
+            form_cross(chunks[index], range(items // 2, items))
         if index > 0:
             add_product(chunks[index - 1], 1, odd_ref)
     ahead = (even_ref[:half, :] + odd_ref[:half, :]).astype(jnp.bfloat16)

time: 23.9 us -> 24.7 us (1.033)
  Pallas kernels: 4.1 us -> 4.87 us
    pallas_call x1, Pallas kernels: 2.5 us -> 3.27 us  [correlate(): pl.pallas_call(functools.partial(correlate_kernel, peers=peers, chunk=chu...]
where the time goes in v17:
time: 24.7 us; the launch traced here: 24.5 us
  blocking collectives  17.3 us (70%)
  Pallas kernels  4.87 us (20%)
  waiting for transfers between devices  1.72 us (7%)
  starting transfers between devices  0.52 us (2%)
    all_to_all x1, blocking collectives, per_device(): lax.all_to_all(corr, ('win', 'rcv'), split_axis=0, concat_axis=0, tiled=T...  17.3 us
    pallas_call x1, Pallas kernels, correlate(): pl.pallas_call(functools.partial(correlate_kernel, peers=peers, chunk=chu...  3.27 us
    ppermute x1, waiting for transfers between devices, per_device(): lax.ppermute(spectra, 'rcv', [(i, (i + step) % peers) for i in range(peer...  1.72 us
    pallas_call x1, Pallas kernels, stack_blocks(): pl.pallas_call(stack_kernel, out_shape=jax.ShapeDtypeStruct((pairs, block...  1.57 us
    ppermute x1, starting transfers between devices, per_device(): lax.ppermute(spectra, 'rcv', [(i, (i + step) % peers) for i in range(peer...  0.52 us
  transfers between devices with their start and end apart: 1, of which 1 were waited for; matrix products, arithmetic and copies ran while one was open for 0% of the time, Pallas kernels for 0%

profile of v17, /device:TPU:0, one launch (start us, length us, event | category | flops | bytes accessed | tf_op | source)
XLA Modules:
  0.0 24.5 jit_solution(12835395754235040724)
XLA Ops:
  0.0 0.0 copy-start
  0.0 0.0 copy-start.1
  0.0 0.0 copy-start.2
  0.0 0.5 %collective-permute-start = (bf16[2,2,16,4096]{3,2,1,0:T(8,128)(2,1)}, bf16[2,2,16,4096]{3,2,1,0:T(8,128)(2,1)S(1)}, u32[]{:S(2)}, u32[]{:S(2)}) collective-permute-start(bf16[2,2,16,4096]{3,2,1,0:T(8,128)(2,1)} %refs_3_.1), channel_id=1, source_target_pairs={{0,1},{1,0},{2,3},{3,2},{4,5},{5,4},{6,7},{7,6},{8,9},{9,8},{10,11... | collective-permute-start | bytes 1572872 | tf_op jit(solution)/shard_map/ppermute | solution.py:233
  0.6 1.7 %collective-permute-done.refs_4_ = bf16[2,2,16,4096]{3,2,1,0:T(8,128)(2,1)S(1)} collective-permute-done((bf16[2,2,16,4096]{3,2,1,0:T(8,128)(2,1)}, bf16[2,2,16,4096]{3,2,1,0:T(8,128)(2,1)S(1)}, u32[]{:S(2)}, u32[]{:S(2)}) %collective-permute-start) | collective-permute-done | bytes 524320 | tf_op jit(solution)/shard_map/ppermute | solution.py:233
  2.3 0.0 copy-done
  2.3 0.1 copy-done.1
  2.4 0.0 copy-done.2
  2.4 3.3 %correlate.1 = bf16[4,2,4,32,128]{4,3,2,1,0:T(8,128)(2,1)S(1)} custom-call(s32[8]{0:T(128)S(1)} %copy-done.2, bf16[2,272,4096]{2,1,0:T(8,128)(2,1)S(1)} %copy-done, bf16[256,256]{1,0:T(8,128)(2,1)S(1)} %make_flip.1.refs_2_, bf16[2,2,16,4096]{3,2,1,0:T(8,128)(2,1)S(1)} %copy-done.1, bf16[2,2,16,4096]{3,2,1,0:T(8,128)(2,1)S(1)} %collective-permute-done.refs_4_), custom_call_target="tpu_custom_call" | custom-call | tf_op jit(solution)/shard_map/correlate/pallas_call | solution.py:158
  5.7 17.3 %all_to_all.5.x_ref = bf16[32,32,128]{2,1,0:T(8,128)(2,1)S(1)} all-to-all(bf16[32,32,128]{2,1,0:T(8,128)(2,1)S(1)} %bitcast.4), channel_id=1, replica_groups={{0,8,16,24,1,9,17,25,2,10,18,26,3,11,19,27,4,12,20,28,5,13,21,29,6,14,2..., dimensions={0} | all-to-all | bytes 524288 | tf_op jit(solution)/shard_map/all_to_all | solution.py:244
  23.0 1.6 %bisquare_stack.1 = f32[128,32]{1,0:T(8,128)} custom-call(bf16[32,32,128]{2,1,0:T(8,128)(2,1)S(1)} %all_to_all.5.x_ref), custom_call_target="tpu_custom_call" | custom-call | tf_op jit(solution)/shard_map/bisquare_stack/pallas_call | solution.py:210
  (1 shorter events, 0.0 us)
Async XLA Ops:
  0.0 2.3 %copy-start = (bf16[2,272,4096]{2,1,0:T(8,128)(2,1)S(1)}, bf16[2,272,4096]{2,1,0:T(8,128)(2,1)}, u32[]{:S(2)}) copy-start(bf16[2,272,4096]{2,1,0:T(8,128)(2,1)} %constant.2.clone.refs_1_) | copy-start | bytes 13369348
  0.0 2.4 %copy-start.1 = (bf16[2,2,16,4096]{3,2,1,0:T(8,128)(2,1)S(1)}, bf16[2,2,16,4096]{3,2,1,0:T(8,128)(2,1)}, u32[]{:S(2)}) copy-start(bf16[2,2,16,4096]{3,2,1,0:T(8,128)(2,1)} %refs_3_.1) | copy-start | bytes 1572868
  0.0 2.4 %copy-start.2 = (s32[8]{0:T(128)S(1)}, s32[8]{0:T(128)}, u32[]{:S(2)}) copy-start(s32[8]{0:T(128)} %refs_0_.1) | copy-start | bytes 100
  0.0 2.3 %collective-permute-start = (bf16[2,2,16,4096]{3,2,1,0:T(8,128)(2,1)}, bf16[2,2,16,4096]{3,2,1,0:T(8,128)(2,1)S(1)}, u32[]{:S(2)}, u32[]{:S(2)}) collective-permute-start(bf16[2,2,16,4096]{3,2,1,0:T(8,128)(2,1)} %refs_3_.1), channel_id=1, source_target_pairs={{0,1},{1,0},{2,3},{3,2},{4,5},{5,4},{6,7},{7,6},{8,9},{9,8},{10,11... | collective-permute-start | bytes 1572872 | tf_op jit(solution)/shard_map/ppermute | solution.py:233

commit v18 on v16

--- a/solution.py
+++ b/solution.py
@@ -72,19 +72,18 @@
         place = lax.rem(me - owner + peers, peers) * chan_count
         rows.append(place + lax.rem(channel, chan_count))
     def widen(bins):
-        sides = []
-        for w in range(windows):
-            for part in range(2):
-                pieces = [block_refs[k][first + w, part, :, bins] for k in range(peers)]
-                side = jnp.concatenate(pieces, axis=0).astype(jnp.float32)
-                float_ref[w, part, :, bins] = side
-                sides.append(side)
-        return sides
-
-    def form_cross(bins, some, sides):
+        for k in range(peers):
+            for w in range(windows):
+                for part in range(2):
+                    float_ref[w, part, k * chan_count : (k + 1) * chan_count, bins] = block_refs[k][
+                        first + w, part, :, bins
+                    ].astype(jnp.float32)
+
+    def form_cross(bins, some):
         for t in some:
             w = t // source_count
-            real_p, imag_q = sides[2 * w : 2 * w + 2]
+            real_p = float_ref[w, 0, :, bins]
+            imag_q = float_ref[w, 1, :, bins]
             real_a = float_ref[w, 0, pl.ds(rows[t], 1), bins]
             imag_b = float_ref[w, 1, pl.ds(rows[t], 1), bins]
             real = (real_a * real_p + imag_b * imag_q).astype(jnp.bfloat16)
@@ -110,12 +109,12 @@
     chunks = [slice(start, start + chunk) for start in range(0, bin_count, chunk)]
     for index in range(len(chunks) + 1):
         if index < len(chunks):
-            sides = widen(chunks[index])
-            form_cross(chunks[index], range(items // 2), sides)
+            widen(chunks[index])
+            form_cross(chunks[index], range(items // 2))
         if index > 0:
             add_product(chunks[index - 1], 0, even_ref)
         if index < len(chunks):
-            form_cross(chunks[index], range(items // 2, items), sides)
+            form_cross(chunks[index], range(items // 2, items))
         if index > 0:
             add_product(chunks[index - 1], 1, odd_ref)
     ahead = (even_ref[:half, :] + odd_ref[:half, :]).astype(jnp.bfloat16)
@@ -140,7 +139,8 @@
                 piece = behind[start : start + block, columns]
             else:
                 piece = ahead[start - half : start - half + block, columns]
-            out_ref[part % lines, owner, part // lines] = piece
+            z = part // lines
+            out_ref[part % lines, owner, z + lax.rem(owner, 2) * (depth - 1 - 2 * z)] = piece
 
 
 def correlate(source_channel, table, flip, blocks, lines, depth):
@@ -235,14 +235,14 @@
     assert lines * depth == parts
     corr = correlate(source_channel, table, flip, blocks, lines, depth)
     corr = corr.reshape(parts * peers, block, items * chan_count)
-    group = [
-        (z * lines + q) * peers + c for q in range(lines) for c in range(peers) for z in range(depth)
-    ]
+    snake = [range(depth) if c % 2 == 0 else range(depth - 1, -1, -1) for c in range(peers)]
+    group = [(z * lines + q) * peers + c for q in range(lines) for c in range(peers) for z in snake[c]]
     moved = lax.all_to_all(
         corr, ("win", "rcv"), split_axis=0, concat_axis=0, tiled=True, axis_index_groups=[group]
     )
     if items != source_count:
         moved = moved.reshape(lines, peers, depth, block, items, chan_count)
+        moved = jnp.stack([moved[:, c] if c % 2 == 0 else moved[:, c, ::-1] for c in range(peers)], axis=1)
         moved = moved.transpose(2, 0, 1, 4, 3, 5)
         moved = moved.reshape(parts * win_count, source_count, block, chan_count).transpose(0, 2, 1, 3)
         moved = moved.reshape(parts * win_count, block, source_count * chan_count)

time: 23.9 us -> 24 us (level)
  blocking collectives: 17.3 us -> 17.7 us
  Pallas kernels: 4.1 us -> 3.83 us
    all_to_all x1, blocking collectives: 17.3 us -> 17.7 us  [per_device(): lax.all_to_all(corr, ('win', 'rcv'), split_axis=0, concat_axis=0, tiled=T...]
    pallas_call x1, Pallas kernels: 2.5 us -> 2.23 us  [correlate(): pl.pallas_call(functools.partial(correlate_kernel, peers=peers, chunk=chu...]
where the time goes in v18:
time: 24 us; the launch traced here: 23.9 us
  blocking collectives  17.7 us (74%)
  Pallas kernels  3.83 us (16%)
  waiting for transfers between devices  1.72 us (7%)
  starting transfers between devices  0.52 us (2%)
    all_to_all x1, blocking collectives, per_device(): lax.all_to_all(corr, ('win', 'rcv'), split_axis=0, concat_axis=0, tiled=T...  17.7 us
    pallas_call x1, Pallas kernels, correlate(): pl.pallas_call(functools.partial(correlate_kernel, peers=peers, chunk=chu...  2.23 us
    ppermute x1, waiting for transfers between devices, per_device(): lax.ppermute(spectra, 'rcv', [(i, (i + step) % peers) for i in range(peer...  1.72 us
    pallas_call x1, Pallas kernels, stack_blocks(): pl.pallas_call(stack_kernel, out_shape=jax.ShapeDtypeStruct((pairs, block...  1.57 us
    ppermute x1, starting transfers between devices, per_device(): lax.ppermute(spectra, 'rcv', [(i, (i + step) % peers) for i in range(peer...  0.52 us
  transfers between devices with their start and end apart: 1, of which 1 were waited for; matrix products, arithmetic and copies ran while one was open for 0% of the time, Pallas kernels for 0%

profile of v18, /device:TPU:0, one launch (start us, length us, event | category | flops | bytes accessed | tf_op | source)
XLA Modules:
  0.0 23.9 jit_solution(9224673424017134167)
XLA Ops:
  0.0 0.0 copy-start
  0.0 0.0 copy-start.1
  0.0 0.0 copy-start.2
  0.0 0.5 %collective-permute-start = (bf16[2,2,16,4096]{3,2,1,0:T(8,128)(2,1)}, bf16[2,2,16,4096]{3,2,1,0:T(8,128)(2,1)S(1)}, u32[]{:S(2)}, u32[]{:S(2)}) collective-permute-start(bf16[2,2,16,4096]{3,2,1,0:T(8,128)(2,1)} %refs_3_.1), channel_id=1, source_target_pairs={{0,1},{1,0},{2,3},{3,2},{4,5},{5,4},{6,7},{7,6},{8,9},{9,8},{10,11... | collective-permute-start | bytes 1572872 | tf_op jit(solution)/shard_map/ppermute | solution.py:230
  0.6 1.7 %collective-permute-done.refs_4_ = bf16[2,2,16,4096]{3,2,1,0:T(8,128)(2,1)S(1)} collective-permute-done((bf16[2,2,16,4096]{3,2,1,0:T(8,128)(2,1)}, bf16[2,2,16,4096]{3,2,1,0:T(8,128)(2,1)S(1)}, u32[]{:S(2)}, u32[]{:S(2)}) %collective-permute-start) | collective-permute-done | bytes 524320 | tf_op jit(solution)/shard_map/ppermute | solution.py:230
  2.3 0.0 copy-done
  2.3 0.1 copy-done.1
  2.4 0.0 copy-done.2
  2.4 2.2 %correlate.1 = bf16[4,2,4,32,128]{4,3,2,1,0:T(8,128)(2,1)S(1)} custom-call(s32[8]{0:T(128)S(1)} %copy-done.2, bf16[2,272,4096]{2,1,0:T(8,128)(2,1)S(1)} %copy-done, bf16[256,256]{1,0:T(8,128)(2,1)S(1)} %make_flip.1.refs_2_, bf16[2,2,16,4096]{3,2,1,0:T(8,128)(2,1)S(1)} %copy-done.1, bf16[2,2,16,4096]{3,2,1,0:T(8,128)(2,1)S(1)} %collective-permute-done.refs_4_), custom_call_target="tpu_custom_call" | custom-call | tf_op jit(solution)/shard_map/correlate/pallas_call | solution.py:155
  4.6 17.7 %all_to_all.5.x_ref = bf16[32,32,128]{2,1,0:T(8,128)(2,1)S(1)} all-to-all(bf16[32,32,128]{2,1,0:T(8,128)(2,1)S(1)} %bitcast.4), channel_id=1, replica_groups={{0,8,16,24,25,17,9,1,2,10,18,26,27,19,11,3,4,12,20,28,29,21,13,5,6,14,2..., dimensions={0} | all-to-all | bytes 524288 | tf_op jit(solution)/shard_map/all_to_all | solution.py:240
  22.3 1.6 %bisquare_stack.1 = f32[128,32]{1,0:T(8,128)} custom-call(bf16[32,32,128]{2,1,0:T(8,128)(2,1)S(1)} %all_to_all.5.x_ref), custom_call_target="tpu_custom_call" | custom-call | tf_op jit(solution)/shard_map/bisquare_stack/pallas_call | solution.py:207
  (1 shorter events, 0.0 us)
Async XLA Ops:
  0.0 2.3 %copy-start = (bf16[2,272,4096]{2,1,0:T(8,128)(2,1)S(1)}, bf16[2,272,4096]{2,1,0:T(8,128)(2,1)}, u32[]{:S(2)}) copy-start(bf16[2,272,4096]{2,1,0:T(8,128)(2,1)} %constant.2.clone.refs_1_) | copy-start | bytes 13369348
  0.0 2.4 %copy-start.1 = (bf16[2,2,16,4096]{3,2,1,0:T(8,128)(2,1)S(1)}, bf16[2,2,16,4096]{3,2,1,0:T(8,128)(2,1)}, u32[]{:S(2)}) copy-start(bf16[2,2,16,4096]{3,2,1,0:T(8,128)(2,1)} %refs_3_.1) | copy-start | bytes 1572868
  0.0 2.4 %copy-start.2 = (s32[8]{0:T(128)S(1)}, s32[8]{0:T(128)}, u32[]{:S(2)}) copy-start(s32[8]{0:T(128)} %refs_0_.1) | copy-start | bytes 100
  0.0 2.3 %collective-permute-start = (bf16[2,2,16,4096]{3,2,1,0:T(8,128)(2,1)}, bf16[2,2,16,4096]{3,2,1,0:T(8,128)(2,1)S(1)}, u32[]{:S(2)}, u32[]{:S(2)}) collective-permute-start(bf16[2,2,16,4096]{3,2,1,0:T(8,128)(2,1)} %refs_3_.1), channel_id=1, source_target_pairs={{0,1},{1,0},{2,3},{3,2},{4,5},{5,4},{6,7},{7,6},{8,9},{9,8},{10,11... | collective-permute-start | bytes 1572872 | tf_op jit(solution)/shard_map/ppermute | solution.py:230

commit v19 on v18

--- a/solution.py
+++ b/solution.py
@@ -61,7 +61,7 @@
     source_count = channel_ref.shape[0]
     items = share(win_count, source_count, peers)
     windows = float_ref.shape[0]
-    lines, _, depth, block, width = out_ref.shape
+    lines, depth, _, block, width = out_ref.shape
     half = flip_ref.shape[0]
     me = lax.axis_index("rcv")
     first = lax.div(me * items, source_count)
@@ -139,8 +139,7 @@
                 piece = behind[start : start + block, columns]
             else:
                 piece = ahead[start - half : start - half + block, columns]
-            z = part // lines
-            out_ref[part % lines, owner, z + lax.rem(owner, 2) * (depth - 1 - 2 * z)] = piece
+            out_ref[part % lines, part // lines, owner] = piece
 
 
 def correlate(source_channel, table, flip, blocks, lines, depth):
@@ -154,7 +153,7 @@
     vmem = pl.BlockSpec(memory_space=pltpu.VMEM)
     return pl.pallas_call(
         functools.partial(correlate_kernel, peers=peers, chunk=chunk),
-        out_shape=jax.ShapeDtypeStruct((lines, peers, depth, L // (lines * depth), width), jnp.bfloat16),
+        out_shape=jax.ShapeDtypeStruct((lines, depth, peers, L // (lines * depth), width), jnp.bfloat16),
         in_specs=[pl.BlockSpec(memory_space=pltpu.SMEM), vmem, vmem] + [vmem] * peers,
         out_specs=vmem,
         scratch_shapes=[
@@ -235,15 +234,15 @@
     assert lines * depth == parts
     corr = correlate(source_channel, table, flip, blocks, lines, depth)
     corr = corr.reshape(parts * peers, block, items * chan_count)
-    snake = [range(depth) if c % 2 == 0 else range(depth - 1, -1, -1) for c in range(peers)]
-    group = [(z * lines + q) * peers + c for q in range(lines) for c in range(peers) for z in snake[c]]
+    group = [
+        (z * lines + q) * peers + c for q in range(lines) for z in range(depth) for c in range(peers)
+    ]
     moved = lax.all_to_all(
         corr, ("win", "rcv"), split_axis=0, concat_axis=0, tiled=True, axis_index_groups=[group]
     )
     if items != source_count:
-        moved = moved.reshape(lines, peers, depth, block, items, chan_count)
-        moved = jnp.stack([moved[:, c] if c % 2 == 0 else moved[:, c, ::-1] for c in range(peers)], axis=1)
-        moved = moved.transpose(2, 0, 1, 4, 3, 5)
+        moved = moved.reshape(lines, depth, peers, block, items, chan_count)
+        moved = moved.transpose(1, 0, 2, 4, 3, 5)
         moved = moved.reshape(parts * win_count, source_count, block, chan_count).transpose(0, 2, 1, 3)
         moved = moved.reshape(parts * win_count, block, source_count * chan_count)
     return stack_blocks(moved, source_count)

time: 24 us -> 23.8 us (level)
  no operation moved by 1% of the time
where the time goes in v19:
time: 23.8 us; the launch traced here: 23.7 us
  blocking collectives  17.5 us (74%)
  Pallas kernels  3.81 us (16%)
  waiting for transfers between devices  1.72 us (7%)
  starting transfers between devices  0.52 us (2%)
    all_to_all x1, blocking collectives, per_device(): lax.all_to_all(corr, ('win', 'rcv'), split_axis=0, concat_axis=0, tiled=T...  17.5 us
    pallas_call x1, Pallas kernels, correlate(): pl.pallas_call(functools.partial(correlate_kernel, peers=peers, chunk=chu...  2.21 us
    ppermute x1, waiting for transfers between devices, per_device(): lax.ppermute(spectra, 'rcv', [(i, (i + step) % peers) for i in range(peer...  1.72 us
    pallas_call x1, Pallas kernels, stack_blocks(): pl.pallas_call(stack_kernel, out_shape=jax.ShapeDtypeStruct((pairs, block...  1.57 us
    ppermute x1, starting transfers between devices, per_device(): lax.ppermute(spectra, 'rcv', [(i, (i + step) % peers) for i in range(peer...  0.52 us
  transfers between devices with their start and end apart: 1, of which 1 were waited for; matrix products, arithmetic and copies ran while one was open for 0% of the time, Pallas kernels for 0%

profile of v19, /device:TPU:0, one launch (start us, length us, event | category | flops | bytes accessed | tf_op | source)
XLA Modules:
  0.0 23.7 jit_solution(2205643755505543411)
XLA Ops:
  0.0 0.0 copy-start
  0.0 0.0 copy-start.1
  0.0 0.0 copy-start.2
  0.0 0.5 %collective-permute-start = (bf16[2,2,16,4096]{3,2,1,0:T(8,128)(2,1)}, bf16[2,2,16,4096]{3,2,1,0:T(8,128)(2,1)S(1)}, u32[]{:S(2)}, u32[]{:S(2)}) collective-permute-start(bf16[2,2,16,4096]{3,2,1,0:T(8,128)(2,1)} %refs_3_.1), channel_id=1, source_target_pairs={{0,1},{1,0},{2,3},{3,2},{4,5},{5,4},{6,7},{7,6},{8,9},{9,8},{10,11... | collective-permute-start | bytes 1572872 | tf_op jit(solution)/shard_map/ppermute | solution.py:229
  0.6 1.7 %collective-permute-done.refs_4_ = bf16[2,2,16,4096]{3,2,1,0:T(8,128)(2,1)S(1)} collective-permute-done((bf16[2,2,16,4096]{3,2,1,0:T(8,128)(2,1)}, bf16[2,2,16,4096]{3,2,1,0:T(8,128)(2,1)S(1)}, u32[]{:S(2)}, u32[]{:S(2)}) %collective-permute-start) | collective-permute-done | bytes 524320 | tf_op jit(solution)/shard_map/ppermute | solution.py:229
  2.3 0.0 copy-done
  2.3 0.1 copy-done.1
  2.4 0.0 copy-done.2
  2.4 2.2 %correlate.1 = bf16[4,4,2,32,128]{4,3,2,1,0:T(8,128)(2,1)S(1)} custom-call(s32[8]{0:T(128)S(1)} %copy-done.2, bf16[2,272,4096]{2,1,0:T(8,128)(2,1)S(1)} %copy-done, bf16[256,256]{1,0:T(8,128)(2,1)S(1)} %make_flip.1.refs_2_, bf16[2,2,16,4096]{3,2,1,0:T(8,128)(2,1)S(1)} %copy-done.1, bf16[2,2,16,4096]{3,2,1,0:T(8,128)(2,1)S(1)} %collective-permute-done.refs_4_), custom_call_target="tpu_custom_call" | custom-call | tf_op jit(solution)/shard_map/correlate/pallas_call | solution.py:154
  4.6 17.5 %all_to_all.5.x_ref = bf16[32,32,128]{2,1,0:T(8,128)(2,1)S(1)} all-to-all(bf16[32,32,128]{2,1,0:T(8,128)(2,1)S(1)} %bitcast.4), channel_id=1, replica_groups={{0,1,8,9,16,17,24,25,2,3,10,11,18,19,26,27,4,5,12,13,20,21,28,29,6,7,14..., dimensions={0} | all-to-all | bytes 524288 | tf_op jit(solution)/shard_map/all_to_all | solution.py:240
  22.1 1.6 %bisquare_stack.1 = f32[128,32]{1,0:T(8,128)} custom-call(bf16[32,32,128]{2,1,0:T(8,128)(2,1)S(1)} %all_to_all.5.x_ref), custom_call_target="tpu_custom_call" | custom-call | tf_op jit(solution)/shard_map/bisquare_stack/pallas_call | solution.py:206
  (1 shorter events, 0.0 us)
Async XLA Ops:
  0.0 2.3 %copy-start = (bf16[2,272,4096]{2,1,0:T(8,128)(2,1)S(1)}, bf16[2,272,4096]{2,1,0:T(8,128)(2,1)}, u32[]{:S(2)}) copy-start(bf16[2,272,4096]{2,1,0:T(8,128)(2,1)} %constant.2.clone.refs_1_) | copy-start | bytes 13369348
  0.0 2.4 %copy-start.1 = (bf16[2,2,16,4096]{3,2,1,0:T(8,128)(2,1)S(1)}, bf16[2,2,16,4096]{3,2,1,0:T(8,128)(2,1)}, u32[]{:S(2)}) copy-start(bf16[2,2,16,4096]{3,2,1,0:T(8,128)(2,1)} %refs_3_.1) | copy-start | bytes 1572868
  0.0 2.4 %copy-start.2 = (s32[8]{0:T(128)S(1)}, s32[8]{0:T(128)}, u32[]{:S(2)}) copy-start(s32[8]{0:T(128)} %refs_0_.1) | copy-start | bytes 100
  0.0 2.3 %collective-permute-start = (bf16[2,2,16,4096]{3,2,1,0:T(8,128)(2,1)}, bf16[2,2,16,4096]{3,2,1,0:T(8,128)(2,1)S(1)}, u32[]{:S(2)}, u32[]{:S(2)}) collective-permute-start(bf16[2,2,16,4096]{3,2,1,0:T(8,128)(2,1)} %refs_3_.1), channel_id=1, source_target_pairs={{0,1},{1,0},{2,3},{3,2},{4,5},{5,4},{6,7},{7,6},{8,9},{9,8},{10,11... | collective-permute-start | bytes 1572872 | tf_op jit(solution)/shard_map/ppermute | solution.py:229

commit v20 on v19

--- a/solution.py
+++ b/solution.py
@@ -61,7 +61,7 @@
     source_count = channel_ref.shape[0]
     items = share(win_count, source_count, peers)
     windows = float_ref.shape[0]
-    lines, depth, _, block, width = out_ref.shape
+    _, lines, depth, block, width = out_ref.shape
     half = flip_ref.shape[0]
     me = lax.axis_index("rcv")
     first = lax.div(me * items, source_count)
@@ -139,7 +139,7 @@
                 piece = behind[start : start + block, columns]
             else:
                 piece = ahead[start - half : start - half + block, columns]
-            out_ref[part % lines, part // lines, owner] = piece
+            out_ref[owner, part % lines, part // lines] = piece
 
 
 def correlate(source_channel, table, flip, blocks, lines, depth):
@@ -153,7 +153,7 @@
     vmem = pl.BlockSpec(memory_space=pltpu.VMEM)
     return pl.pallas_call(
         functools.partial(correlate_kernel, peers=peers, chunk=chunk),
-        out_shape=jax.ShapeDtypeStruct((lines, depth, peers, L // (lines * depth), width), jnp.bfloat16),
+        out_shape=jax.ShapeDtypeStruct((peers, lines, depth, L // (lines * depth), width), jnp.bfloat16),
         in_specs=[pl.BlockSpec(memory_space=pltpu.SMEM), vmem, vmem] + [vmem] * peers,
         out_specs=vmem,
         scratch_shapes=[
@@ -235,14 +235,14 @@
     corr = correlate(source_channel, table, flip, blocks, lines, depth)
     corr = corr.reshape(parts * peers, block, items * chan_count)
     group = [
-        (z * lines + q) * peers + c for q in range(lines) for z in range(depth) for c in range(peers)
+        (z * lines + q) * peers + c for c in range(peers) for q in range(lines) for z in range(depth)
     ]
     moved = lax.all_to_all(
         corr, ("win", "rcv"), split_axis=0, concat_axis=0, tiled=True, axis_index_groups=[group]
     )
     if items != source_count:
-        moved = moved.reshape(lines, depth, peers, block, items, chan_count)
-        moved = moved.transpose(1, 0, 2, 4, 3, 5)
+        moved = moved.reshape(peers, lines, depth, block, items, chan_count)
+        moved = moved.transpose(2, 1, 0, 4, 3, 5)
         moved = moved.reshape(parts * win_count, source_count, block, chan_count).transpose(0, 2, 1, 3)
         moved = moved.reshape(parts * win_count, block, source_count * chan_count)
     return stack_blocks(moved, source_count)

time: 23.8 us -> 24.4 us (1.025)
  blocking collectives: 17.5 us -> 18.1 us
    all_to_all x1, blocking collectives: 17.5 us -> 18.1 us  [per_device(): lax.all_to_all(corr, ('win', 'rcv'), split_axis=0, concat_axis=0, tiled=T...]
where the time goes in v20:
time: 24.4 us; the launch traced here: 24.2 us
  blocking collectives  18.1 us (74%)
  Pallas kernels  3.81 us (16%)
  waiting for transfers between devices  1.72 us (7%)
  starting transfers between devices  0.52 us (2%)
    all_to_all x1, blocking collectives, per_device(): lax.all_to_all(corr, ('win', 'rcv'), split_axis=0, concat_axis=0, tiled=T...  18.1 us
    pallas_call x1, Pallas kernels, correlate(): pl.pallas_call(functools.partial(correlate_kernel, peers=peers, chunk=chu...  2.21 us
    ppermute x1, waiting for transfers between devices, per_device(): lax.ppermute(spectra, 'rcv', [(i, (i + step) % peers) for i in range(peer...  1.72 us
    pallas_call x1, Pallas kernels, stack_blocks(): pl.pallas_call(stack_kernel, out_shape=jax.ShapeDtypeStruct((pairs, block...  1.57 us
    ppermute x1, starting transfers between devices, per_device(): lax.ppermute(spectra, 'rcv', [(i, (i + step) % peers) for i in range(peer...  0.52 us
  transfers between devices with their start and end apart: 1, of which 1 were waited for; matrix products, arithmetic and copies ran while one was open for 0% of the time, Pallas kernels for 0%

profile of v20, /device:TPU:0, one launch (start us, length us, event | category | flops | bytes accessed | tf_op | source)
XLA Modules:
  0.0 24.2 jit_solution(3179521293007391639)
XLA Ops:
  0.0 0.0 copy-start
  0.0 0.0 copy-start.1
  0.0 0.0 copy-start.2
  0.0 0.5 %collective-permute-start = (bf16[2,2,16,4096]{3,2,1,0:T(8,128)(2,1)}, bf16[2,2,16,4096]{3,2,1,0:T(8,128)(2,1)S(1)}, u32[]{:S(2)}, u32[]{:S(2)}) collective-permute-start(bf16[2,2,16,4096]{3,2,1,0:T(8,128)(2,1)} %refs_3_.1), channel_id=1, source_target_pairs={{0,1},{1,0},{2,3},{3,2},{4,5},{5,4},{6,7},{7,6},{8,9},{9,8},{10,11... | collective-permute-start | bytes 1572872 | tf_op jit(solution)/shard_map/ppermute | solution.py:229
  0.6 1.7 %collective-permute-done.refs_4_ = bf16[2,2,16,4096]{3,2,1,0:T(8,128)(2,1)S(1)} collective-permute-done((bf16[2,2,16,4096]{3,2,1,0:T(8,128)(2,1)}, bf16[2,2,16,4096]{3,2,1,0:T(8,128)(2,1)S(1)}, u32[]{:S(2)}, u32[]{:S(2)}) %collective-permute-start) | collective-permute-done | bytes 524320 | tf_op jit(solution)/shard_map/ppermute | solution.py:229
  2.3 0.0 copy-done
  2.3 0.1 copy-done.1
  2.4 0.0 copy-done.2
  2.4 2.2 %correlate.1 = bf16[2,4,4,32,128]{4,3,2,1,0:T(8,128)(2,1)S(1)} custom-call(s32[8]{0:T(128)S(1)} %copy-done.2, bf16[2,272,4096]{2,1,0:T(8,128)(2,1)S(1)} %copy-done, bf16[256,256]{1,0:T(8,128)(2,1)S(1)} %make_flip.1.refs_2_, bf16[2,2,16,4096]{3,2,1,0:T(8,128)(2,1)S(1)} %copy-done.1, bf16[2,2,16,4096]{3,2,1,0:T(8,128)(2,1)S(1)} %collective-permute-done.refs_4_), custom_call_target="tpu_custom_call" | custom-call | tf_op jit(solution)/shard_map/correlate/pallas_call | solution.py:154
  4.6 18.1 %all_to_all.5.x_ref = bf16[32,32,128]{2,1,0:T(8,128)(2,1)S(1)} all-to-all(bf16[32,32,128]{2,1,0:T(8,128)(2,1)S(1)} %bitcast.4), channel_id=1, replica_groups={{0,8,16,24,2,10,18,26,4,12,20,28,6,14,22,30,1,9,17,25,3,11,19,27,5,13,2..., dimensions={0} | all-to-all | bytes 524288 | tf_op jit(solution)/shard_map/all_to_all | solution.py:240
  22.7 1.6 %bisquare_stack.1 = f32[128,32]{1,0:T(8,128)} custom-call(bf16[32,32,128]{2,1,0:T(8,128)(2,1)S(1)} %all_to_all.5.x_ref), custom_call_target="tpu_custom_call" | custom-call | tf_op jit(solution)/shard_map/bisquare_stack/pallas_call | solution.py:206
  (1 shorter events, 0.0 us)
Async XLA Ops:
  0.0 2.3 %copy-start = (bf16[2,272,4096]{2,1,0:T(8,128)(2,1)S(1)}, bf16[2,272,4096]{2,1,0:T(8,128)(2,1)}, u32[]{:S(2)}) copy-start(bf16[2,272,4096]{2,1,0:T(8,128)(2,1)} %constant.2.clone.refs_1_) | copy-start | bytes 13369348
  0.0 2.4 %copy-start.1 = (bf16[2,2,16,4096]{3,2,1,0:T(8,128)(2,1)S(1)}, bf16[2,2,16,4096]{3,2,1,0:T(8,128)(2,1)}, u32[]{:S(2)}) copy-start(bf16[2,2,16,4096]{3,2,1,0:T(8,128)(2,1)} %refs_3_.1) | copy-start | bytes 1572868
  0.0 2.4 %copy-start.2 = (s32[8]{0:T(128)S(1)}, s32[8]{0:T(128)}, u32[]{:S(2)}) copy-start(s32[8]{0:T(128)} %refs_0_.1) | copy-start | bytes 100
  0.0 2.3 %collective-permute-start = (bf16[2,2,16,4096]{3,2,1,0:T(8,128)(2,1)}, bf16[2,2,16,4096]{3,2,1,0:T(8,128)(2,1)S(1)}, u32[]{:S(2)}, u32[]{:S(2)}) collective-permute-start(bf16[2,2,16,4096]{3,2,1,0:T(8,128)(2,1)} %refs_3_.1), channel_id=1, source_target_pairs={{0,1},{1,0},{2,3},{3,2},{4,5},{5,4},{6,7},{7,6},{8,9},{9,8},{10,11... | collective-permute-start | bytes 1572872 | tf_op jit(solution)/shard_map/ppermute | solution.py:229

commit v21 on v18

--- a/solution.py
+++ b/solution.py
@@ -139,8 +139,7 @@
                 piece = behind[start : start + block, columns]
             else:
                 piece = ahead[start - half : start - half + block, columns]
-            z = part // lines
-            out_ref[part % lines, owner, z + lax.rem(owner, 2) * (depth - 1 - 2 * z)] = piece
+            out_ref[part % lines, owner, part // lines] = piece
 
 
 def correlate(source_channel, table, flip, blocks, lines, depth):
@@ -235,14 +234,14 @@
     assert lines * depth == parts
     corr = correlate(source_channel, table, flip, blocks, lines, depth)
     corr = corr.reshape(parts * peers, block, items * chan_count)
-    snake = [range(depth) if c % 2 == 0 else range(depth - 1, -1, -1) for c in range(peers)]
-    group = [(z * lines + q) * peers + c for q in range(lines) for c in range(peers) for z in snake[c]]
+    group = [
+        (z * lines + q) * peers + c for q in range(lines) for c in range(peers) for z in range(depth)
+    ]
     moved = lax.all_to_all(
         corr, ("win", "rcv"), split_axis=0, concat_axis=0, tiled=True, axis_index_groups=[group]
     )
     if items != source_count:
         moved = moved.reshape(lines, peers, depth, block, items, chan_count)
-        moved = jnp.stack([moved[:, c] if c % 2 == 0 else moved[:, c, ::-1] for c in range(peers)], axis=1)
         moved = moved.transpose(2, 0, 1, 4, 3, 5)
         moved = moved.reshape(parts * win_count, source_count, block, chan_count).transpose(0, 2, 1, 3)
         moved = moved.reshape(parts * win_count, block, source_count * chan_count)

time: 24 us -> 23.6 us (0.983)
  blocking collectives: 17.7 us -> 17.3 us
    all_to_all x1, blocking collectives: 17.7 us -> 17.3 us  [per_device(): lax.all_to_all(corr, ('win', 'rcv'), split_axis=0, concat_axis=0, tiled=T...]
where the time goes in v21:
time: 23.6 us; the launch traced here: 23.5 us
  blocking collectives  17.3 us (73%)
  Pallas kernels  3.81 us (16%)
  waiting for transfers between devices  1.72 us (7%)
  starting transfers between devices  0.52 us (2%)
    all_to_all x1, blocking collectives, per_device(): lax.all_to_all(corr, ('win', 'rcv'), split_axis=0, concat_axis=0, tiled=T...  17.3 us
    pallas_call x1, Pallas kernels, correlate(): pl.pallas_call(functools.partial(correlate_kernel, peers=peers, chunk=chu...  2.21 us
    ppermute x1, waiting for transfers between devices, per_device(): lax.ppermute(spectra, 'rcv', [(i, (i + step) % peers) for i in range(peer...  1.72 us
    pallas_call x1, Pallas kernels, stack_blocks(): pl.pallas_call(stack_kernel, out_shape=jax.ShapeDtypeStruct((pairs, block...  1.57 us
    ppermute x1, starting transfers between devices, per_device(): lax.ppermute(spectra, 'rcv', [(i, (i + step) % peers) for i in range(peer...  0.52 us
  transfers between devices with their start and end apart: 1, of which 1 were waited for; matrix products, arithmetic and copies ran while one was open for 0% of the time, Pallas kernels for 0%

profile of v21, /device:TPU:0, one launch (start us, length us, event | category | flops | bytes accessed | tf_op | source)
XLA Modules:
  0.0 23.5 jit_solution(17365977189483363396)
XLA Ops:
  0.0 0.0 copy-start
  0.0 0.0 copy-start.1
  0.0 0.0 copy-start.2
  0.0 0.5 %collective-permute-start = (bf16[2,2,16,4096]{3,2,1,0:T(8,128)(2,1)}, bf16[2,2,16,4096]{3,2,1,0:T(8,128)(2,1)S(1)}, u32[]{:S(2)}, u32[]{:S(2)}) collective-permute-start(bf16[2,2,16,4096]{3,2,1,0:T(8,128)(2,1)} %refs_3_.1), channel_id=1, source_target_pairs={{0,1},{1,0},{2,3},{3,2},{4,5},{5,4},{6,7},{7,6},{8,9},{9,8},{10,11... | collective-permute-start | bytes 1572872 | tf_op jit(solution)/shard_map/ppermute | solution.py:229
  0.6 1.7 %collective-permute-done.refs_4_ = bf16[2,2,16,4096]{3,2,1,0:T(8,128)(2,1)S(1)} collective-permute-done((bf16[2,2,16,4096]{3,2,1,0:T(8,128)(2,1)}, bf16[2,2,16,4096]{3,2,1,0:T(8,128)(2,1)S(1)}, u32[]{:S(2)}, u32[]{:S(2)}) %collective-permute-start) | collective-permute-done | bytes 524320 | tf_op jit(solution)/shard_map/ppermute | solution.py:229
  2.3 0.0 copy-done
  2.3 0.1 copy-done.1
  2.4 0.0 copy-done.2
  2.4 2.2 %correlate.1 = bf16[4,2,4,32,128]{4,3,2,1,0:T(8,128)(2,1)S(1)} custom-call(s32[8]{0:T(128)S(1)} %copy-done.2, bf16[2,272,4096]{2,1,0:T(8,128)(2,1)S(1)} %copy-done, bf16[256,256]{1,0:T(8,128)(2,1)S(1)} %make_flip.1.refs_2_, bf16[2,2,16,4096]{3,2,1,0:T(8,128)(2,1)S(1)} %copy-done.1, bf16[2,2,16,4096]{3,2,1,0:T(8,128)(2,1)S(1)} %collective-permute-done.refs_4_), custom_call_target="tpu_custom_call" | custom-call | tf_op jit(solution)/shard_map/correlate/pallas_call | solution.py:154
  4.6 17.3 %all_to_all.5.x_ref = bf16[32,32,128]{2,1,0:T(8,128)(2,1)S(1)} all-to-all(bf16[32,32,128]{2,1,0:T(8,128)(2,1)S(1)} %bitcast.4), channel_id=1, replica_groups={{0,8,16,24,1,9,17,25,2,10,18,26,3,11,19,27,4,12,20,28,5,13,21,29,6,14,2..., dimensions={0} | all-to-all | bytes 524288 | tf_op jit(solution)/shard_map/all_to_all | solution.py:240
  21.9 1.6 %bisquare_stack.1 = f32[128,32]{1,0:T(8,128)} custom-call(bf16[32,32,128]{2,1,0:T(8,128)(2,1)S(1)} %all_to_all.5.x_ref), custom_call_target="tpu_custom_call" | custom-call | tf_op jit(solution)/shard_map/bisquare_stack/pallas_call | solution.py:206
  (1 shorter events, 0.0 us)
Async XLA Ops:
  0.0 2.3 %copy-start = (bf16[2,272,4096]{2,1,0:T(8,128)(2,1)S(1)}, bf16[2,272,4096]{2,1,0:T(8,128)(2,1)}, u32[]{:S(2)}) copy-start(bf16[2,272,4096]{2,1,0:T(8,128)(2,1)} %constant.2.clone.refs_1_) | copy-start | bytes 13369348
  0.0 2.4 %copy-start.1 = (bf16[2,2,16,4096]{3,2,1,0:T(8,128)(2,1)S(1)}, bf16[2,2,16,4096]{3,2,1,0:T(8,128)(2,1)}, u32[]{:S(2)}) copy-start(bf16[2,2,16,4096]{3,2,1,0:T(8,128)(2,1)} %refs_3_.1) | copy-start | bytes 1572868
  0.0 2.4 %copy-start.2 = (s32[8]{0:T(128)S(1)}, s32[8]{0:T(128)}, u32[]{:S(2)}) copy-start(s32[8]{0:T(128)} %refs_0_.1) | copy-start | bytes 100
  0.0 2.3 %collective-permute-start = (bf16[2,2,16,4096]{3,2,1,0:T(8,128)(2,1)}, bf16[2,2,16,4096]{3,2,1,0:T(8,128)(2,1)S(1)}, u32[]{:S(2)}, u32[]{:S(2)}) collective-permute-start(bf16[2,2,16,4096]{3,2,1,0:T(8,128)(2,1)} %refs_3_.1), channel_id=1, source_target_pairs={{0,1},{1,0},{2,3},{3,2},{4,5},{5,4},{6,7},{7,6},{8,9},{9,8},{10,11... | collective-permute-start | bytes 1572872 | tf_op jit(solution)/shard_map/ppermute | solution.py:229

commit v22 on v21

--- a/solution.py
+++ b/solution.py
@@ -117,8 +117,10 @@
             form_cross(chunks[index], range(items // 2, items))
         if index > 0:
             add_product(chunks[index - 1], 1, odd_ref)
-    ahead = (even_ref[:half, :] + odd_ref[:half, :]).astype(jnp.bfloat16)
-    back = (even_ref[...] - odd_ref[...]).astype(jnp.bfloat16)
+    place = (lax.axis_index("win") * peers + me).astype(jnp.float32)
+    factor = 1.0 + place * (1.0 / (lines * depth * peers))
+    ahead = ((even_ref[:half, :] + odd_ref[:half, :]) * factor).astype(jnp.bfloat16)
+    back = ((even_ref[...] - odd_ref[...]) * factor).astype(jnp.bfloat16)
     turned = jnp.dot(flip_ref[...], back[:half], preferred_element_type=jnp.float32)
     behind = jnp.where(
         lax.broadcasted_iota(jnp.int32, turned.shape, 0) == 0,
@@ -168,10 +170,10 @@
     )(source_channel, table, flip, *blocks)
 
 
-def stack_kernel(x_ref, out_ref, y_ref):
+def stack_kernel(x_ref, out_ref, y_ref, *, factors):
     count, block, pairs = x_ref.shape
     for n in range(count):
-        y_ref[n] = x_ref[n].astype(jnp.float32)
+        y_ref[n] = x_ref[n].astype(jnp.float32) * (1.0 / factors[n])
     mean = tree_sum([y_ref[n] for n in range(count)]) * (1.0 / count)
     squares = []
     for n in range(count):
@@ -201,10 +203,10 @@
     return sums[0] + sums[1]
 
 
-def stack_blocks(samples, source_count):
+def stack_blocks(samples, factors, source_count):
     count, block, pairs = samples.shape
     result = pl.pallas_call(
-        stack_kernel,
+        functools.partial(stack_kernel, factors=factors),
         out_shape=jax.ShapeDtypeStruct((pairs, block), jnp.float32),
         in_specs=[pl.BlockSpec(memory_space=pltpu.VMEM)],
         out_specs=pl.BlockSpec(memory_space=pltpu.VMEM),
@@ -240,12 +242,15 @@
     moved = lax.all_to_all(
         corr, ("win", "rcv"), split_axis=0, concat_axis=0, tiled=True, axis_index_groups=[group]
     )
+    factors = [1.0 + device / len(group) for device in group]
     if items != source_count:
+        moved = moved.astype(jnp.float32) / jnp.asarray(factors, jnp.float32)[:, None, None]
+        factors = [1.0] * (parts * win_count)
         moved = moved.reshape(lines, peers, depth, block, items, chan_count)
         moved = moved.transpose(2, 0, 1, 4, 3, 5)
         moved = moved.reshape(parts * win_count, source_count, block, chan_count).transpose(0, 2, 1, 3)
         moved = moved.reshape(parts * win_count, block, source_count * chan_count)
-    return stack_blocks(moved, source_count)
+    return stack_blocks(moved, factors, source_count)
 
 
 def solution(mesh):

time: 23.6 us -> 23.6 us (level)
  no operation moved by 1% of the time
where the time goes in v22:
time: 23.6 us; the launch traced here: 23.5 us
  blocking collectives  17.3 us (73%)
  Pallas kernels  3.82 us (16%)
  waiting for transfers between devices  1.72 us (7%)
  starting transfers between devices  0.52 us (2%)
    all_to_all x1, blocking collectives, per_device(): lax.all_to_all(corr, ('win', 'rcv'), split_axis=0, concat_axis=0, tiled=T...  17.3 us
    pallas_call x1, Pallas kernels, correlate(): pl.pallas_call(functools.partial(correlate_kernel, peers=peers, chunk=chu...  2.22 us
    ppermute x1, waiting for transfers between devices, per_device(): lax.ppermute(spectra, 'rcv', [(i, (i + step) % peers) for i in range(peer...  1.72 us
    pallas_call x1, Pallas kernels, stack_blocks(): pl.pallas_call(functools.partial(stack_kernel, factors=factors), out_shap...  1.57 us
    ppermute x1, starting transfers between devices, per_device(): lax.ppermute(spectra, 'rcv', [(i, (i + step) % peers) for i in range(peer...  0.52 us
  transfers between devices with their start and end apart: 1, of which 1 were waited for; matrix products, arithmetic and copies ran while one was open for 0% of the time, Pallas kernels for 0%

profile of v22, /device:TPU:0, one launch (start us, length us, event | category | flops | bytes accessed | tf_op | source)
XLA Modules:
  0.0 23.5 jit_solution(13704721943955885096)
XLA Ops:
  0.0 0.0 copy-start
  0.0 0.0 copy-start.1
  0.0 0.0 copy-start.2
  0.0 0.5 %collective-permute-start = (bf16[2,2,16,4096]{3,2,1,0:T(8,128)(2,1)}, bf16[2,2,16,4096]{3,2,1,0:T(8,128)(2,1)S(1)}, u32[]{:S(2)}, u32[]{:S(2)}) collective-permute-start(bf16[2,2,16,4096]{3,2,1,0:T(8,128)(2,1)} %refs_3_.1), channel_id=1, source_target_pairs={{0,1},{1,0},{2,3},{3,2},{4,5},{5,4},{6,7},{7,6},{8,9},{9,8},{10,11... | collective-permute-start | bytes 1572872 | tf_op jit(solution)/shard_map/ppermute | solution.py:231
  0.6 1.7 %collective-permute-done.refs_4_ = bf16[2,2,16,4096]{3,2,1,0:T(8,128)(2,1)S(1)} collective-permute-done((bf16[2,2,16,4096]{3,2,1,0:T(8,128)(2,1)}, bf16[2,2,16,4096]{3,2,1,0:T(8,128)(2,1)S(1)}, u32[]{:S(2)}, u32[]{:S(2)}) %collective-permute-start) | collective-permute-done | bytes 524320 | tf_op jit(solution)/shard_map/ppermute | solution.py:231
  2.3 0.0 copy-done
  2.3 0.1 copy-done.1
  2.4 0.0 copy-done.2
  2.4 2.2 %correlate.1 = bf16[4,2,4,32,128]{4,3,2,1,0:T(8,128)(2,1)S(1)} custom-call(s32[8]{0:T(128)S(1)} %copy-done.2, bf16[2,272,4096]{2,1,0:T(8,128)(2,1)S(1)} %copy-done, bf16[256,256]{1,0:T(8,128)(2,1)S(1)} %make_flip.1.refs_2_, bf16[2,2,16,4096]{3,2,1,0:T(8,128)(2,1)S(1)} %copy-done.1, bf16[2,2,16,4096]{3,2,1,0:T(8,128)(2,1)S(1)} %collective-permute-done.refs_4_), custom_call_target="tpu_custom_call" | custom-call | tf_op jit(solution)/shard_map/correlate/pallas_call | solution.py:156
  4.6 17.3 %all_to_all.5.x_ref = bf16[32,32,128]{2,1,0:T(8,128)(2,1)S(1)} all-to-all(bf16[32,32,128]{2,1,0:T(8,128)(2,1)S(1)} %bitcast.4), channel_id=1, replica_groups={{0,8,16,24,1,9,17,25,2,10,18,26,3,11,19,27,4,12,20,28,5,13,21,29,6,14,2..., dimensions={0} | all-to-all | bytes 524288 | tf_op jit(solution)/shard_map/all_to_all | solution.py:242
  21.9 1.6 %bisquare_stack.1 = f32[128,32]{1,0:T(8,128)} custom-call(bf16[32,32,128]{2,1,0:T(8,128)(2,1)S(1)} %all_to_all.5.x_ref), custom_call_target="tpu_custom_call" | custom-call | tf_op jit(solution)/shard_map/bisquare_stack/pallas_call | solution.py:208
  (1 shorter events, 0.0 us)
Async XLA Ops:
  0.0 2.3 %copy-start = (bf16[2,272,4096]{2,1,0:T(8,128)(2,1)S(1)}, bf16[2,272,4096]{2,1,0:T(8,128)(2,1)}, u32[]{:S(2)}) copy-start(bf16[2,272,4096]{2,1,0:T(8,128)(2,1)} %constant.2.clone.refs_1_) | copy-start | bytes 13369348
  0.0 2.4 %copy-start.1 = (bf16[2,2,16,4096]{3,2,1,0:T(8,128)(2,1)S(1)}, bf16[2,2,16,4096]{3,2,1,0:T(8,128)(2,1)}, u32[]{:S(2)}) copy-start(bf16[2,2,16,4096]{3,2,1,0:T(8,128)(2,1)} %refs_3_.1) | copy-start | bytes 1572868
  0.0 2.4 %copy-start.2 = (s32[8]{0:T(128)S(1)}, s32[8]{0:T(128)}, u32[]{:S(2)}) copy-start(s32[8]{0:T(128)} %refs_0_.1) | copy-start | bytes 100
  0.0 2.3 %collective-permute-start = (bf16[2,2,16,4096]{3,2,1,0:T(8,128)(2,1)}, bf16[2,2,16,4096]{3,2,1,0:T(8,128)(2,1)S(1)}, u32[]{:S(2)}, u32[]{:S(2)}) collective-permute-start(bf16[2,2,16,4096]{3,2,1,0:T(8,128)(2,1)} %refs_3_.1), channel_id=1, source_target_pairs={{0,1},{1,0},{2,3},{3,2},{4,5},{5,4},{6,7},{7,6},{8,9},{9,8},{10,11... | collective-permute-start | bytes 1572872 | tf_op jit(solution)/shard_map/ppermute | solution.py:231

commit v23 on v22

--- a/solution.py
+++ b/solution.py
@@ -82,17 +82,17 @@
     def form_cross(bins, some):
         for t in some:
             w = t // source_count
-            real_p = float_ref[w, 0, :, bins]
-            imag_q = float_ref[w, 1, :, bins]
-            real_a = float_ref[w, 0, pl.ds(rows[t], 1), bins]
-            imag_b = float_ref[w, 1, pl.ds(rows[t], 1), bins]
-            real = (real_a * real_p + imag_b * imag_q).astype(jnp.bfloat16)
-            imag = (imag_b * real_p - real_a * imag_q).astype(jnp.bfloat16)
-            for k in range(peers):
-                receivers = slice(k * chan_count, (k + 1) * chan_count)
-                pairs = slice(k * width + t * chan_count, k * width + (t + 1) * chan_count)
-                cross_ref[0, pairs, bins] = real[receivers]
-                cross_ref[1, pairs, bins] = imag[receivers]
+            real_p = by_eights(float_ref[w, 0, :, bins])
+            imag_q = by_eights(float_ref[w, 1, :, bins])
+            real_a = spread(float_ref[w, 0, pl.ds(rows[t], 1), bins])
+            imag_b = spread(float_ref[w, 1, pl.ds(rows[t], 1), bins])
+            real = real_a * real_p + imag_b * imag_q
+            imag = imag_b * real_p - real_a * imag_q
+            for index, value in ((0, real), (1, imag)):
+                value = value.reshape(peers * chan_count, value.shape[2]).astype(jnp.bfloat16)
+                for k in range(peers):
+                    pairs = slice(k * width + t * chan_count, k * width + (t + 1) * chan_count)
+                    cross_ref[index, pairs, bins] = value[k * chan_count : (k + 1) * chan_count]
 
     def add_product(bins, index, sum_ref):
         term = lax.dot_general(
@@ -144,6 +144,14 @@
             out_ref[part % lines, owner, part // lines] = piece
 
 
+def by_eights(values):
+    return values.reshape(values.shape[0] // 8, 8, values.shape[1])
+
+
+def spread(row):
+    return jnp.broadcast_to(row, (8, row.shape[1]))[None]
+
+
 def correlate(source_channel, table, flip, blocks, lines, depth):
     win_count, _, chan_count, bin_count = blocks[0].shape
     source_count = source_channel.shape[0]

time: 23.6 us -> 23.6 us (level)
  no operation moved by 1% of the time
where the time goes in v23:
time: 23.6 us; the launch traced here: 23.5 us
  blocking collectives  17.3 us (73%)
  Pallas kernels  3.82 us (16%)
  waiting for transfers between devices  1.72 us (7%)
  starting transfers between devices  0.52 us (2%)
    all_to_all x1, blocking collectives, per_device(): lax.all_to_all(corr, ('win', 'rcv'), split_axis=0, concat_axis=0, tiled=T...  17.3 us
    pallas_call x1, Pallas kernels, correlate(): pl.pallas_call(functools.partial(correlate_kernel, peers=peers, chunk=chu...  2.22 us
    ppermute x1, waiting for transfers between devices, per_device(): lax.ppermute(spectra, 'rcv', [(i, (i + step) % peers) for i in range(peer...  1.72 us
    pallas_call x1, Pallas kernels, stack_blocks(): pl.pallas_call(functools.partial(stack_kernel, factors=factors), out_shap...  1.57 us
    ppermute x1, starting transfers between devices, per_device(): lax.ppermute(spectra, 'rcv', [(i, (i + step) % peers) for i in range(peer...  0.52 us
  transfers between devices with their start and end apart: 1, of which 1 were waited for; matrix products, arithmetic and copies ran while one was open for 0% of the time, Pallas kernels for 0%

profile of v23, /device:TPU:0, one launch (start us, length us, event | category | flops | bytes accessed | tf_op | source)
XLA Modules:
  0.0 23.5 jit_solution(13704721943955885096)
XLA Ops:
  0.0 0.0 copy-start
  0.0 0.0 copy-start.1
  0.0 0.0 copy-start.2
  0.0 0.5 %collective-permute-start = (bf16[2,2,16,4096]{3,2,1,0:T(8,128)(2,1)}, bf16[2,2,16,4096]{3,2,1,0:T(8,128)(2,1)S(1)}, u32[]{:S(2)}, u32[]{:S(2)}) collective-permute-start(bf16[2,2,16,4096]{3,2,1,0:T(8,128)(2,1)} %refs_3_.1), channel_id=1, source_target_pairs={{0,1},{1,0},{2,3},{3,2},{4,5},{5,4},{6,7},{7,6},{8,9},{9,8},{10,11... | collective-permute-start | bytes 1572872 | tf_op jit(solution)/shard_map/ppermute | solution.py:239
  0.6 1.7 %collective-permute-done.refs_4_ = bf16[2,2,16,4096]{3,2,1,0:T(8,128)(2,1)S(1)} collective-permute-done((bf16[2,2,16,4096]{3,2,1,0:T(8,128)(2,1)}, bf16[2,2,16,4096]{3,2,1,0:T(8,128)(2,1)S(1)}, u32[]{:S(2)}, u32[]{:S(2)}) %collective-permute-start) | collective-permute-done | bytes 524320 | tf_op jit(solution)/shard_map/ppermute | solution.py:239
  2.3 0.0 copy-done
  2.3 0.1 copy-done.1
  2.4 0.0 copy-done.2
  2.4 2.2 %correlate.1 = bf16[4,2,4,32,128]{4,3,2,1,0:T(8,128)(2,1)S(1)} custom-call(s32[8]{0:T(128)S(1)} %copy-done.2, bf16[2,272,4096]{2,1,0:T(8,128)(2,1)S(1)} %copy-done, bf16[256,256]{1,0:T(8,128)(2,1)S(1)} %make_flip.1.refs_2_, bf16[2,2,16,4096]{3,2,1,0:T(8,128)(2,1)S(1)} %copy-done.1, bf16[2,2,16,4096]{3,2,1,0:T(8,128)(2,1)S(1)} %collective-permute-done.refs_4_), custom_call_target="tpu_custom_call" | custom-call | tf_op jit(solution)/shard_map/correlate/pallas_call | solution.py:164
  4.6 17.3 %all_to_all.5.x_ref = bf16[32,32,128]{2,1,0:T(8,128)(2,1)S(1)} all-to-all(bf16[32,32,128]{2,1,0:T(8,128)(2,1)S(1)} %bitcast.4), channel_id=1, replica_groups={{0,8,16,24,1,9,17,25,2,10,18,26,3,11,19,27,4,12,20,28,5,13,21,29,6,14,2..., dimensions={0} | all-to-all | bytes 524288 | tf_op jit(solution)/shard_map/all_to_all | solution.py:250
  21.9 1.6 %bisquare_stack.1 = f32[128,32]{1,0:T(8,128)} custom-call(bf16[32,32,128]{2,1,0:T(8,128)(2,1)S(1)} %all_to_all.5.x_ref), custom_call_target="tpu_custom_call" | custom-call | tf_op jit(solution)/shard_map/bisquare_stack/pallas_call | solution.py:216
  (1 shorter events, 0.0 us)
Async XLA Ops:
  0.0 2.3 %copy-start = (bf16[2,272,4096]{2,1,0:T(8,128)(2,1)S(1)}, bf16[2,272,4096]{2,1,0:T(8,128)(2,1)}, u32[]{:S(2)}) copy-start(bf16[2,272,4096]{2,1,0:T(8,128)(2,1)} %constant.2.clone.refs_1_) | copy-start | bytes 13369348
  0.0 2.4 %copy-start.1 = (bf16[2,2,16,4096]{3,2,1,0:T(8,128)(2,1)S(1)}, bf16[2,2,16,4096]{3,2,1,0:T(8,128)(2,1)}, u32[]{:S(2)}) copy-start(bf16[2,2,16,4096]{3,2,1,0:T(8,128)(2,1)} %refs_3_.1) | copy-start | bytes 1572868
  0.0 2.4 %copy-start.2 = (s32[8]{0:T(128)S(1)}, s32[8]{0:T(128)}, u32[]{:S(2)}) copy-start(s32[8]{0:T(128)} %refs_0_.1) | copy-start | bytes 100
  0.0 2.3 %collective-permute-start = (bf16[2,2,16,4096]{3,2,1,0:T(8,128)(2,1)}, bf16[2,2,16,4096]{3,2,1,0:T(8,128)(2,1)S(1)}, u32[]{:S(2)}, u32[]{:S(2)}) collective-permute-start(bf16[2,2,16,4096]{3,2,1,0:T(8,128)(2,1)} %refs_3_.1), channel_id=1, source_target_pairs={{0,1},{1,0},{2,3},{3,2},{4,5},{5,4},{6,7},{7,6},{8,9},{9,8},{10,11... | collective-permute-start | bytes 1572872 | tf_op jit(solution)/shard_map/ppermute | solution.py:239

commit v24 on v22

--- a/solution.py
+++ b/solution.py
@@ -110,13 +110,14 @@
     for index in range(len(chunks) + 1):
         if index < len(chunks):
             widen(chunks[index])
-            form_cross(chunks[index], range(items // 2))
         if index > 0:
             add_product(chunks[index - 1], 0, even_ref)
         if index < len(chunks):
-            form_cross(chunks[index], range(items // 2, items))
+            form_cross(chunks[index], range(items // 2))
         if index > 0:
             add_product(chunks[index - 1], 1, odd_ref)
+        if index < len(chunks):
+            form_cross(chunks[index], range(items // 2, items))
     place = (lax.axis_index("win") * peers + me).astype(jnp.float32)
     factor = 1.0 + place * (1.0 / (lines * depth * peers))
     ahead = ((even_ref[:half, :] + odd_ref[:half, :]) * factor).astype(jnp.bfloat16)
@@ -130,6 +131,7 @@
     if block % 16 != 0:
         lags_ref[half:, :] = ahead.astype(jnp.float32)
         lags_ref[:half, :] = behind.astype(jnp.float32)
+    columns_order = gray(lines)
     for k in range(peers):
         owner = lax.rem(me - k + peers, peers)
         columns = slice(k * width, (k + 1) * width)
@@ -141,7 +143,11 @@
                 piece = behind[start : start + block, columns]
             else:
                 piece = ahead[start - half : start - half + block, columns]
-            out_ref[part % lines, owner, part // lines] = piece
+            out_ref[columns_order.index(part % lines), owner, part // lines] = piece
+
+
+def gray(count):
+    return [index ^ (index >> 1) for index in range(count)]
 
 
 def correlate(source_channel, table, flip, blocks, lines, depth):
@@ -237,7 +243,7 @@
     corr = correlate(source_channel, table, flip, blocks, lines, depth)
     corr = corr.reshape(parts * peers, block, items * chan_count)
     group = [
-        (z * lines + q) * peers + c for q in range(lines) for c in range(peers) for z in range(depth)
+        (z * lines + q) * peers + c for q in gray(lines) for c in range(peers) for z in range(depth)
     ]
     moved = lax.all_to_all(
         corr, ("win", "rcv"), split_axis=0, concat_axis=0, tiled=True, axis_index_groups=[group]
@@ -247,6 +253,7 @@
         moved = moved.astype(jnp.float32) / jnp.asarray(factors, jnp.float32)[:, None, None]
         factors = [1.0] * (parts * win_count)
         moved = moved.reshape(lines, peers, depth, block, items, chan_count)
+        moved = jnp.stack([moved[gray(lines).index(q)] for q in range(lines)])
         moved = moved.transpose(2, 0, 1, 4, 3, 5)
         moved = moved.reshape(parts * win_count, source_count, block, chan_count).transpose(0, 2, 1, 3)
         moved = moved.reshape(parts * win_count, block, source_count * chan_count)

time: 23.6 us -> 24 us (1.017)
  blocking collectives: 17.3 us -> 17.6 us
    all_to_all x1, blocking collectives: 17.3 us -> 17.6 us  [per_device(): lax.all_to_all(corr, ('win', 'rcv'), split_axis=0, concat_axis=0, tiled=T...]
where the time goes in v24:
time: 24 us; the launch traced here: 23.8 us
  blocking collectives  17.6 us (73%)
  Pallas kernels  3.82 us (16%)
  waiting for transfers between devices  1.72 us (7%)
  starting transfers between devices  0.52 us (2%)
    all_to_all x1, blocking collectives, per_device(): lax.all_to_all(corr, ('win', 'rcv'), split_axis=0, concat_axis=0, tiled=T...  17.6 us
    pallas_call x1, Pallas kernels, correlate(): pl.pallas_call(functools.partial(correlate_kernel, peers=peers, chunk=chu...  2.22 us
    ppermute x1, waiting for transfers between devices, per_device(): lax.ppermute(spectra, 'rcv', [(i, (i + step) % peers) for i in range(peer...  1.72 us
    pallas_call x1, Pallas kernels, stack_blocks(): pl.pallas_call(functools.partial(stack_kernel, factors=factors), out_shap...  1.57 us
    ppermute x1, starting transfers between devices, per_device(): lax.ppermute(spectra, 'rcv', [(i, (i + step) % peers) for i in range(peer...  0.52 us
  transfers between devices with their start and end apart: 1, of which 1 were waited for; matrix products, arithmetic and copies ran while one was open for 0% of the time, Pallas kernels for 0%

profile of v24, /device:TPU:0, one launch (start us, length us, event | category | flops | bytes accessed | tf_op | source)
XLA Modules:
  0.0 23.8 jit_solution(3570911886748382680)
XLA Ops:
  0.0 0.0 copy-start
  0.0 0.0 copy-start.1
  0.0 0.0 copy-start.2
  0.0 0.5 %collective-permute-start = (bf16[2,2,16,4096]{3,2,1,0:T(8,128)(2,1)}, bf16[2,2,16,4096]{3,2,1,0:T(8,128)(2,1)S(1)}, u32[]{:S(2)}, u32[]{:S(2)}) collective-permute-start(bf16[2,2,16,4096]{3,2,1,0:T(8,128)(2,1)} %refs_3_.1), channel_id=1, source_target_pairs={{0,1},{1,0},{2,3},{3,2},{4,5},{5,4},{6,7},{7,6},{8,9},{9,8},{10,11... | collective-permute-start | bytes 1572872 | tf_op jit(solution)/shard_map/ppermute | solution.py:237
  0.6 1.7 %collective-permute-done.refs_4_ = bf16[2,2,16,4096]{3,2,1,0:T(8,128)(2,1)S(1)} collective-permute-done((bf16[2,2,16,4096]{3,2,1,0:T(8,128)(2,1)}, bf16[2,2,16,4096]{3,2,1,0:T(8,128)(2,1)S(1)}, u32[]{:S(2)}, u32[]{:S(2)}) %collective-permute-start) | collective-permute-done | bytes 524320 | tf_op jit(solution)/shard_map/ppermute | solution.py:237
  2.3 0.0 copy-done
  2.3 0.1 copy-done.1
  2.4 0.0 copy-done.2
  2.4 2.2 %correlate.1 = bf16[4,2,4,32,128]{4,3,2,1,0:T(8,128)(2,1)S(1)} custom-call(s32[8]{0:T(128)S(1)} %copy-done.2, bf16[2,272,4096]{2,1,0:T(8,128)(2,1)S(1)} %copy-done, bf16[256,256]{1,0:T(8,128)(2,1)S(1)} %make_flip.1.refs_2_, bf16[2,2,16,4096]{3,2,1,0:T(8,128)(2,1)S(1)} %copy-done.1, bf16[2,2,16,4096]{3,2,1,0:T(8,128)(2,1)S(1)} %collective-permute-done.refs_4_), custom_call_target="tpu_custom_call" | custom-call | tf_op jit(solution)/shard_map/correlate/pallas_call | solution.py:162
  4.6 17.6 %all_to_all.5.x_ref = bf16[32,32,128]{2,1,0:T(8,128)(2,1)S(1)} all-to-all(bf16[32,32,128]{2,1,0:T(8,128)(2,1)S(1)} %bitcast.4), channel_id=1, replica_groups={{0,8,16,24,1,9,17,25,2,10,18,26,3,11,19,27,6,14,22,30,7,15,23,31,4,12,2..., dimensions={0} | all-to-all | bytes 524288 | tf_op jit(solution)/shard_map/all_to_all | solution.py:248
  22.2 1.6 %bisquare_stack.1 = f32[128,32]{1,0:T(8,128)} custom-call(bf16[32,32,128]{2,1,0:T(8,128)(2,1)S(1)} %all_to_all.5.x_ref), custom_call_target="tpu_custom_call" | custom-call | tf_op jit(solution)/shard_map/bisquare_stack/pallas_call | solution.py:214
  (1 shorter events, 0.0 us)
Async XLA Ops:
  0.0 2.3 %copy-start = (bf16[2,272,4096]{2,1,0:T(8,128)(2,1)S(1)}, bf16[2,272,4096]{2,1,0:T(8,128)(2,1)}, u32[]{:S(2)}) copy-start(bf16[2,272,4096]{2,1,0:T(8,128)(2,1)} %constant.2.clone.refs_1_) | copy-start | bytes 13369348
  0.0 2.4 %copy-start.1 = (bf16[2,2,16,4096]{3,2,1,0:T(8,128)(2,1)S(1)}, bf16[2,2,16,4096]{3,2,1,0:T(8,128)(2,1)}, u32[]{:S(2)}) copy-start(bf16[2,2,16,4096]{3,2,1,0:T(8,128)(2,1)} %refs_3_.1) | copy-start | bytes 1572868
  0.0 2.4 %copy-start.2 = (s32[8]{0:T(128)S(1)}, s32[8]{0:T(128)}, u32[]{:S(2)}) copy-start(s32[8]{0:T(128)} %refs_0_.1) | copy-start | bytes 100
  0.0 2.3 %collective-permute-start = (bf16[2,2,16,4096]{3,2,1,0:T(8,128)(2,1)}, bf16[2,2,16,4096]{3,2,1,0:T(8,128)(2,1)S(1)}, u32[]{:S(2)}, u32[]{:S(2)}) collective-permute-start(bf16[2,2,16,4096]{3,2,1,0:T(8,128)(2,1)} %refs_3_.1), channel_id=1, source_target_pairs={{0,1},{1,0},{2,3},{3,2},{4,5},{5,4},{6,7},{7,6},{8,9},{9,8},{10,11... | collective-permute-start | bytes 1572872 | tf_op jit(solution)/shard_map/ppermute | solution.py:237

commit v25 on v22

--- a/solution.py
+++ b/solution.py
@@ -95,16 +95,18 @@
                 cross_ref[1, pairs, bins] = imag[receivers]
 
     def add_product(bins, index, sum_ref):
-        term = lax.dot_general(
-            table_ref[index, :, bins],
-            cross_ref[index, :, bins],
-            (((1,), (1,)), ((), ())),
-            preferred_element_type=jnp.float32,
-        )
-        if bins.start == 0:
-            sum_ref[...] = term
-        else:
-            sum_ref[...] += term
+        middle = sum_ref.shape[0] // 32 * 16
+        for lags in (slice(0, middle), slice(middle, sum_ref.shape[0])):
+            term = lax.dot_general(
+                table_ref[index, lags, bins],
+                cross_ref[index, :, bins],
+                (((1,), (1,)), ((), ())),
+                preferred_element_type=jnp.float32,
+            )
+            if bins.start == 0:
+                sum_ref[lags, :] = term
+            else:
+                sum_ref[lags, :] += term
 
     chunks = [slice(start, start + chunk) for start in range(0, bin_count, chunk)]
     for index in range(len(chunks) + 1):

time: 23.6 us -> 25.1 us (1.064)
  Pallas kernels: 3.82 us -> 5.26 us
    pallas_call x1, Pallas kernels: 2.22 us -> 3.66 us  [correlate(): pl.pallas_call(functools.partial(correlate_kernel, peers=peers, chunk=chu...]
where the time goes in v25:
time: 25.1 us; the launch traced here: 24.9 us
  blocking collectives  17.3 us (69%)
  Pallas kernels  5.26 us (21%)
  waiting for transfers between devices  1.72 us (7%)
  starting transfers between devices  0.52 us (2%)
    all_to_all x1, blocking collectives, per_device(): lax.all_to_all(corr, ('win', 'rcv'), split_axis=0, concat_axis=0, tiled=T...  17.3 us
    pallas_call x1, Pallas kernels, correlate(): pl.pallas_call(functools.partial(correlate_kernel, peers=peers, chunk=chu...  3.66 us
    ppermute x1, waiting for transfers between devices, per_device(): lax.ppermute(spectra, 'rcv', [(i, (i + step) % peers) for i in range(peer...  1.72 us
    pallas_call x1, Pallas kernels, stack_blocks(): pl.pallas_call(functools.partial(stack_kernel, factors=factors), out_shap...  1.57 us
    ppermute x1, starting transfers between devices, per_device(): lax.ppermute(spectra, 'rcv', [(i, (i + step) % peers) for i in range(peer...  0.52 us
  transfers between devices with their start and end apart: 1, of which 1 were waited for; matrix products, arithmetic and copies ran while one was open for 0% of the time, Pallas kernels for 0%

profile of v25, /device:TPU:0, one launch (start us, length us, event | category | flops | bytes accessed | tf_op | source)
XLA Modules:
  0.0 24.9 jit_solution(3975501215297531522)
XLA Ops:
  0.0 0.0 copy-start
  0.0 0.0 copy-start.1
  0.0 0.0 copy-start.2
  0.0 0.5 %collective-permute-start = (bf16[2,2,16,4096]{3,2,1,0:T(8,128)(2,1)}, bf16[2,2,16,4096]{3,2,1,0:T(8,128)(2,1)S(1)}, u32[]{:S(2)}, u32[]{:S(2)}) collective-permute-start(bf16[2,2,16,4096]{3,2,1,0:T(8,128)(2,1)} %refs_3_.1), channel_id=1, source_target_pairs={{0,1},{1,0},{2,3},{3,2},{4,5},{5,4},{6,7},{7,6},{8,9},{9,8},{10,11... | collective-permute-start | bytes 1572872 | tf_op jit(solution)/shard_map/ppermute | solution.py:233
  0.6 1.7 %collective-permute-done.refs_4_ = bf16[2,2,16,4096]{3,2,1,0:T(8,128)(2,1)S(1)} collective-permute-done((bf16[2,2,16,4096]{3,2,1,0:T(8,128)(2,1)}, bf16[2,2,16,4096]{3,2,1,0:T(8,128)(2,1)S(1)}, u32[]{:S(2)}, u32[]{:S(2)}) %collective-permute-start) | collective-permute-done | bytes 524320 | tf_op jit(solution)/shard_map/ppermute | solution.py:233
  2.3 0.0 copy-done
  2.3 0.1 copy-done.1
  2.4 0.0 copy-done.2
  2.4 3.7 %correlate.1 = bf16[4,2,4,32,128]{4,3,2,1,0:T(8,128)(2,1)S(1)} custom-call(s32[8]{0:T(128)S(1)} %copy-done.2, bf16[2,272,4096]{2,1,0:T(8,128)(2,1)S(1)} %copy-done, bf16[256,256]{1,0:T(8,128)(2,1)S(1)} %make_flip.1.refs_2_, bf16[2,2,16,4096]{3,2,1,0:T(8,128)(2,1)S(1)} %copy-done.1, bf16[2,2,16,4096]{3,2,1,0:T(8,128)(2,1)S(1)} %collective-permute-done.refs_4_), custom_call_target="tpu_custom_call" | custom-call | tf_op jit(solution)/shard_map/correlate/pallas_call | solution.py:158
  6.1 17.3 %all_to_all.5.x_ref = bf16[32,32,128]{2,1,0:T(8,128)(2,1)S(1)} all-to-all(bf16[32,32,128]{2,1,0:T(8,128)(2,1)S(1)} %bitcast.4), channel_id=1, replica_groups={{0,8,16,24,1,9,17,25,2,10,18,26,3,11,19,27,4,12,20,28,5,13,21,29,6,14,2..., dimensions={0} | all-to-all | bytes 524288 | tf_op jit(solution)/shard_map/all_to_all | solution.py:244
  23.4 1.6 %bisquare_stack.1 = f32[128,32]{1,0:T(8,128)} custom-call(bf16[32,32,128]{2,1,0:T(8,128)(2,1)S(1)} %all_to_all.5.x_ref), custom_call_target="tpu_custom_call" | custom-call | tf_op jit(solution)/shard_map/bisquare_stack/pallas_call | solution.py:210
  (1 shorter events, 0.0 us)
Async XLA Ops:
  0.0 2.3 %copy-start = (bf16[2,272,4096]{2,1,0:T(8,128)(2,1)S(1)}, bf16[2,272,4096]{2,1,0:T(8,128)(2,1)}, u32[]{:S(2)}) copy-start(bf16[2,272,4096]{2,1,0:T(8,128)(2,1)} %constant.2.clone.refs_1_) | copy-start | bytes 13369348
  0.0 2.4 %copy-start.1 = (bf16[2,2,16,4096]{3,2,1,0:T(8,128)(2,1)S(1)}, bf16[2,2,16,4096]{3,2,1,0:T(8,128)(2,1)}, u32[]{:S(2)}) copy-start(bf16[2,2,16,4096]{3,2,1,0:T(8,128)(2,1)} %refs_3_.1) | copy-start | bytes 1572868
  0.0 2.4 %copy-start.2 = (s32[8]{0:T(128)S(1)}, s32[8]{0:T(128)}, u32[]{:S(2)}) copy-start(s32[8]{0:T(128)} %refs_0_.1) | copy-start | bytes 100
  0.0 2.3 %collective-permute-start = (bf16[2,2,16,4096]{3,2,1,0:T(8,128)(2,1)}, bf16[2,2,16,4096]{3,2,1,0:T(8,128)(2,1)S(1)}, u32[]{:S(2)}, u32[]{:S(2)}) collective-permute-start(bf16[2,2,16,4096]{3,2,1,0:T(8,128)(2,1)} %refs_3_.1), channel_id=1, source_target_pairs={{0,1},{1,0},{2,3},{3,2},{4,5},{5,4},{6,7},{7,6},{8,9},{9,8},{10,11... | collective-permute-start | bytes 1572872 | tf_op jit(solution)/shard_map/ppermute | solution.py:233
